TPU v7x, 32 devices: a whole 2x2x4 slice. The times are simulated.
32 devices in a mesh: dp: 4 (over y, x), expert: 8 (over z, core).
Axes of the slice: x: 2, y: 2, z: 4, core: 2. Of those that a mesh axis runs over, the one named last changes fastest.
Arguments:
- grad_out: bfloat16 [1024, 4096], P('expert', 'dp'), may hold values from -6 to 6
- routes: int32 [1024, 8], P('expert'), may hold values from 0 to 15, as said below
- slots: int32 [1024, 8], P('expert'), may hold values from 0 to 511, as said below
- gates: bfloat16 [1024, 8], P('expert'), may hold values from 0.099609375 to 1
- capacity: int32 [16], P('expert'), may hold values from 192 to 384, as said below
- hidden: bfloat16 [16, 384, 2048], P('expert', None, 'dp'), may hold values from -0.1796875 to 0.1796875
- down_weight: bfloat16 [16, 2048, 4096], P('expert', None, 'dp'), may hold values from -0.125 to 0.125
Outputs:
- hidden_grad: float32 [16, 384, 2048], P('expert', None, 'dp')
- gate_grad: float32 [1024, 8], P('expert')
Inputs may be any that keep to these rules, and one draw needn't show every extreme that they name: `routes`: each row names 8 different experts; the tokens of one index of expert name each expert at most 64 times, and some experts exactly 64 times. slots[t, k] is the number of copies (t2, k2) before (t, k) in row-major order over all tokens with the same expert; an expert's slots are distinct. Some expert has capacity 384 and at least 384 copies.
All inputs are finite; a program needn't handle non-finite values.
Results may differ from a plain program's by a relative error of at most 0.0003.
Values may be sent and summed in bfloat16 or wider, within the bound.
No kernel may reach another device: no remote copies, remote signals or barrier semaphores. Data moves between devices by JAX's collectives and lax.ppermute only.
A program may use at most 128 MiB of HBM per device.

v0:
```python
import jax
import jax.numpy as jnp
from jax import lax
from jax.sharding import PartitionSpec as P


def local_ranks(route_grid, expert_total):
    onehot = (route_grid[..., None] == jnp.arange(expert_total, dtype=jnp.int32)).astype(jnp.int32)
    before = jnp.cumsum(onehot, axis=-2) - onehot
    return jnp.sum(before * onehot, axis=-1)


def capacity_of(local_expert, capacity):
    picks = local_expert[..., None] == jnp.arange(capacity.shape[0], dtype=jnp.int32)
    return jnp.sum(jnp.where(picks, capacity, 0), axis=-1)


def shards(grad_out, routes, slots, gates, capacity, hidden, down_weight):
    peer_count = lax.axis_size("expert")
    experts_here = down_weight.shape[0]
    slot_count = hidden.shape[1]
    tok_rows, top_count = routes.shape
    feature_width = grad_out.shape[1]
    expert_total = experts_here * peer_count
    most_rows = top_count * max(2, (tok_rows + expert_total - 1) // expert_total)
    slot_total = experts_here * slot_count
    route_flat = routes.reshape(-1)
    slot_flat = slots.reshape(-1)
    dest_pos = route_flat * most_rows + local_ranks(route_flat, expert_total)
    send_rows = (
        jnp.zeros((expert_total * most_rows, feature_width), jnp.bfloat16)
        .at[dest_pos]
        .set(jnp.repeat(grad_out, top_count, axis=0))
    )
    send_gate = (
        jnp.zeros((expert_total * most_rows,), jnp.bfloat16).at[dest_pos].set(gates.reshape(-1))
    )
    send_slot = (
        jnp.full((expert_total * most_rows,), slot_count, jnp.int32).at[dest_pos].set(slot_flat)
    )
    recv_rows, recv_gate, recv_slot = (
        lax.all_to_all(
            send_rows.reshape(peer_count, experts_here * most_rows, feature_width),
            "expert",
            split_axis=0,
            concat_axis=0,
            tiled=True,
        ),
        lax.all_to_all(
            send_gate.reshape(peer_count, experts_here * most_rows),
            "expert",
            split_axis=0,
            concat_axis=0,
            tiled=True,
        ),
        lax.all_to_all(
            send_slot.reshape(peer_count, experts_here * most_rows),
            "expert",
            split_axis=0,
            concat_axis=0,
            tiled=True,
        ),
    )
    local_expert = jnp.broadcast_to(
        (jnp.arange(experts_here * most_rows, dtype=jnp.int32) // most_rows)[None, :],
        recv_slot.shape,
    )
    usable = recv_slot < capacity_of(local_expert, capacity)
    slot_table = jnp.where(usable, local_expert * slot_count + recv_slot, slot_total).reshape(-1)
    slot_rows = (
        jnp.zeros((slot_total, feature_width), jnp.bfloat16)
        .at[slot_table]
        .set(recv_rows.reshape(-1, feature_width), mode="drop")
    )
    slot_gate = (
        jnp.zeros((slot_total,), jnp.bfloat16)
        .at[slot_table]
        .set(recv_gate.reshape(-1), mode="drop")
    )
    slot_blocks = slot_rows.reshape(experts_here, slot_count, feature_width)
    share_rows = lax.psum_scatter(
        jnp.einsum("efd,ecd->fec", down_weight, slot_blocks, preferred_element_type=jnp.float32),
        "dp",
        scatter_dimension=0,
        tiled=True,
    )
    hidden_share = jnp.transpose(share_rows, (1, 2, 0))
    hidden_grad = (
        slot_gate.reshape(experts_here, slot_count)[..., None].astype(jnp.float32) * hidden_share
    )
    partial_grad = jnp.sum(hidden.astype(jnp.float32) * hidden_share, axis=-1)
    slot_grad = lax.psum(partial_grad, "dp").reshape(-1)
    picked = slot_grad[jnp.minimum(slot_table, slot_total - 1)]
    outgoing = jnp.where(slot_table < slot_total, picked, jnp.float32(0.0)).reshape(
        peer_count, experts_here * most_rows
    )
    incoming = lax.all_to_all(outgoing, "expert", split_axis=0, concat_axis=0, tiled=True).reshape(
        -1
    )
    gate_grad = incoming[dest_pos].reshape(tok_rows, top_count)
    return (hidden_grad, gate_grad)


def solution(mesh):
    placed = (
        P("expert", "dp"),
        P("expert", None),
        P("expert", None),
        P("expert", None),
        P("expert"),
        P("expert", None, "dp"),
        P("expert", None, "dp"),
    )
    return jax.shard_map(
        shards,
        mesh=mesh,
        in_specs=placed,
        out_specs=(P("expert", None, "dp"), P("expert", None)),
        check_vma=False,
    )
```

profile of v0, /device:TPU:0, one launch (start us, length us, event | category | flops | bytes accessed | tf_op | source)
XLA Modules:
  0.0 212.2 jit_solution(7946474631862493231)
XLA Ops:
  7.2 0.7 broadcast_multiply_fusion
  7.9 0.8 copy.32
  8.7 0.1 eq.37
  8.8 0.1 eq.33
  8.9 0.1 copy.31
  9.0 0.1 mul.41
  9.1 4.5 %reduce-window.6 = s32[16,8,128]{2,1,0:T(8,128)S(1)} reduce-window(s32[16,8,128]{2,1,0:T(8,128)S(1)} %fusion.10, s32[]{:T(128)} %constant.36.clone.1), window={size=1x1x128 pad=0_0x0_0x127_0}, to_apply=%region_0.0 | reduce-window | flops 2080768 | bytes 131076 | tf_op jit(solution)/shard_map/reduce-window
  13.7 0.1 copy.34
  14.0 0.8 copy.36
  14.8 0.1 reshape.231
  15.0 4.9 %scatter_custom_fusion = s32[1024]{0:T(1024)} fusion(s32[1024]{0:T(1024)S(1)} %bitcast.71, s32[1024]{0:T(1024)S(1)} %reshape.231, s32[]{:T(128)} %constant.17.clone.1), kind=kCustom, calls=%fused_computation.38 | custom fusion | bytes 4100 | tf_op jit(solution)/shard_map/scatter | solution.py:39
  19.8 6.3 %all-to-all-start = ((s32[8,1,128]{2,1,0:T(1,128)}), s32[8,1,128]{2,1,0:T(1,128)S(1)}, u32[]{:S(2)}, u32[]{:S(2)}) async-start(s32[8,1,128]{2,1,0:T(1,128)} %bitcast.4), calls=%async_computation | async-start | bytes 8192 | tf_op jit(solution)/shard_map/all_to_all | solution.py:56
  26.2 6.8 %scatter_custom_fusion.3 = bf16[1024,1024]{1,0:T(8,128)(2,1)} fusion(s32[1024]{0:T(1024)S(1)} %bitcast.72, bf16[128,1024]{1,0:T(8,128)(2,1)S(1)} %copy-done, bf16[]{:T(256)} %constant.15.clone.1), kind=kCustom, calls=%fused_computation.8 | custom fusion | bytes 2359298 | tf_op jit(solution)/shard_map/scatter | solution.py:33
  33.0 5.2 %all-to-all-start.2 = ((bf16[8,128,1024]{2,1,0:T(8,128)(2,1)}), bf16[8,128,1024]{2,1,0:T(8,128)(2,1)S(1)}, u32[]{:S(2)}, u32[]{:S(2)}) async-start(bf16[8,128,1024]{2,1,0:T(8,128)(2,1)} %bitcast.11), calls=%async_computation.2 | async-start | bytes 4194304 | tf_op jit(solution)/shard_map/all_to_all | solution.py:42
  38.4 48.9 %all-to-all-done.2 = bf16[8,128,1024]{2,1,0:T(8,128)(2,1)S(1)} async-done(((bf16[8,128,1024]{2,1,0:T(8,128)(2,1)}), bf16[8,128,1024]{2,1,0:T(8,128)(2,1)S(1)}, u32[]{:S(2)}, u32[]{:S(2)}) %all-to-all-start.2) | async-done | bytes 2097184 | tf_op jit(solution)/shard_map/all_to_all | solution.py:42
  87.3 6.5 %scatter_custom_fusion.4 = bf16[768,1024]{1,0:T(8,128)(2,1)} fusion(s32[1024]{0:T(1024)S(1)} %bitcast.78, bf16[1024,1024]{1,0:T(8,128)(2,1)S(1)} %bitcast.64, bf16[]{:T(256)} %constant.15.clone.1), kind=kCustom, calls=%fused_computation.15 | custom fusion | bytes 1572866 | tf_op jit(solution)/shard_map/scatter | solution.py:73
  93.8 10.0 %convolution_bitcast_fusion = f32[2048,2,384]{0,2,1:T(8,128)} fusion(bf16[2,384,1024]{2,1,0:T(8,128)(2,1)} %bitcast.65, bf16[2,2048,1024]{2,1,0:T(8,128)(2,1)} %param.13), kind=kOutput, calls=%fused_computation.7 | convolution fusion | flops 3221225472 | bytes 16252928 | tf_op jit(solution)/shard_map/efd,ecd->fec/dot_general | solution.py:82
  103.8 0.7 copy-done.2
  104.5 0.1 copy.37
  104.6 0.1 reshape.239
  104.7 7.6 %scatter_custom_fusion.1 = bf16[1024]{0:T(1024)(128)(2,1)S(1)} fusion(s32[1024]{0:T(1024)S(1)} %bitcast.73, bf16[1024]{0:T(1024)(128)(2,1)S(1)} %reshape.239, bf16[]{:T(256)} %constant.15.clone.1), kind=kCustom, calls=%fused_computation.41 | custom fusion | bytes 2050 | tf_op jit(solution)/shard_map/scatter | solution.py:36
  112.3 7.9 %all_to_all.32 = bf16[8,1,128]{2,1,0:T(2,128)(2,1)S(1)} all-to-all(bf16[8,1,128]{2,1,0:T(2,128)(2,1)S(1)} %copy.38), channel_id=1, replica_groups=mesh['dp'=4,'expert'=8] {'expert'}, dimensions={0} | all-to-all | bytes 4096 | tf_op jit(solution)/shard_map/all_to_all | solution.py:49
  120.2 7.6 %scatter_custom_fusion.2 = bf16[768]{0:T(1024)(128)(2,1)S(1)} fusion(s32[1024]{0:T(1024)S(1)} %bitcast.79, bf16[1024]{0:T(1024)(128)(2,1)S(1)} %bitcast.80, bf16[]{:T(256)} %constant.15.clone.1), kind=kCustom, calls=%fused_computation.46 | custom fusion | bytes 1538 | tf_op jit(solution)/shard_map/scatter | solution.py:78
  127.9 45.2 %reduce-scatter.2.cloned.1.call-done = f32[512,2,384]{0,2,1:T(8,128)} async-done(((f32[2048,2,384]{0,2,1:T(8,128)}), f32[512,2,384]{0,2,1:T(8,128)}) %reduce-scatter.2.cloned.1.call-update) | async-done | bytes 1572880 | tf_op jit(solution)/shard_map/reduce_scatter | solution.py:81
  173.1 2.8 %fusion.2 = (f32[2,384]{1,0:T(2,128)S(1)}, f32[2,384,512]{2,1,0:T(8,128)}) fusion(f32[512,2,384]{0,2,1:T(8,128)} %reduce-scatter.2.cloned.1.call-done, bf16[2,384,512]{2,1,0:T(8,128)(2,1)S(1)} %copy-done.1, f32[2,384]{1,0:T(2,128)S(1)} %reshape.210), kind=kLoop, calls=%fused_computation.12 | loop fusion | flops 1572096 | bytes 3938304 | tf_op jit(solution)/shard_map/reduce_sum | solution.py:91
  175.9 8.9 %psum.7 = f32[768]{0:T(1024)S(1)} all-reduce(f32[768]{0:T(1024)S(1)} %reshape.207), channel_id=1, replica_groups=mesh['dp'=4,'expert'=8] {'dp'}, use_global_device_ids=true, to_apply=%region_11.12 | all-reduce | flops 768 | bytes 6144 | tf_op jit(solution)/shard_map/psum | solution.py:92
  184.8 4.5 %gather_fusion = f32[1024]{0:T(1024)S(1)} fusion(f32[768]{0:T(1024)S(1)} %psum.7, s32[1024]{0:T(1024)S(1)} %broadcast_clamp_fusion.1), kind=kCustom, calls=%fused_computation | custom fusion | bytes 12288 | tf_op jit(solution)/shard_map/gather | solution.py:93
  189.3 0.6 bitcast_select_fusion
  189.9 4.6 %all-to-all-start.3 = ((f32[8,1,128]{2,1,0:T(1,128)}), f32[8,1,128]{2,1,0:T(1,128)S(1)}, u32[]{:S(2)}, u32[]{:S(2)}) async-start(f32[8,1,128]{2,1,0:T(1,128)} %bitcast.21), calls=%async_computation.4 | async-start | bytes 8192 | tf_op jit(solution)/shard_map/all_to_all | solution.py:97
  194.6 5.5 %all-to-all-done.3 = f32[8,1,128]{2,1,0:T(1,128)S(1)} async-done(((f32[8,1,128]{2,1,0:T(1,128)}), f32[8,1,128]{2,1,0:T(1,128)S(1)}, u32[]{:S(2)}, u32[]{:S(2)}) %all-to-all-start.3) | async-done | bytes 4128 | tf_op jit(solution)/shard_map/all_to_all | solution.py:97
  200.0 4.5 %gather_fusion.1 = f32[1024]{0:T(1024)S(1)} fusion(f32[1024]{0:T(1024)S(1)} %bitcast.63, s32[1024]{0:T(1024)S(1)} %broadcast_clamp_fusion), kind=kCustom, calls=%fused_computation.1 | custom fusion | bytes 12288 | tf_op jit(solution)/shard_map/gather | solution.py:100
  204.7 0.7 copy.42
  (31 shorter events, 0.6 us)
Async XLA Ops:
  7.2 19.0 %copy-start = (bf16[128,1024]{1,0:T(8,128)(2,1)S(1)}, bf16[128,1024]{1,0:T(8,128)(2,1)}, u32[]{:S(2)}) copy-start(bf16[128,1024]{1,0:T(8,128)(2,1)} %param.7) | copy-start | bytes 786436
  19.8 13.2 %all-to-all-start = ((s32[8,1,128]{2,1,0:T(1,128)}), s32[8,1,128]{2,1,0:T(1,128)S(1)}, u32[]{:S(2)}, u32[]{:S(2)}) async-start(s32[8,1,128]{2,1,0:T(1,128)} %bitcast.4), calls=%async_computation | async-start | bytes 8192 | tf_op jit(solution)/shard_map/all_to_all | solution.py:56
  33.0 5.3 %copy-start.3 = (s32[2]{0:T(128)S(1)}, s32[2]{0:T(128)}, u32[]{:S(2)}) copy-start(s32[2]{0:T(128)} %param.11) | copy-start | bytes 28
  33.0 54.3 %all-to-all-start.2 = ((bf16[8,128,1024]{2,1,0:T(8,128)(2,1)}), bf16[8,128,1024]{2,1,0:T(8,128)(2,1)S(1)}, u32[]{:S(2)}, u32[]{:S(2)}) async-start(bf16[8,128,1024]{2,1,0:T(8,128)(2,1)} %bitcast.11), calls=%async_computation.2 | async-start | bytes 4194304 | tf_op jit(solution)/shard_map/all_to_all | solution.py:42
  38.2 134.8 %reduce-scatter.2.cloned.1.call-start = ((), (), s32[]{:S(2)}) async-start(), calls=%async_computation.5 | async-start | bytes 7864320 | tf_op jit(solution)/shard_map/reduce_scatter | solution.py:81
  103.8 0.7 copy-start.2
  103.8 69.3 %copy-start.1 = (bf16[2,384,512]{2,1,0:T(8,128)(2,1)S(1)}, bf16[2,384,512]{2,1,0:T(8,128)(2,1)}, u32[]{:S(2)}) copy-start(bf16[2,384,512]{2,1,0:T(8,128)(2,1)} %param.12) | copy-start | bytes 2359300
  189.9 10.1 %all-to-all-start.3 = ((f32[8,1,128]{2,1,0:T(1,128)}), f32[8,1,128]{2,1,0:T(1,128)S(1)}, u32[]{:S(2)}, u32[]{:S(2)}) async-start(f32[8,1,128]{2,1,0:T(1,128)} %bitcast.21), calls=%async_computation.4 | async-start | bytes 8192 | tf_op jit(solution)/shard_map/all_to_all | solution.py:97
Sparse Core Ops, SparseCore 0:
  103.9 69.0 reduce-scatter.1
where the time goes:
time: 213 us; the launch traced here: 212 us
  waiting for transfers between devices  99.6 us (47%)
  local copies, waits for them, and re-layouts  46.4 us (22%)
  blocking collectives  16.8 us (8%)
  starting transfers between devices  16.2 us (8%)
  between operations  14.2 us (7%)
  matrix products  9.98 us (5%)
  other arithmetic  8.96 us (4%)
    all_to_all x1, waiting for transfers between devices, shards(): lax.all_to_all(send_rows.reshape(peer_count, experts_here * most_rows, fe...  48.9 us
    reduce_scatter x1, waiting for transfers between devices, shards(): lax.psum_scatter(jnp.einsum('efd,ecd->fec', down_weight, slot_blocks, pre...  45.2 us
    dot_general x1, matrix products, shards(): jnp.einsum('efd,ecd->fec', down_weight, slot_blocks, preferred_element_ty...  9.98 us
    psum x1, blocking collectives, shards(): slot_grad = lax.psum(partial_grad, 'dp').reshape(-1)  8.91 us
    all_to_all x1, blocking collectives, shards(): lax.all_to_all(send_gate.reshape(peer_count, experts_here * most_rows), '...  7.92 us
    scatter x1, local copies, waits for them, and re-layouts, shards(): jnp.zeros((expert_total * most_rows,), jnp.bfloat16).at[dest_pos]  7.58 us
    scatter x1, local copies, waits for them, and re-layouts, shards(): slot_gate = jnp.zeros((slot_total,), jnp.bfloat16).at[slot_table].set(rec...  7.57 us
    scatter x1, local copies, waits for them, and re-layouts, shards(): send_rows = jnp.zeros((expert_total * most_rows, feature_width), jnp.bflo...  6.84 us
  transfers between devices with their start and end apart: 4, of which 3 were waited for; matrix products, arithmetic and copies ran while one was open for 11% of the time, Pallas kernels for 0%

commit v1 on v0

--- a/solution.py
+++ b/solution.py
@@ -1,7 +1,18 @@
+import functools
+import math
+
 import jax
 import jax.numpy as jnp
 from jax import lax
+from jax.experimental import pallas as pl
+from jax.experimental.pallas import tpu as pltpu
 from jax.sharding import PartitionSpec as P
+
+STEPS = 32766.0
+TAIL = 16
+VMEM = pl.BlockSpec(memory_space=pltpu.VMEM)
+ANY = pl.BlockSpec(memory_space=pl.ANY)
+SMEM = pl.BlockSpec(memory_space=pltpu.SMEM)
 
 
 def local_ranks(route_grid, expert_total):
@@ -15,7 +26,7 @@
     return jnp.sum(jnp.where(picks, capacity, 0), axis=-1)
 
 
-def shards(grad_out, routes, slots, gates, capacity, hidden, down_weight):
+def general(grad_out, routes, slots, gates, capacity, hidden, down_weight):
     peer_count = lax.axis_size("expert")
     experts_here = down_weight.shape[0]
     slot_count = hidden.shape[1]
@@ -38,29 +49,12 @@
     send_slot = (
         jnp.full((expert_total * most_rows,), slot_count, jnp.int32).at[dest_pos].set(slot_flat)
     )
-    recv_rows, recv_gate, recv_slot = (
-        lax.all_to_all(
-            send_rows.reshape(peer_count, experts_here * most_rows, feature_width),
-            "expert",
-            split_axis=0,
-            concat_axis=0,
-            tiled=True,
-        ),
-        lax.all_to_all(
-            send_gate.reshape(peer_count, experts_here * most_rows),
-            "expert",
-            split_axis=0,
-            concat_axis=0,
-            tiled=True,
-        ),
-        lax.all_to_all(
-            send_slot.reshape(peer_count, experts_here * most_rows),
-            "expert",
-            split_axis=0,
-            concat_axis=0,
-            tiled=True,
-        ),
-    )
+    exchange = functools.partial(
+        lax.all_to_all, axis_name="expert", split_axis=0, concat_axis=0, tiled=True
+    )
+    recv_rows = exchange(send_rows.reshape(peer_count, experts_here * most_rows, feature_width))
+    recv_gate = exchange(send_gate.reshape(peer_count, experts_here * most_rows))
+    recv_slot = exchange(send_slot.reshape(peer_count, experts_here * most_rows))
     local_expert = jnp.broadcast_to(
         (jnp.arange(experts_here * most_rows, dtype=jnp.int32) // most_rows)[None, :],
         recv_slot.shape,
@@ -94,14 +88,498 @@
     outgoing = jnp.where(slot_table < slot_total, picked, jnp.float32(0.0)).reshape(
         peer_count, experts_here * most_rows
     )
-    incoming = lax.all_to_all(outgoing, "expert", split_axis=0, concat_axis=0, tiled=True).reshape(
-        -1
-    )
+    incoming = exchange(outgoing).reshape(-1)
     gate_grad = incoming[dest_pos].reshape(tok_rows, top_count)
-    return (hidden_grad, gate_grad)
+    return hidden_grad, gate_grad
+
+
+ORDER = ((0, 1, 2), (1, 0, 2), (2, 1, 0), (2, 1, 0))
+MIB = 2**20
+
+
+def cost(shapes, flops=0):
+    size = sum(math.prod(a.shape) * a.dtype.itemsize for a in shapes)
+    return pl.CostEstimate(flops=flops, bytes_accessed=size, transcendentals=0)
+
+
+def hbm(array):
+    return pltpu.with_memory_space_constraint(array, pltpu.HBM)
+
+
+def like(shape, kind=jnp.float32):
+    return jax.ShapeDtypeStruct(shape, kind)
+
+
+def place():
+    me, rank = lax.axis_index("expert"), lax.axis_index("dp")
+    return me // 2, lax.rem(me, 2), lax.rem(rank, 2), rank // 2
+
+
+def chip_of(z, step):
+    chip = jnp.int32(ORDER[0][step])
+    for at_z in range(1, len(ORDER)):
+        chip = jnp.where(z == at_z, ORDER[at_z][step], chip)
+    return chip
+
+
+def encode(values):
+    peak = jnp.maximum(jnp.max(jnp.abs(values), keepdims=True), 1e-30)
+    power = jnp.floor(jnp.log2(peak)) + 1.0
+    scaled = values * (jnp.exp2(-power) * (STEPS * STEPS))
+    code = jnp.round(scaled * lax.rsqrt(jnp.abs(scaled) + 1e-20))
+    return code.astype(jnp.int32).astype(jnp.int16), power
+
+
+def powers_block(powers, width):
+    spans = [jnp.broadcast_to(power, (TAIL, width // len(powers))) for power in powers]
+    return jnp.concatenate(spans, axis=1).astype(jnp.int32).astype(jnp.int16)
+
+
+def decode(coded, part, parts):
+    rows = (coded.shape[0] - TAIL) // parts
+    lane = part * (coded.shape[1] // parts)
+    power = coded[parts * rows :, lane : lane + 128].astype(jnp.int32).astype(jnp.float32)
+    code = coded[part * rows : (part + 1) * rows, :].astype(jnp.int32).astype(jnp.float32)
+    scale = jnp.exp2(jnp.max(power, keepdims=True)) * (1.0 / (STEPS * STEPS))
+    return code * jnp.abs(code) * scale
+
+
+def prepare_kernel(
+    most, rows, routes, slots, gates, hidden, out, first, others, routes_in, slots_in, gates_in, sem
+):
+    tokens, top = rows.shape[0], routes.shape[0]
+    z, core, _, _ = place()
+    pairs = [(routes, routes_in), (slots, slots_in), (gates, gates_in), (rows, out.at[:tokens])]
+    for step in range(3):
+        start = pl.multiple_of(chip_of(z, step) * (2 * most), 2 * most)
+        for local in range(2):
+            span = others.at[local, 2 * most * (step - 1) : 2 * most * step] if step else first.at[local]
+            pairs.append((hidden.at[local, pl.ds(start, 2 * most)], span))
+    copies = [pltpu.make_async_copy(a, b, sem.at[i]) for i, (a, b) in enumerate(pairs)]
+    for copy in copies:
+        copy.start()
+    for copy in copies[:3]:
+        copy.wait()
+    rank = slots_in[...] - (2 * z + core) * most
+    parts = [routes_in[...], rank, gates_in[...]]
+    packed = jnp.concatenate([part.astype(jnp.float32) for part in parts], axis=1)
+    packed = jnp.concatenate([packed, jnp.zeros((TAIL - top, 3 * tokens), jnp.float32)], axis=0)
+    out[tokens:, : 3 * tokens] = packed.astype(jnp.bfloat16)
+    out[tokens:, 3 * tokens :] = jnp.zeros((TAIL, out.shape[1] - 3 * tokens), jnp.bfloat16)
+    for copy in copies[3:]:
+        copy.wait()
+
+
+def prepare(most, grad_out, routes, slots, gates, hidden):
+    tokens, feats = grad_out.shape
+    top = routes.shape[1]
+    experts, _, width = hidden.shape
+    return pl.pallas_call(
+        functools.partial(prepare_kernel, most),
+        in_specs=[ANY] * 5,
+        out_specs=[VMEM] * 3,
+        out_shape=[
+            like((tokens + TAIL, feats), jnp.bfloat16),
+            like((experts, 2 * most, width), jnp.bfloat16),
+            like((experts, 4 * most, width), jnp.bfloat16),
+        ],
+        scratch_shapes=[
+            pltpu.VMEM((top, tokens), jnp.int32),
+            pltpu.VMEM((top, tokens), jnp.int32),
+            pltpu.VMEM((top, tokens), jnp.bfloat16),
+            pltpu.SemaphoreType.DMA((10,)),
+        ],
+        compiler_params=pltpu.CompilerParams(vmem_limit_bytes=8 * MIB),
+        cost_estimate=cost([grad_out, grad_out, hidden]),
+        name="prepare",
+    )(*(hbm(a) for a in (grad_out, routes.T, slots.T, gates.T, hidden)))
+
+
+def load_kernel(after, weight, out, sem):
+    copy = pltpu.make_async_copy(weight, out, sem)
+    copy.start()
+    copy.wait()
+
+
+def load(after, weight):
+    return pl.pallas_call(
+        load_kernel,
+        in_specs=[ANY, ANY],
+        out_specs=VMEM,
+        out_shape=like(weight.shape, weight.dtype),
+        scratch_shapes=[pltpu.SemaphoreType.DMA],
+        cost_estimate=cost([weight, weight]),
+        compiler_params=pltpu.CompilerParams(vmem_limit_bytes=16 * MIB),
+        name="load_weight",
+    )(after, hbm(weight))
+
+
+def pick_kernel(rules, count, *refs):
+    sem = refs[-1]
+    outs = refs[-1 - len(rules) : -1]
+    z = place()[0]
+    for number, rule in enumerate(rules):
+        for source in sorted(set(rule)):
+            wanted = functools.reduce(
+                jnp.logical_or, [z == at_z for at_z in range(len(rule)) if rule[at_z] == source]
+            )
+
+            @pl.when(wanted)
+            def _(source=source, number=number):
+                pltpu.make_async_copy(refs[source], outs[number], sem.at[number]).start()
+
+    for number in range(len(rules)):
+        pltpu.make_async_copy(refs[0], outs[number], sem.at[number]).wait()
+
+
+def pick(rules, blocks, after):
+    return pl.pallas_call(
+        functools.partial(pick_kernel, rules, len(blocks)),
+        in_specs=[VMEM] * len(blocks) + [ANY] * len(after),
+        out_specs=[VMEM] * len(rules),
+        out_shape=[like(blocks[0].shape, blocks[0].dtype)] * len(rules),
+        scratch_shapes=[pltpu.SemaphoreType.DMA((len(rules),))],
+        compiler_params=pltpu.CompilerParams(vmem_limit_bytes=8 * MIB),
+        cost_estimate=cost(blocks),
+        name="pick",
+    )(*blocks, *after)
+
+
+def take_kernel(over_x, over_y, one, other, sem):
+    copies = [
+        pltpu.make_async_copy(over_x.at[0], one, sem.at[0]),
+        pltpu.make_async_copy(over_y.at[1], other, sem.at[1]),
+    ]
+    for copy in copies:
+        copy.start()
+    for copy in copies:
+        copy.wait()
+
+
+def take(over_x, over_y):
+    out = like(over_x.shape[1:], over_x.dtype)
+    return pl.pallas_call(
+        take_kernel,
+        in_specs=[VMEM] * 2,
+        out_specs=[VMEM] * 2,
+        out_shape=[out, out],
+        scratch_shapes=[pltpu.SemaphoreType.DMA((2,))],
+        compiler_params=pltpu.CompilerParams(vmem_limit_bytes=8 * MIB),
+        cost_estimate=cost([out, out]),
+        name="take",
+    )(over_x, over_y)
+
+
+def expert_view(info, expert, top):
+    tokens = info.shape[1] // 3
+    at = info[:top, :tokens] == expert.astype(jnp.float32)
+    rank = jnp.sum(jnp.where(at, info[:top, tokens : 2 * tokens] + 1.0, 0.0), axis=0, keepdims=True) - 1.0
+    gate = jnp.sum(jnp.where(at, info[:top, 2 * tokens :], 0.0), axis=0, keepdims=True)
+    return at, rank, gate
+
+
+def rank_picks(rank, count, first, limit):
+    numbers = lax.broadcasted_iota(jnp.int32, (count, rank.shape[1]), 0)
+    hit = (numbers.astype(jnp.float32) == rank) & (first + numbers < limit)
+    return jnp.where(hit, 1.0, 0.0)
+
+
+def share_kernel(local, most, top, group, earlier, waits, cap, weight, *refs):
+    blocks, refs = refs[: 2 * len(group)], refs[2 * len(group) :]
+    if earlier is None:
+        send, keep, info, rows = refs[waits:]
+    else:
+        stored, befores = refs[:4], refs[4 : 4 + earlier]
+        send, keep, gates, mine, theirs, rows, info, grads = refs[4 + earlier + waits :]
+    z, core, x, y = place()
+    tokens = blocks[0].shape[0] - TAIL
+    total, width = keep.shape[1], keep.shape[2]
+    expert = (2 * z + core) * 2 + local
+
+    def gather(at, block, side):
+        table = block[tokens:, : 3 * tokens].astype(jnp.float32)
+        info[2 * at + side] = table
+        _, rank, gate = expert_view(table, expert, top)
+        first = (2 * chip_of(z, group[at]) + side) * most
+        picks = rank_picks(rank, most, first, cap[local])
+        span = pl.ds(pl.multiple_of((2 * at + side) * most, most), most)
+        rows[span, :] = jnp.dot(
+            picks.astype(jnp.bfloat16), block[:tokens, :], preferred_element_type=jnp.float32
+        ).astype(jnp.bfloat16)
+        if earlier is not None:
+            weights = jnp.sum(picks * gate, axis=1, keepdims=True)
+            gates[span, :] = jnp.broadcast_to(weights, (most, gates.shape[1]))
+
+    for swap in range(2):
+        side = lax.rem(core + swap, 2)
+        for at in range(len(group)):
+            gather(at, blocks[2 * at + swap], side)
+
+    powers = []
+    for number, (sent, onward) in enumerate(((1, 1), (1, 0), (0, 1), (0, 0))):
+        dx, dy = (sent, onward) if local == 0 else (onward, sent)
+        piece = 2 * lax.rem(y + dy, 2) + lax.rem(x + dx, 2)
+        part = lax.dot_general(
+            rows[...],
+            weight[local, pl.ds(pl.multiple_of(piece * width, width), width), :],
+            (((1,), (1,)), ((), ())),
+            preferred_element_type=jnp.float32,
+        )
+        if earlier is not None:
+            there = stored[3][...] if dx and dy else stored[2 * dy + dx][local]
+            grad = there.astype(jnp.float32) * part
+            grad = jnp.sum(grad, axis=1, keepdims=True)
+            grads[...] = grads[...] + grad if number else grad
+        if sent:
+            code, power = encode(part)
+            send[(1 - onward) * total : (2 - onward) * total, :] = code
+            powers.append(power)
+        else:
+            keep[1 - onward] = part
+    send[2 * total :, :] = powers_block(powers, width)
+
+    if earlier is not None:
+        for out, befores_of in ((mine, befores[0::2]), (theirs, befores[1::2])):
+            out[...] = sum((b[...] for b in befores_of), jnp.zeros(out.shape, jnp.float32))
+        for at, step in enumerate(group):
+            chip = chip_of(z, step)
+            for out, side in ((mine, core), (theirs, 1 - core)):
+                named, rank, _ = expert_view(info[2 * at + side], expert, top)
+                picks = rank_picks(rank, most, (2 * chip + side) * most, cap[local])
+                span = pl.ds(pl.multiple_of((2 * at + side) * most, most), most)
+                back = jnp.sum(picks * grads[span, :], axis=0, keepdims=True)
+                out[chip] = out[chip] + jnp.where(named, back, 0.0)
+
+
+def partial_share(local, most, top, group, cap, weight, blocks, stored=None, befores=(), after=()):
+    tokens, feats = blocks[0].shape[0] - TAIL, blocks[0].shape[1]
+    width = weight.shape[1] // 4
+    total = 2 * most * len(group)
+    tables = (2 * len(group), TAIL, 3 * tokens)
+    outs = [like((2 * total + TAIL, width), jnp.int16), like((2, total, width))]
+    scratch = [pltpu.VMEM((total, feats), jnp.bfloat16)]
+    args = [cap, weight, *blocks]
+    if stored is None:
+        outs.append(like(tables))
+    else:
+        outs += [like((total, 128)), like((3, top, tokens)), like((3, top, tokens))]
+        scratch += [pltpu.VMEM(tables, jnp.float32), pltpu.VMEM((total, 1), jnp.float32)]
+        args += [*stored, *befores]
+    earlier = None if stored is None else len(befores)
+    return pl.pallas_call(
+        functools.partial(share_kernel, local, most, top, group, earlier, len(after)),
+        in_specs=[SMEM] + [VMEM] * (len(args) - 1) + [ANY] * len(after),
+        out_specs=[VMEM] * len(outs),
+        out_shape=outs,
+        scratch_shapes=scratch,
+        cost_estimate=cost([weight, *blocks], 8 * total * width * feats),
+        compiler_params=pltpu.CompilerParams(vmem_limit_bytes=28 * MIB),
+        name=f"share_{local}",
+    )(*args, *after)
+
+
+def middle_kernel(got, keep, *refs):
+    send, rest = refs[-2:]
+    rows, width = rest.shape
+    code, power = encode(keep[0] + decode(got, 0, 2))
+    send[:rows, :] = code
+    send[rows:, :] = powers_block([power], width)
+    rest[...] = keep[1] + decode(got, 1, 2)
+
+
+def middle(got, keep, after=()):
+    _, rows, width = keep.shape
+    return pl.pallas_call(
+        middle_kernel,
+        in_specs=[VMEM, VMEM] + [ANY] * len(after),
+        out_specs=[VMEM, VMEM],
+        out_shape=[like((rows + TAIL, width), jnp.int16), like((rows, width))],
+        cost_estimate=cost([got, keep, keep]),
+        compiler_params=pltpu.CompilerParams(vmem_limit_bytes=8 * MIB),
+        name="middle",
+    )(got, keep, *after)
+
+
+def first_finish_kernel(
+    most, top, cap, hidden, info, got0, rest0, got1, rest1, more_mine, more_theirs, out, mine, theirs
+):
+    z, core, _, _ = place()
+    chip = chip_of(z, 0)
+    mine[...] = more_mine[...]
+    theirs[...] = more_theirs[...]
+    for local, (got, rest) in enumerate(((got0, rest0), (got1, rest1))):
+        out[local] = rest[...] + decode(got, 0, 1)
+        for parts, side in ((mine, core), (theirs, 1 - core)):
+            span = pl.ds(pl.multiple_of(side * most, most), most)
+            named, rank, gate = expert_view(info[side], (2 * z + core) * 2 + local, top)
+            picks = rank_picks(rank, most, (2 * chip + side) * most, cap[local])
+            weight = jnp.sum(picks * gate, axis=1, keepdims=True)
+            share = out[local, span, :]
+            grad = jnp.sum(hidden[local, span, :].astype(jnp.float32) * share, axis=1, keepdims=True)
+            out[local, span, :] = weight * share
+            back = jnp.sum(picks * grad, axis=0, keepdims=True)
+            parts[chip] = parts[chip] + jnp.where(named, back, 0.0)
+
+
+def first_finish(most, top, cap, hidden, info, sums, parts):
+    tokens = info.shape[2] // 3
+    return pl.pallas_call(
+        functools.partial(first_finish_kernel, most, top),
+        in_specs=[SMEM] + [VMEM] * 8,
+        out_specs=[VMEM] * 3,
+        out_shape=[like(hidden.shape), like((3, top, tokens)), like((3, top, tokens))],
+        compiler_params=pltpu.CompilerParams(vmem_limit_bytes=8 * MIB),
+        cost_estimate=cost([*sums, hidden]),
+        name="first_finish",
+    )(cap, hidden, info, *sums, *parts)
+
+
+def finish_kernel(most, first, got0, rest0, gates0, got1, rest1, gates1, *refs):
+    totals, (out, gate_grad) = refs[:-2], refs[-2:]
+    gate_grad[...] = sum((total[...] for total in totals[1:]), totals[0][...])
+    z = place()[0]
+    spans = [pl.ds(pl.multiple_of(chip_of(z, s) * (2 * most), 2 * most), 2 * most) for s in range(3)]
+    for local, (got, rest, gates) in enumerate(((got0, rest0, gates0), (got1, rest1, gates1))):
+        out[local, spans[0], :] = first[local]
+        grad = gates[:, :1] * (rest[...] + decode(got, 0, 1))
+        out[local, spans[1], :] = grad[: 2 * most]
+        out[local, spans[2], :] = grad[2 * most :]
+
+
+def finish(most, first, sums, totals):
+    experts, rows, width = first.shape
+    return pl.pallas_call(
+        functools.partial(finish_kernel, most),
+        in_specs=[VMEM] * (7 + len(totals)),
+        out_specs=[VMEM, VMEM],
+        out_shape=[like((experts, 3 * rows, width)), like(totals[0].shape)],
+        compiler_params=pltpu.CompilerParams(vmem_limit_bytes=16 * MIB),
+        cost_estimate=cost([*sums, first, first]),
+        name="finish",
+    )(first, *sums, *totals)
+
+
+def chips_kernel(mine, got, stay, away):
+    z = place()[0]
+    low, mid, high = (mine[i] + got[i] for i in range(3))
+    none = jnp.zeros(low.shape, jnp.float32)
+    stay[0] = jnp.where(z < 2, low, high)
+    stay[1] = jnp.where(z < 2, mid, none)
+    away[0] = jnp.where(z < 2, high, low)
+    away[1] = jnp.where(z < 2, none, mid)
+
+
+def chip_kernel(kept, got, stay, away):
+    odd = lax.rem(place()[0], 2) == 1
+    even_part, odd_part = (kept[i] + got[i] for i in range(2))
+    stay[...] = jnp.where(odd, odd_part, even_part)
+    away[...] = jnp.where(odd, even_part, odd_part)
+
+
+def add_kernel(*refs):
+    total = refs[0][...]
+    for ref in refs[1:-1]:
+        total = total + ref[...]
+    refs[-1][...] = total
+
+
+def small(kernel, outs, *args):
+    return pl.pallas_call(
+        kernel,
+        in_specs=[VMEM] * len(args),
+        out_specs=[VMEM] * len(outs),
+        out_shape=outs,
+        compiler_params=pltpu.CompilerParams(vmem_limit_bytes=2 * MIB),
+        cost_estimate=cost(args),
+        name=kernel.__name__,
+    )(*args)
+
+
+def blockwise(most, grad_out, routes, slots, gates, capacity, hidden, down_weight):
+    peers, ranks = lax.axis_size("expert"), lax.axis_size("dp")
+    tokens, top = routes.shape
+
+    def along(rows, pairs):
+        return lax.ppermute(rows, "expert", [(2 * a + c, 2 * b + c) for a, b in pairs for c in range(2)])
+
+    def across(rows):
+        return lax.ppermute(rows, "expert", [(i, i ^ 1) for i in range(peers)])
+
+    def over(rows, flip):
+        return lax.ppermute(rows, "dp", [(i, i ^ flip) for i in range(ranks)])
+
+    block, first_hidden, other_hidden = prepare(most, grad_out, routes, slots, gates, hidden)
+    up1 = along(block, [(0, 1), (1, 2), (2, 3)])
+    down1 = along(block, [(2, 1), (1, 0)])
+    stored = [other_hidden, over(other_hidden, 1), over(other_hidden, 2)]
+    passed = take(stored[1], stored[2])
+    far_stored = [over(passed[0], 2), over(passed[1], 1)]
+    weight = load(block, down_weight)
+
+    (first,) = pick(((0, 0, 0, 1),), (block, up1), (weight,))
+    up2 = along(up1, [(1, 2), (2, 3)])
+    pair = (first, across(first))
+    sent, kept = [], []
+    for local in range(2):
+        send, keep, info = partial_share(
+            local, most, top, (0,), capacity, weight, pair, after=passed if local else ()
+        )
+        sent.append(send)
+        kept.append(keep)
+
+    second, relay = pick(((1, 0, 0, 2), (1, 1, 2, 2)), (up1, down1, up2), (*sent, *far_stored))
+    third = along(relay, [(2, 3), (1, 0)])
+    blocks = [second, across(second)]
+
+    sums, onward = [], []
+    for local in range(2):
+        send, rest = middle(over(sent[local], 1 + local), kept[local])
+        onward.append(send)
+        sums += [over(send, 2 - local), rest]
+    (third,) = pick(((1, 0, 0, 1),), (relay, third), onward)
+    blocks += [third, across(third)]
+
+    halves = []
+    before = []
+    for local in range(2):
+        send, keep, gate, *before = partial_share(
+            local, most, top, (1, 2), capacity, weight, blocks, [*stored, far_stored[local]], before,
+            (sums[0], sums[2]) if local else onward,
+        )
+        halves.append((over(send, 1 + local), keep, gate))
+    first_grad, mine, theirs = first_finish(most, top, capacity, first_hidden, info, sums, before)
+
+    one = like((top, tokens))
+    two = like((2, top, tokens))
+    stay, away = small(chips_kernel, [two, two], mine, across(theirs))
+    stay, away = small(
+        chip_kernel, [one, one], stay, along(away, [(z, z ^ 2) for z in range(peers // 2)])
+    )
+    (total,) = small(add_kernel, [one], stay, along(away, [(z, z ^ 1) for z in range(peers // 2)]))
+    whole = [total] + [over(total, flip) for flip in range(1, ranks)]
+
+    sums = []
+    for local, (got, keep, gate) in enumerate(halves):
+        send, rest = middle(got, keep, (total,))
+        sums += [over(send, 2 - local), rest, gate]
+    hidden_grad, gate_grad = finish(most, first_grad, sums, whole)
+    return hidden_grad, gate_grad.T
 
 
 def solution(mesh):
+    peers, ranks = mesh.shape["expert"], mesh.shape["dp"]
+
+    def shards(grad_out, routes, slots, gates, capacity, hidden, down_weight):
+        tokens, top = routes.shape
+        experts = down_weight.shape[0] * peers
+        most = top * max(2, (tokens + experts - 1) // experts)
+        full = most * experts == tokens * top
+        fits = peers == 8 and hidden.shape[1] == 6 * most and 3 * tokens <= grad_out.shape[1]
+        square = ranks == 4 and down_weight.shape[0] == 2 and experts <= 256 and most <= 256
+        if full and fits and square:
+            return blockwise(most, grad_out, routes, slots, gates, capacity, hidden, down_weight)
+        return general(grad_out, routes, slots, gates, capacity, hidden, down_weight)
+
     placed = (
         P("expert", "dp"),
         P("expert", None),

time: 213 us -> 75 us (0.35)
  waiting for transfers between devices: 99.6 us -> 24.9 us
  local copies, waits for them, and re-layouts: 46.4 us -> 0.01 us
  Pallas kernels: 0 us -> 20.1 us
  blocking collectives: 16.8 us -> 0 us
  between operations: 14.2 us -> 0.84 us
  starting transfers between devices: 16.2 us -> 28.9 us
  matrix products: 9.98 us -> 0 us
  other arithmetic: 8.96 us -> 0 us
    all_to_all x3 -> x0, waiting for transfers between devices: 54.4 us -> none  [the longest x1 48.9 us: shards(): lax.all_to_all(send_rows.reshape(peer_count, experts_here * most_rows, fe...]
    reduce_scatter x1 -> x0, waiting for transfers between devices: 45.2 us -> none  [shards(): lax.psum_scatter(jnp.einsum('efd,ecd->fec', down_weight, slot_blocks, pre...]
    scatter x5 -> x0, local copies, waits for them, and re-layouts: 33.4 us -> none  [the longest x1 7.58 us: shards(): jnp.zeros((expert_total * most_rows,), jnp.bfloat16).at[dest_pos]]
    ppermute x0 -> x25, starting transfers between devices: none -> 28.9 us  [the longest x15 15.9 us: over(): return lax.ppermute(rows, 'dp', [(i, i ^ flip) for i in range(ranks)])]
    ppermute x0 -> x25, waiting for transfers between devices: none -> 24.9 us  [the longest x15 13.8 us: over(): return lax.ppermute(rows, 'dp', [(i, i ^ flip) for i in range(ranks)])]
    pallas_call x0 -> x19, Pallas kernels: none -> 20.1 us  [the longest x4 10.3 us: partial_share(): pl.pallas_call(functools.partial(share_kernel, local, most, top, group, e...]
    all_to_all x3 -> x0, starting transfers between devices: 16.2 us -> none  [the longest x1 6.33 us: shards(): lax.all_to_all(send_slot.reshape(peer_count, experts_here * most_rows), '...]
    dot_general x1 -> x0, matrix products: 9.98 us -> none  [shards(): jnp.einsum('efd,ecd->fec', down_weight, slot_blocks, preferred_element_ty...]
  transfers between devices with their start and end apart: 4 -> 25, of which waited for: 3 -> 14; matrix products, arithmetic and copies ran while one was open for 11% -> 0% of each run, Pallas kernels for 0% -> 19%
where the time goes in v1:
time: 75 us; the launch traced here: 74.7 us
  starting transfers between devices  28.9 us (39%)
  waiting for transfers between devices  24.9 us (33%)
  Pallas kernels  20.1 us (27%)
  between operations  0.84 us (1%)
    ppermute x15, starting transfers between devices, over(): return lax.ppermute(rows, 'dp', [(i, i ^ flip) for i in range(ranks)])  15.9 us
    ppermute x15, waiting for transfers between devices, over(): return lax.ppermute(rows, 'dp', [(i, i ^ flip) for i in range(ranks)])  13.8 us
    ppermute x6, starting transfers between devices, along(): lax.ppermute(rows, 'expert', [(2 * a + c, 2 * b + c) for a, b in pairs fo...  12.8 us
    pallas_call x4, Pallas kernels, partial_share(): pl.pallas_call(functools.partial(share_kernel, local, most, top, group, e...  10.3 us
    ppermute x6, waiting for transfers between devices, along(): lax.ppermute(rows, 'expert', [(2 * a + c, 2 * b + c) for a, b in pairs fo...  9.86 us
    pallas_call x1, Pallas kernels, load(): pl.pallas_call(load_kernel, in_specs=[ANY, ANY], out_specs=VMEM, out_shap...  3.39 us
    pallas_call x4, Pallas kernels, middle(): pl.pallas_call(middle_kernel, in_specs=[VMEM, VMEM] + [ANY] * len(after),...  2.17 us
    pallas_call x1, Pallas kernels, finish(): pl.pallas_call(functools.partial(finish_kernel, most), in_specs=[VMEM] *...  1.52 us
  transfers between devices with their start and end apart: 25, of which 14 were waited for; matrix products, arithmetic and copies ran while one was open for 0% of the time, Pallas kernels for 19%

profile of v1, /device:TPU:0, one launch (start us, length us, event | category | flops | bytes accessed | tf_op | source)
XLA Modules:
  0.0 74.7 jit_solution(3011676652580464499)
XLA Ops:
  0.6 1.4 %prepare.1 = (bf16[144,1024]{1,0:T(8,128)(2,1)S(1)}, bf16[2,128,512]{2,1,0:T(8,128)(2,1)S(1)}, bf16[2,256,512]{2,1,0:T(8,128)(2,1)S(1)}) custom-call(bf16[128,1024]{1,0:T(8,128)(2,1)} %rows.1, s32[8,128]{1,0:T(8,128)} %bitcast.4, s32[8,128]{1,0:T(8,128)} %bitcast.5, bf16[8,128]{1,0:T(8,128)(2,1)} %bitcast.6, bf16[2,384,512]{2,1,0:T(8,128)(2,1)} %hidden.1), custom_call_target="tpu_custom_call" | custom-call | bytes 1310720 | tf_op jit(solution)/shard_map/prepare/pallas_call | solution.py:177
  2.0 3.0 %collective-permute-start.3 = (bf16[2,256,512]{2,1,0:T(8,128)(2,1)S(1)}, bf16[2,256,512]{2,1,0:T(8,128)(2,1)S(1)}, u32[]{:S(2)}, u32[]{:S(2)}) collective-permute-start(bf16[2,256,512]{2,1,0:T(8,128)(2,1)S(1)} %get-tuple-element.43.refs_4_), channel_id=1, source_target_pairs={{0,16},{8,24},{16,0},{24,8},{1,17},{9,25},{17,1},{25,9},{2,18},{10... | collective-permute-start | bytes 1572872 | tf_op jit(solution)/shard_map/ppermute | solution.py:509
  5.0 1.5 %collective-permute-start.2 = (bf16[2,256,512]{2,1,0:T(8,128)(2,1)S(1)}, bf16[2,256,512]{2,1,0:T(8,128)(2,1)S(1)}, u32[]{:S(2)}, u32[]{:S(2)}) collective-permute-start(bf16[2,256,512]{2,1,0:T(8,128)(2,1)S(1)} %get-tuple-element.43.refs_4_), channel_id=1, source_target_pairs={{0,8},{8,0},{16,24},{24,16},{1,9},{9,1},{17,25},{25,17},{2,10},{10... | collective-permute-start | bytes 1572872 | tf_op jit(solution)/shard_map/ppermute | solution.py:509
  6.5 3.5 %collective-permute-start = (bf16[144,1024]{1,0:T(8,128)(2,1)S(1)}, bf16[144,1024]{1,0:T(8,128)(2,1)S(1)}, u32[]{:S(2)}, u32[]{:S(2)}) collective-permute-start(bf16[144,1024]{1,0:T(8,128)(2,1)S(1)} %get-tuple-element.42.after.refs_0_), channel_id=1, source_target_pairs={{0,2},{1,3},{2,4},{3,5},{4,6},{5,7},{8,10},{9,11},{10,12},{11,13},... | collective-permute-start | bytes 884744 | tf_op jit(solution)/shard_map/ppermute | solution.py:503
  10.0 3.4 %load_weight.1.refs_2_.weight = bf16[2,2048,1024]{2,1,0:T(8,128)(2,1)S(1)} custom-call(bf16[144,1024]{1,0:T(8,128)(2,1)S(1)} %get-tuple-element.42.after.refs_0_, bf16[2,2048,1024]{2,1,0:T(8,128)(2,1)} %weight.1), custom_call_target="tpu_custom_call" | custom-call | bytes 16777216 | tf_op jit(solution)/shard_map/load_weight/pallas_call | solution.py:205
  13.4 2.3 %collective-permute-done.refs_1_.refs_0_ = bf16[144,1024]{1,0:T(8,128)(2,1)S(1)} collective-permute-done((bf16[144,1024]{1,0:T(8,128)(2,1)S(1)}, bf16[144,1024]{1,0:T(8,128)(2,1)S(1)}, u32[]{:S(2)}, u32[]{:S(2)}) %collective-permute-start) | collective-permute-done | bytes 294944 | tf_op jit(solution)/shard_map/ppermute | solution.py:503
  15.8 1.3 %collective-permute-start.8 = (bf16[144,1024]{1,0:T(8,128)(2,1)S(1)}, bf16[144,1024]{1,0:T(8,128)(2,1)S(1)}, u32[]{:S(2)}, u32[]{:S(2)}) collective-permute-start(bf16[144,1024]{1,0:T(8,128)(2,1)S(1)} %get-tuple-element.42.after.refs_0_), channel_id=1, source_target_pairs={{4,2},{5,3},{2,0},{3,1},{12,10},{13,11},{10,8},{11,9},{20,18},{21,... | collective-permute-start | bytes 884744 | tf_op jit(solution)/shard_map/ppermute | solution.py:503
  17.1 0.7 collective-permute-start.9
  18.9 1.6 %collective-permute-start.11 = (bf16[256,512]{1,0:T(8,128)(2,1)S(1)}, bf16[256,512]{1,0:T(8,128)(2,1)S(1)}, u32[]{:S(2)}, u32[]{:S(2)}) collective-permute-start(bf16[256,512]{1,0:T(8,128)(2,1)S(1)} %get-tuple-element.45.refs_3_), channel_id=1, source_target_pairs={{0,8},{8,0},{16,24},{24,16},{1,9},{9,1},{17,25},{25,17},{2,10},{10... | collective-permute-start | bytes 786440 | tf_op jit(solution)/shard_map/ppermute | solution.py:509
  20.6 2.2 %share_1.2 = (s16[272,512]{1,0:T(8,128)(2,1)S(1)}, f32[2,128,512]{2,1,0:T(8,128)S(1)}, f32[2,16,384]{2,1,0:T(8,128)S(1)}) custom-call(s32[2]{0:T(128)S(1)} %copy-done, bf16[2,2048,1024]{2,1,0:T(8,128)(2,1)S(1)} %load_weight.1.refs_2_.weight, bf16[144,1024]{1,0:T(8,128)(2,1)S(1)} %pick.3.refs_0_, bf16[144,1024]{1,0:T(8,128)(2,1)S(1)} %collective-permute-done.1.refs_1_, ...), custom_call_target="tpu_custom_call" | custom-call | flops 536870912 | bytes 8978432 | tf_op jit(solution)/shard_map/share_1/pallas_call | solution.py:369
  22.8 2.7 %share_0.2 = (s16[272,512]{1,0:T(8,128)(2,1)S(1)}, f32[2,128,512]{2,1,0:T(8,128)S(1)}, f32[2,16,384]{2,1,0:T(8,128)}) custom-call(s32[2]{0:T(128)S(1)} %copy-done, bf16[2,2048,1024]{2,1,0:T(8,128)(2,1)S(1)} %load_weight.1.refs_2_.weight, bf16[144,1024]{1,0:T(8,128)(2,1)S(1)} %pick.3.refs_0_, bf16[144,1024]{1,0:T(8,128)(2,1)S(1)} %collective-permute-done.1.refs_1_), custom_call_target="tpu_custom_call" | custom-call | flops 536870912 | bytes 8978432 | tf_op jit(solution)/shard_map/share_0/pallas_call | solution.py:369
  25.5 2.4 %collective-permute-done.8.refs_1_ = bf16[144,1024]{1,0:T(8,128)(2,1)S(1)} collective-permute-done((bf16[144,1024]{1,0:T(8,128)(2,1)S(1)}, bf16[144,1024]{1,0:T(8,128)(2,1)S(1)}, u32[]{:S(2)}, u32[]{:S(2)}) %collective-permute-start.8) | collective-permute-done | bytes 294944 | tf_op jit(solution)/shard_map/ppermute | solution.py:503
  28.1 1.3 %collective-permute-start.13 = (bf16[144,1024]{1,0:T(8,128)(2,1)S(1)}, bf16[144,1024]{1,0:T(8,128)(2,1)S(1)}, u32[]{:S(2)}, u32[]{:S(2)}) collective-permute-start(bf16[144,1024]{1,0:T(8,128)(2,1)S(1)} %get-tuple-element.56.refs_0_), channel_id=1, source_target_pairs={{4,6},{5,7},{2,0},{3,1},{12,14},{13,15},{10,8},{11,9},{20,22},{21,... | collective-permute-start | bytes 884744 | tf_op jit(solution)/shard_map/ppermute | solution.py:503
  30.5 7.4 %collective-permute-done.4.got = s16[272,512]{1,0:T(8,128)(2,1)S(1)} collective-permute-done((s16[272,512]{1,0:T(8,128)(2,1)S(1)}, s16[272,512]{1,0:T(8,128)(2,1)S(1)}, u32[]{:S(2)}, u32[]{:S(2)}) %collective-permute-start.4) | collective-permute-done | bytes 278560 | tf_op jit(solution)/shard_map/ppermute | solution.py:509
  38.8 1.4 %collective-permute-done.13.refs_1_ = bf16[144,1024]{1,0:T(8,128)(2,1)S(1)} collective-permute-done((bf16[144,1024]{1,0:T(8,128)(2,1)S(1)}, bf16[144,1024]{1,0:T(8,128)(2,1)S(1)}, u32[]{:S(2)}, u32[]{:S(2)}) %collective-permute-start.13) | collective-permute-done | bytes 294944 | tf_op jit(solution)/shard_map/ppermute | solution.py:503
  40.3 1.5 %collective-permute-start.5 = (s16[144,512]{1,0:T(8,128)(2,1)S(1)}, s16[144,512]{1,0:T(8,128)(2,1)S(1)}, u32[]{:S(2)}, u32[]{:S(2)}) collective-permute-start(s16[144,512]{1,0:T(8,128)(2,1)S(1)} %get-tuple-element.49.refs_2_.refs_8_), channel_id=1, source_target_pairs={{0,16},{8,24},{16,0},{24,8},{1,17},{9,25},{17,1},{25,9},{2,18},{10... | collective-permute-start | bytes 442376 | tf_op jit(solution)/shard_map/ppermute | solution.py:509
  42.4 2.7 %share_0.3 = (s16[528,512]{1,0:T(8,128)(2,1)S(1)}, f32[2,256,512]{2,1,0:T(8,128)S(1)}, f32[256,128]{1,0:T(8,128)S(1)}, f32[3,8,128]{2,1,0:T(8,128)S(1)}, f32[3,8,128]{2,1,0:T(8,128)S(1)}) custom-call(s32[2]{0:T(128)S(1)} %copy-done, bf16[2,2048,1024]{2,1,0:T(8,128)(2,1)S(1)} %load_weight.1.refs_2_.weight, bf16[144,1024]{1,0:T(8,128)(2,1)S(1)} %get-tuple-element.55.refs_0_, ...), custom_call_target="tpu_custom_call" | custom-call | flops 1073741824 | bytes 9568256 | tf_op jit(solution)/shard_map/share_0/pallas_call | solution.py:369
  45.1 1.5 %collective-permute-done.5.refs_10_.got0 = s16[144,512]{1,0:T(8,128)(2,1)S(1)} collective-permute-done((s16[144,512]{1,0:T(8,128)(2,1)S(1)}, s16[144,512]{1,0:T(8,128)(2,1)S(1)}, u32[]{:S(2)}, u32[]{:S(2)}) %collective-permute-start.5) | collective-permute-done | bytes 147488 | tf_op jit(solution)/shard_map/ppermute | solution.py:509
  46.6 1.1 %collective-permute-done.7.refs_11_.got1 = s16[144,512]{1,0:T(8,128)(2,1)S(1)} collective-permute-done((s16[144,512]{1,0:T(8,128)(2,1)S(1)}, s16[144,512]{1,0:T(8,128)(2,1)S(1)}, u32[]{:S(2)}, u32[]{:S(2)}) %collective-permute-start.7) | collective-permute-done | bytes 147488 | tf_op jit(solution)/shard_map/ppermute | solution.py:509
  47.7 2.7 %share_1.3 = (s16[528,512]{1,0:T(8,128)(2,1)S(1)}, f32[2,256,512]{2,1,0:T(8,128)S(1)}, f32[256,128]{1,0:T(8,128)S(1)}, f32[3,8,128]{2,1,0:T(8,128)S(1)}, f32[3,8,128]{2,1,0:T(8,128)S(1)}) custom-call(s32[2]{0:T(128)S(1)} %copy-done, bf16[2,2048,1024]{2,1,0:T(8,128)(2,1)S(1)} %load_weight.1.refs_2_.weight, bf16[144,1024]{1,0:T(8,128)(2,1)S(1)} %get-tuple-element.55.refs_0_, ...), custom_call_target="tpu_custom_call" | custom-call | flops 1073741824 | bytes 9568256 | tf_op jit(solution)/shard_map/share_1/pallas_call | solution.py:369
  51.7 0.9 %first_finish.1 = (f32[2,128,512]{2,1,0:T(8,128)S(1)}, f32[3,8,128]{2,1,0:T(8,128)S(1)}, f32[3,8,128]{2,1,0:T(8,128)S(1)}) custom-call(s32[2]{0:T(128)S(1)} %copy-done, bf16[2,128,512]{2,1,0:T(8,128)(2,1)S(1)} %get-tuple-element.41.hidden, f32[2,16,384]{2,1,0:T(8,128)S(1)} %get-tuple-element.46.info, ...), custom_call_target="tpu_custom_call" | custom-call | bytes 1081344 | tf_op jit(solution)/shard_map/first_finish/pallas_call | solution.py:426
  52.7 1.2 %collective-permute-done.16.got = f32[3,8,128]{2,1,0:T(8,128)S(1)} collective-permute-done((f32[3,8,128]{2,1,0:T(8,128)S(1)}, f32[3,8,128]{2,1,0:T(8,128)S(1)}, u32[]{:S(2)}, u32[]{:S(2)}) %collective-permute-start.16) | collective-permute-done | bytes 12320 | tf_op jit(solution)/shard_map/ppermute | solution.py:506
  53.9 4.7 %collective-permute-start.17 = (f32[2,8,128]{2,1,0:T(8,128)S(1)}, f32[2,8,128]{2,1,0:T(8,128)S(1)}, u32[]{:S(2)}, u32[]{:S(2)}) collective-permute-start(f32[2,8,128]{2,1,0:T(8,128)S(1)} %get-tuple-element.67), channel_id=1, source_target_pairs={{0,4},{1,5},{2,6},{3,7},{4,0},{5,1},{6,2},{7,3},{8,12},{9,13},{10,... | collective-permute-start | bytes 24584 | tf_op jit(solution)/shard_map/ppermute | solution.py:503
  58.5 1.6 %collective-permute-done.17.got = f32[2,8,128]{2,1,0:T(8,128)S(1)} collective-permute-done((f32[2,8,128]{2,1,0:T(8,128)S(1)}, f32[2,8,128]{2,1,0:T(8,128)S(1)}, u32[]{:S(2)}, u32[]{:S(2)}) %collective-permute-start.17) | collective-permute-done | bytes 8224 | tf_op jit(solution)/shard_map/ppermute | solution.py:503
  60.2 1.4 %collective-permute-start.18 = (f32[8,128]{1,0:T(8,128)S(1)}, f32[8,128]{1,0:T(8,128)S(1)}, u32[]{:S(2)}, u32[]{:S(2)}) collective-permute-start(f32[8,128]{1,0:T(8,128)S(1)} %get-tuple-element.69), channel_id=1, source_target_pairs={{0,2},{1,3},{2,0},{3,1},{4,6},{5,7},{6,4},{7,5},{8,10},{9,11},{10,... | collective-permute-start | bytes 12296 | tf_op jit(solution)/shard_map/ppermute | solution.py:503
  61.6 2.2 %collective-permute-done.18.refs_1_ = f32[8,128]{1,0:T(8,128)S(1)} collective-permute-done((f32[8,128]{1,0:T(8,128)S(1)}, f32[8,128]{1,0:T(8,128)S(1)}, u32[]{:S(2)}, u32[]{:S(2)}) %collective-permute-start.18) | collective-permute-done | bytes 4128 | tf_op jit(solution)/shard_map/ppermute | solution.py:503
  66.0 0.8 %collective-permute-start.19 = (s16[272,512]{1,0:T(8,128)(2,1)S(1)}, s16[272,512]{1,0:T(8,128)(2,1)S(1)}, u32[]{:S(2)}, u32[]{:S(2)}) collective-permute-start(s16[272,512]{1,0:T(8,128)(2,1)S(1)} %get-tuple-element.70), channel_id=1, source_target_pairs={{0,16},{8,24},{16,0},{24,8},{1,17},{9,25},{17,1},{25,9},{2,18},{10... | collective-permute-start | bytes 835592 | tf_op jit(solution)/shard_map/ppermute | solution.py:509
  66.8 2.2 %collective-permute-start.24 = (f32[8,128]{1,0:T(8,128)S(1)}, f32[8,128]{1,0:T(8,128)S(1)}, u32[]{:S(2)}, u32[]{:S(2)}) collective-permute-start(f32[8,128]{1,0:T(8,128)S(1)} %add_kernel.1.refs_0_), channel_id=1, source_target_pairs={{0,24},{8,16},{16,8},{24,0},{1,25},{9,17},{17,9},{25,1},{2,26},{10... | collective-permute-start | bytes 12296 | tf_op jit(solution)/shard_map/ppermute | solution.py:509
  69.6 0.7 collective-permute-start.22
  70.3 1.7 %collective-permute-done.24.refs_3_ = f32[8,128]{1,0:T(8,128)S(1)} collective-permute-done((f32[8,128]{1,0:T(8,128)S(1)}, f32[8,128]{1,0:T(8,128)S(1)}, u32[]{:S(2)}, u32[]{:S(2)}) %collective-permute-start.24) | collective-permute-done | bytes 4128 | tf_op jit(solution)/shard_map/ppermute | solution.py:509
  72.0 0.9 %collective-permute-done.23.refs_2_ = f32[8,128]{1,0:T(8,128)S(1)} collective-permute-done((f32[8,128]{1,0:T(8,128)S(1)}, f32[8,128]{1,0:T(8,128)S(1)}, u32[]{:S(2)}, u32[]{:S(2)}) %collective-permute-start.23) | collective-permute-done | bytes 4128 | tf_op jit(solution)/shard_map/ppermute | solution.py:509
  73.2 1.5 %finish.1 = (f32[2,384,512]{2,1,0:T(8,128)}, f32[8,128]{1,0:T(8,128)}) custom-call(f32[2,128,512]{2,1,0:T(8,128)S(1)} %get-tuple-element.61.first, s16[272,512]{1,0:T(8,128)(2,1)S(1)} %collective-permute-done.19.got0, f32[256,512]{1,0:T(8,128)S(1)} %get-tuple-element.71.rest0, f32[256,128]{1,0:T(8,128)S(1)} %get-tuple-element.72.gates0, ...), custom_call_target="tpu_custom_call" | custom-call | bytes 2916352 | tf_op jit(solution)/shard_map/finish/pallas_call | solution.py:451
  (39 shorter events, 8.4 us)
Async XLA Ops:
  2.0 15.8 %collective-permute-start.3 = (bf16[2,256,512]{2,1,0:T(8,128)(2,1)S(1)}, bf16[2,256,512]{2,1,0:T(8,128)(2,1)S(1)}, u32[]{:S(2)}, u32[]{:S(2)}) collective-permute-start(bf16[2,256,512]{2,1,0:T(8,128)(2,1)S(1)} %get-tuple-element.43.refs_4_), channel_id=1, source_target_pairs={{0,16},{8,24},{16,0},{24,8},{1,17},{9,25},{17,1},{25,9},{2,18},{10... | collective-permute-start | bytes 1572872 | tf_op jit(solution)/shard_map/ppermute | solution.py:509
  5.0 13.4 %collective-permute-start.2 = (bf16[2,256,512]{2,1,0:T(8,128)(2,1)S(1)}, bf16[2,256,512]{2,1,0:T(8,128)(2,1)S(1)}, u32[]{:S(2)}, u32[]{:S(2)}) collective-permute-start(bf16[2,256,512]{2,1,0:T(8,128)(2,1)S(1)} %get-tuple-element.43.refs_4_), channel_id=1, source_target_pairs={{0,8},{8,0},{16,24},{24,16},{1,9},{9,1},{17,25},{25,17},{2,10},{10... | collective-permute-start | bytes 1572872 | tf_op jit(solution)/shard_map/ppermute | solution.py:509
  6.5 9.2 %collective-permute-start = (bf16[144,1024]{1,0:T(8,128)(2,1)S(1)}, bf16[144,1024]{1,0:T(8,128)(2,1)S(1)}, u32[]{:S(2)}, u32[]{:S(2)}) collective-permute-start(bf16[144,1024]{1,0:T(8,128)(2,1)S(1)} %get-tuple-element.42.after.refs_0_), channel_id=1, source_target_pairs={{0,2},{1,3},{2,4},{3,5},{4,6},{5,7},{8,10},{9,11},{10,12},{11,13},... | collective-permute-start | bytes 884744 | tf_op jit(solution)/shard_map/ppermute | solution.py:503
  13.4 7.1 %copy-start = (s32[2]{0:T(128)S(1)}, s32[2]{0:T(128)}, u32[]{:S(2)}) copy-start(s32[2]{0:T(128)} %cap.9) | copy-start | bytes 28
  15.8 4.8 %collective-permute-start.1 = (bf16[144,1024]{1,0:T(8,128)(2,1)S(1)}, bf16[144,1024]{1,0:T(8,128)(2,1)S(1)}, u32[]{:S(2)}, u32[]{:S(2)}) collective-permute-start(bf16[144,1024]{1,0:T(8,128)(2,1)S(1)} %pick.3.refs_0_), channel_id=1, source_target_pairs={{0,1},{1,0},{2,3},{3,2},{4,5},{5,4},{6,7},{7,6},{8,9},{9,8},{10,11... | collective-permute-start | bytes 884744 | tf_op jit(solution)/shard_map/ppermute | solution.py:506
  15.8 12.0 %collective-permute-start.8 = (bf16[144,1024]{1,0:T(8,128)(2,1)S(1)}, bf16[144,1024]{1,0:T(8,128)(2,1)S(1)}, u32[]{:S(2)}, u32[]{:S(2)}) collective-permute-start(bf16[144,1024]{1,0:T(8,128)(2,1)S(1)} %get-tuple-element.42.after.refs_0_), channel_id=1, source_target_pairs={{4,2},{5,3},{2,0},{3,1},{12,10},{13,11},{10,8},{11,9},{20,18},{21,... | collective-permute-start | bytes 884744 | tf_op jit(solution)/shard_map/ppermute | solution.py:503
  17.1 10.7 %collective-permute-start.9 = (bf16[144,1024]{1,0:T(8,128)(2,1)S(1)}, bf16[144,1024]{1,0:T(8,128)(2,1)S(1)}, u32[]{:S(2)}, u32[]{:S(2)}) collective-permute-start(bf16[144,1024]{1,0:T(8,128)(2,1)S(1)} %collective-permute-done.refs_1_.refs_0_), channel_id=1, source_target_pairs={{2,4},{3,5},{4,6},{5,7},{10,12},{11,13},{12,14},{13,15},{18,20},{1... | collective-permute-start | bytes 884744 | tf_op jit(solution)/shard_map/ppermute | solution.py:503
  18.5 9.4 %collective-permute-start.10 = (bf16[256,512]{1,0:T(8,128)(2,1)S(1)}, bf16[256,512]{1,0:T(8,128)(2,1)S(1)}, u32[]{:S(2)}, u32[]{:S(2)}) collective-permute-start(bf16[256,512]{1,0:T(8,128)(2,1)S(1)} %get-tuple-element.44.refs_2_), channel_id=1, source_target_pairs={{0,16},{8,24},{16,0},{24,8},{1,17},{9,25},{17,1},{25,9},{2,18},{10... | collective-permute-start | bytes 786440 | tf_op jit(solution)/shard_map/ppermute | solution.py:509
  18.9 9.0 %collective-permute-start.11 = (bf16[256,512]{1,0:T(8,128)(2,1)S(1)}, bf16[256,512]{1,0:T(8,128)(2,1)S(1)}, u32[]{:S(2)}, u32[]{:S(2)}) collective-permute-start(bf16[256,512]{1,0:T(8,128)(2,1)S(1)} %get-tuple-element.45.refs_3_), channel_id=1, source_target_pairs={{0,8},{8,0},{16,24},{24,16},{1,9},{9,1},{17,25},{25,17},{2,10},{10... | collective-permute-start | bytes 786440 | tf_op jit(solution)/shard_map/ppermute | solution.py:509
  28.1 12.1 %collective-permute-start.13 = (bf16[144,1024]{1,0:T(8,128)(2,1)S(1)}, bf16[144,1024]{1,0:T(8,128)(2,1)S(1)}, u32[]{:S(2)}, u32[]{:S(2)}) collective-permute-start(bf16[144,1024]{1,0:T(8,128)(2,1)S(1)} %get-tuple-element.56.refs_0_), channel_id=1, source_target_pairs={{4,6},{5,7},{2,0},{3,1},{12,14},{13,15},{10,8},{11,9},{20,22},{21,... | collective-permute-start | bytes 884744 | tf_op jit(solution)/shard_map/ppermute | solution.py:503
  29.4 8.5 %collective-permute-start.4 = (s16[272,512]{1,0:T(8,128)(2,1)S(1)}, s16[272,512]{1,0:T(8,128)(2,1)S(1)}, u32[]{:S(2)}, u32[]{:S(2)}) collective-permute-start(s16[272,512]{1,0:T(8,128)(2,1)S(1)} %get-tuple-element.47.refs_3_), channel_id=1, source_target_pairs={{0,8},{8,0},{16,24},{24,16},{1,9},{9,1},{17,25},{25,17},{2,10},{10... | collective-permute-start | bytes 835592 | tf_op jit(solution)/shard_map/ppermute | solution.py:509
  30.0 8.4 %collective-permute-start.6 = (s16[272,512]{1,0:T(8,128)(2,1)S(1)}, s16[272,512]{1,0:T(8,128)(2,1)S(1)}, u32[]{:S(2)}, u32[]{:S(2)}) collective-permute-start(s16[272,512]{1,0:T(8,128)(2,1)S(1)} %get-tuple-element.51.refs_4_), channel_id=1, source_target_pairs={{0,16},{8,24},{16,0},{24,8},{1,17},{9,25},{17,1},{25,9},{2,18},{10... | collective-permute-start | bytes 835592 | tf_op jit(solution)/shard_map/ppermute | solution.py:509
  30.5 11.9 %collective-permute-start.12 = (bf16[144,1024]{1,0:T(8,128)(2,1)S(1)}, bf16[144,1024]{1,0:T(8,128)(2,1)S(1)}, u32[]{:S(2)}, u32[]{:S(2)}) collective-permute-start(bf16[144,1024]{1,0:T(8,128)(2,1)S(1)} %get-tuple-element.55.refs_0_), channel_id=1, source_target_pairs={{0,1},{1,0},{2,3},{3,2},{4,5},{5,4},{6,7},{7,6},{8,9},{9,8},{10,11... | collective-permute-start | bytes 884744 | tf_op jit(solution)/shard_map/ppermute | solution.py:506
  40.3 2.1 %collective-permute-start.14 = (bf16[144,1024]{1,0:T(8,128)(2,1)S(1)}, bf16[144,1024]{1,0:T(8,128)(2,1)S(1)}, u32[]{:S(2)}, u32[]{:S(2)}) collective-permute-start(bf16[144,1024]{1,0:T(8,128)(2,1)S(1)} %pick.5.refs_2_), channel_id=1, source_target_pairs={{0,1},{1,0},{2,3},{3,2},{4,5},{5,4},{6,7},{7,6},{8,9},{9,8},{10,11... | collective-permute-start | bytes 884744 | tf_op jit(solution)/shard_map/ppermute | solution.py:506
  40.3 6.3 %collective-permute-start.5 = (s16[144,512]{1,0:T(8,128)(2,1)S(1)}, s16[144,512]{1,0:T(8,128)(2,1)S(1)}, u32[]{:S(2)}, u32[]{:S(2)}) collective-permute-start(s16[144,512]{1,0:T(8,128)(2,1)S(1)} %get-tuple-element.49.refs_2_.refs_8_), channel_id=1, source_target_pairs={{0,16},{8,24},{16,0},{24,8},{1,17},{9,25},{17,1},{25,9},{2,18},{10... | collective-permute-start | bytes 442376 | tf_op jit(solution)/shard_map/ppermute | solution.py:509
  41.8 5.9 %collective-permute-start.7 = (s16[144,512]{1,0:T(8,128)(2,1)S(1)}, s16[144,512]{1,0:T(8,128)(2,1)S(1)}, u32[]{:S(2)}, u32[]{:S(2)}) collective-permute-start(s16[144,512]{1,0:T(8,128)(2,1)S(1)} %get-tuple-element.53.refs_3_.refs_9_), channel_id=1, source_target_pairs={{0,8},{8,0},{16,24},{24,16},{1,9},{9,1},{17,25},{25,17},{2,10},{10... | collective-permute-start | bytes 442376 | tf_op jit(solution)/shard_map/ppermute | solution.py:509
  50.5 13.6 %collective-permute-start.20 = (s16[528,512]{1,0:T(8,128)(2,1)S(1)}, s16[528,512]{1,0:T(8,128)(2,1)S(1)}, u32[]{:S(2)}, u32[]{:S(2)}) collective-permute-start(s16[528,512]{1,0:T(8,128)(2,1)S(1)} %get-tuple-element.73), channel_id=1, source_target_pairs={{0,16},{8,24},{16,0},{24,8},{1,17},{9,25},{17,1},{25,9},{2,18},{10... | collective-permute-start | bytes 1622024 | tf_op jit(solution)/shard_map/ppermute | solution.py:509
  51.1 14.2 %collective-permute-start.15 = (s16[528,512]{1,0:T(8,128)(2,1)S(1)}, s16[528,512]{1,0:T(8,128)(2,1)S(1)}, u32[]{:S(2)}, u32[]{:S(2)}) collective-permute-start(s16[528,512]{1,0:T(8,128)(2,1)S(1)} %get-tuple-element.62), channel_id=1, source_target_pairs={{0,8},{8,0},{16,24},{24,16},{1,9},{9,1},{17,25},{25,17},{2,10},{10... | collective-permute-start | bytes 1622024 | tf_op jit(solution)/shard_map/ppermute | solution.py:509
  52.6 1.2 %collective-permute-start.16 = (f32[3,8,128]{2,1,0:T(8,128)S(1)}, f32[3,8,128]{2,1,0:T(8,128)S(1)}, u32[]{:S(2)}, u32[]{:S(2)}) collective-permute-start(f32[3,8,128]{2,1,0:T(8,128)S(1)} %get-tuple-element.65), channel_id=1, source_target_pairs={{0,1},{1,0},{2,3},{3,2},{4,5},{5,4},{6,7},{7,6},{8,9},{9,8},{10,11... | collective-permute-start | bytes 36872 | tf_op jit(solution)/shard_map/ppermute | solution.py:506
  53.9 6.3 %collective-permute-start.17 = (f32[2,8,128]{2,1,0:T(8,128)S(1)}, f32[2,8,128]{2,1,0:T(8,128)S(1)}, u32[]{:S(2)}, u32[]{:S(2)}) collective-permute-start(f32[2,8,128]{2,1,0:T(8,128)S(1)} %get-tuple-element.67), channel_id=1, source_target_pairs={{0,4},{1,5},{2,6},{3,7},{4,0},{5,1},{6,2},{7,3},{8,12},{9,13},{10,... | collective-permute-start | bytes 24584 | tf_op jit(solution)/shard_map/ppermute | solution.py:503
  60.2 3.6 %collective-permute-start.18 = (f32[8,128]{1,0:T(8,128)S(1)}, f32[8,128]{1,0:T(8,128)S(1)}, u32[]{:S(2)}, u32[]{:S(2)}) collective-permute-start(f32[8,128]{1,0:T(8,128)S(1)} %get-tuple-element.69), channel_id=1, source_target_pairs={{0,2},{1,3},{2,0},{3,1},{4,6},{5,7},{6,4},{7,5},{8,10},{9,11},{10,... | collective-permute-start | bytes 12296 | tf_op jit(solution)/shard_map/ppermute | solution.py:503
  64.7 8.5 %collective-permute-start.21 = (s16[272,512]{1,0:T(8,128)(2,1)S(1)}, s16[272,512]{1,0:T(8,128)(2,1)S(1)}, u32[]{:S(2)}, u32[]{:S(2)}) collective-permute-start(s16[272,512]{1,0:T(8,128)(2,1)S(1)} %get-tuple-element.75), channel_id=1, source_target_pairs={{0,8},{8,0},{16,24},{24,16},{1,9},{9,1},{17,25},{25,17},{2,10},{10... | collective-permute-start | bytes 835592 | tf_op jit(solution)/shard_map/ppermute | solution.py:509
  66.0 7.2 %collective-permute-start.19 = (s16[272,512]{1,0:T(8,128)(2,1)S(1)}, s16[272,512]{1,0:T(8,128)(2,1)S(1)}, u32[]{:S(2)}, u32[]{:S(2)}) collective-permute-start(s16[272,512]{1,0:T(8,128)(2,1)S(1)} %get-tuple-element.70), channel_id=1, source_target_pairs={{0,16},{8,24},{16,0},{24,8},{1,17},{9,25},{17,1},{25,9},{2,18},{10... | collective-permute-start | bytes 835592 | tf_op jit(solution)/shard_map/ppermute | solution.py:509
  66.8 5.2 %collective-permute-start.24 = (f32[8,128]{1,0:T(8,128)S(1)}, f32[8,128]{1,0:T(8,128)S(1)}, u32[]{:S(2)}, u32[]{:S(2)}) collective-permute-start(f32[8,128]{1,0:T(8,128)S(1)} %add_kernel.1.refs_0_), channel_id=1, source_target_pairs={{0,24},{8,16},{16,8},{24,0},{1,25},{9,17},{17,9},{25,1},{2,26},{10... | collective-permute-start | bytes 12296 | tf_op jit(solution)/shard_map/ppermute | solution.py:509
  69.0 3.9 %collective-permute-start.23 = (f32[8,128]{1,0:T(8,128)S(1)}, f32[8,128]{1,0:T(8,128)S(1)}, u32[]{:S(2)}, u32[]{:S(2)}) collective-permute-start(f32[8,128]{1,0:T(8,128)S(1)} %add_kernel.1.refs_0_), channel_id=1, source_target_pairs={{0,16},{8,24},{16,0},{24,8},{1,17},{9,25},{17,1},{25,9},{2,18},{10... | collective-permute-start | bytes 12296 | tf_op jit(solution)/shard_map/ppermute | solution.py:509
  69.6 3.6 %collective-permute-start.22 = (f32[8,128]{1,0:T(8,128)S(1)}, f32[8,128]{1,0:T(8,128)S(1)}, u32[]{:S(2)}, u32[]{:S(2)}) collective-permute-start(f32[8,128]{1,0:T(8,128)S(1)} %add_kernel.1.refs_0_), channel_id=1, source_target_pairs={{0,8},{8,0},{16,24},{24,16},{1,9},{9,1},{17,25},{25,17},{2,10},{10... | collective-permute-start | bytes 12296 | tf_op jit(solution)/shard_map/ppermute | solution.py:509

commit v2 on v1

--- a/solution.py
+++ b/solution.py
@@ -522,22 +522,23 @@
     sent, kept = [], []
     for local in range(2):
         send, keep, info = partial_share(
-            local, most, top, (0,), capacity, weight, pair, after=passed if local else ()
+            local, most, top, (0,), capacity, weight, pair, after=()
         )
         sent.append(send)
         kept.append(keep)
 
-    second, relay = pick(((1, 0, 0, 2), (1, 1, 2, 2)), (up1, down1, up2), (*sent, *far_stored))
+    (relay,) = pick(((1, 1, 2, 2),), (up1, down1, up2), sent)
     third = along(relay, [(2, 3), (1, 0)])
-    blocks = [second, across(second)]
 
     sums, onward = [], []
     for local in range(2):
         send, rest = middle(over(sent[local], 1 + local), kept[local])
         onward.append(send)
         sums += [over(send, 2 - local), rest]
-    (third,) = pick(((1, 0, 0, 1),), (relay, third), onward)
-    blocks += [third, across(third)]
+    (second,) = pick(((1, 0, 0, 2),), (up1, down1, up2), (*onward, *far_stored))
+    second_far = across(second)
+    (third,) = pick(((1, 0, 0, 1),), (relay, third), (second_far,))
+    blocks = [second, second_far, third, across(third)]
 
     halves = []
     before = []

time: 75 us -> 75.5 us (level)
  starting transfers between devices: 28.9 us -> 35.7 us
  waiting for transfers between devices: 24.9 us -> 18.6 us
    ppermute x15, starting transfers between devices: 15.9 us -> 19.7 us  [over(): return lax.ppermute(rows, 'dp', [(i, i ^ flip) for i in range(ranks)])]
    ppermute x6, waiting for transfers between devices: 9.86 us -> 6.46 us  [along(): lax.ppermute(rows, 'expert', [(2 * a + c, 2 * b + c) for a, b in pairs fo...]
    ppermute x15, waiting for transfers between devices: 13.8 us -> 10.9 us  [over(): return lax.ppermute(rows, 'dp', [(i, i ^ flip) for i in range(ranks)])]
    ppermute x6, starting transfers between devices: 12.8 us -> 15.7 us  [along(): lax.ppermute(rows, 'expert', [(2 * a + c, 2 * b + c) for a, b in pairs fo...]
  transfers between devices with their start and end apart: 25 -> 25, of which waited for: 14 -> 12; matrix products, arithmetic and copies ran while one was open for 0% -> 0% of each run, Pallas kernels for 19% -> 19%
where the time goes in v2:
time: 75.5 us; the launch traced here: 75.2 us
  starting transfers between devices  35.7 us (47%)
  Pallas kernels  20.1 us (27%)
  waiting for transfers between devices  18.6 us (25%)
  between operations  0.88 us (1%)
    ppermute x15, starting transfers between devices, over(): return lax.ppermute(rows, 'dp', [(i, i ^ flip) for i in range(ranks)])  19.7 us
    ppermute x6, starting transfers between devices, along(): lax.ppermute(rows, 'expert', [(2 * a + c, 2 * b + c) for a, b in pairs fo...  15.7 us
    ppermute x15, waiting for transfers between devices, over(): return lax.ppermute(rows, 'dp', [(i, i ^ flip) for i in range(ranks)])  10.9 us
    pallas_call x4, Pallas kernels, partial_share(): pl.pallas_call(functools.partial(share_kernel, local, most, top, group, e...  10.3 us
    ppermute x6, waiting for transfers between devices, along(): lax.ppermute(rows, 'expert', [(2 * a + c, 2 * b + c) for a, b in pairs fo...  6.46 us
    pallas_call x1, Pallas kernels, load(): pl.pallas_call(load_kernel, in_specs=[ANY, ANY], out_specs=VMEM, out_shap...  3.39 us
    pallas_call x4, Pallas kernels, middle(): pl.pallas_call(middle_kernel, in_specs=[VMEM, VMEM] + [ANY] * len(after),...  2.17 us
    pallas_call x1, Pallas kernels, finish(): pl.pallas_call(functools.partial(finish_kernel, most), in_specs=[VMEM] *...  1.52 us
  transfers between devices with their start and end apart: 25, of which 12 were waited for; matrix products, arithmetic and copies ran while one was open for 0% of the time, Pallas kernels for 19%

profile of v2, /device:TPU:0, one launch (start us, length us, event | category | flops | bytes accessed | tf_op | source)
XLA Modules:
  0.0 75.2 jit_solution(13259585077694323022)
XLA Ops:
  0.6 1.4 %prepare.1 = (bf16[144,1024]{1,0:T(8,128)(2,1)S(1)}, bf16[2,128,512]{2,1,0:T(8,128)(2,1)S(1)}, bf16[2,256,512]{2,1,0:T(8,128)(2,1)S(1)}) custom-call(bf16[128,1024]{1,0:T(8,128)(2,1)} %rows.1, s32[8,128]{1,0:T(8,128)} %bitcast.4, s32[8,128]{1,0:T(8,128)} %bitcast.5, bf16[8,128]{1,0:T(8,128)(2,1)} %bitcast.6, bf16[2,384,512]{2,1,0:T(8,128)(2,1)} %hidden.1), custom_call_target="tpu_custom_call" | custom-call | bytes 1310720 | tf_op jit(solution)/shard_map/prepare/pallas_call | solution.py:177
  2.0 4.9 %collective-permute-start = (bf16[144,1024]{1,0:T(8,128)(2,1)S(1)}, bf16[144,1024]{1,0:T(8,128)(2,1)S(1)}, u32[]{:S(2)}, u32[]{:S(2)}) collective-permute-start(bf16[144,1024]{1,0:T(8,128)(2,1)S(1)} %get-tuple-element.40.after.refs_0_), channel_id=1, source_target_pairs={{0,2},{1,3},{2,4},{3,5},{4,6},{5,7},{8,10},{9,11},{10,12},{11,13},... | collective-permute-start | bytes 884744 | tf_op jit(solution)/shard_map/ppermute | solution.py:503
  7.0 1.6 %collective-permute-start.9 = (bf16[2,256,512]{2,1,0:T(8,128)(2,1)S(1)}, bf16[2,256,512]{2,1,0:T(8,128)(2,1)S(1)}, u32[]{:S(2)}, u32[]{:S(2)}) collective-permute-start(bf16[2,256,512]{2,1,0:T(8,128)(2,1)S(1)} %get-tuple-element.50.refs_4_), channel_id=1, source_target_pairs={{0,16},{8,24},{16,0},{24,8},{1,17},{9,25},{17,1},{25,9},{2,18},{10... | collective-permute-start | bytes 1572872 | tf_op jit(solution)/shard_map/ppermute | solution.py:509
  8.5 1.5 %collective-permute-start.8 = (bf16[2,256,512]{2,1,0:T(8,128)(2,1)S(1)}, bf16[2,256,512]{2,1,0:T(8,128)(2,1)S(1)}, u32[]{:S(2)}, u32[]{:S(2)}) collective-permute-start(bf16[2,256,512]{2,1,0:T(8,128)(2,1)S(1)} %get-tuple-element.50.refs_4_), channel_id=1, source_target_pairs={{0,8},{8,0},{16,24},{24,16},{1,9},{9,1},{17,25},{25,17},{2,10},{10... | collective-permute-start | bytes 1572872 | tf_op jit(solution)/shard_map/ppermute | solution.py:509
  10.0 3.4 %load_weight.1.refs_2_.weight = bf16[2,2048,1024]{2,1,0:T(8,128)(2,1)S(1)} custom-call(bf16[144,1024]{1,0:T(8,128)(2,1)S(1)} %get-tuple-element.40.after.refs_0_, bf16[2,2048,1024]{2,1,0:T(8,128)(2,1)} %weight.1), custom_call_target="tpu_custom_call" | custom-call | bytes 16777216 | tf_op jit(solution)/shard_map/load_weight/pallas_call | solution.py:205
  13.6 1.3 %collective-permute-start.6 = (bf16[144,1024]{1,0:T(8,128)(2,1)S(1)}, bf16[144,1024]{1,0:T(8,128)(2,1)S(1)}, u32[]{:S(2)}, u32[]{:S(2)}) collective-permute-start(bf16[144,1024]{1,0:T(8,128)(2,1)S(1)} %get-tuple-element.40.after.refs_0_), channel_id=1, source_target_pairs={{4,2},{5,3},{2,0},{3,1},{12,10},{13,11},{10,8},{11,9},{20,18},{21,... | collective-permute-start | bytes 884744 | tf_op jit(solution)/shard_map/ppermute | solution.py:503
  15.6 2.7 %share_0.2 = (s16[272,512]{1,0:T(8,128)(2,1)S(1)}, f32[2,128,512]{2,1,0:T(8,128)S(1)}, f32[2,16,384]{2,1,0:T(8,128)}) custom-call(s32[2]{0:T(128)S(1)} %copy-done, bf16[2,2048,1024]{2,1,0:T(8,128)(2,1)S(1)} %load_weight.1.refs_2_.weight, bf16[144,1024]{1,0:T(8,128)(2,1)S(1)} %pick.4.refs_0_, bf16[144,1024]{1,0:T(8,128)(2,1)S(1)} %collective-permute-done.1.refs_1_), custom_call_target="tpu_custom_call" | custom-call | flops 536870912 | bytes 8978432 | tf_op jit(solution)/shard_map/share_0/pallas_call | solution.py:369
  18.3 1.2 %collective-permute-start.2 = (s16[272,512]{1,0:T(8,128)(2,1)S(1)}, s16[272,512]{1,0:T(8,128)(2,1)S(1)}, u32[]{:S(2)}, u32[]{:S(2)}) collective-permute-start(s16[272,512]{1,0:T(8,128)(2,1)S(1)} %get-tuple-element.42.refs_3_), channel_id=1, source_target_pairs={{0,8},{8,0},{16,24},{24,16},{1,9},{9,1},{17,25},{25,17},{2,10},{10... | collective-permute-start | bytes 835592 | tf_op jit(solution)/shard_map/ppermute | solution.py:509
  19.5 2.2 %share_1.2 = (s16[272,512]{1,0:T(8,128)(2,1)S(1)}, f32[2,128,512]{2,1,0:T(8,128)S(1)}, f32[2,16,384]{2,1,0:T(8,128)S(1)}) custom-call(s32[2]{0:T(128)S(1)} %copy-done, bf16[2,2048,1024]{2,1,0:T(8,128)(2,1)S(1)} %load_weight.1.refs_2_.weight, bf16[144,1024]{1,0:T(8,128)(2,1)S(1)} %pick.4.refs_0_, bf16[144,1024]{1,0:T(8,128)(2,1)S(1)} %collective-permute-done.1.refs_1_), custom_call_target="tpu_custom_call" | custom-call | flops 536870912 | bytes 8978432 | tf_op jit(solution)/shard_map/share_1/pallas_call | solution.py:369
  21.8 1.6 %collective-permute-start.4 = (s16[272,512]{1,0:T(8,128)(2,1)S(1)}, s16[272,512]{1,0:T(8,128)(2,1)S(1)}, u32[]{:S(2)}, u32[]{:S(2)}) collective-permute-start(s16[272,512]{1,0:T(8,128)(2,1)S(1)} %get-tuple-element.46.refs_4_), channel_id=1, source_target_pairs={{0,16},{8,24},{16,0},{24,8},{1,17},{9,25},{17,1},{25,9},{2,18},{10... | collective-permute-start | bytes 835592 | tf_op jit(solution)/shard_map/ppermute | solution.py:509
  24.0 1.4 %collective-permute-done.6.refs_1_ = bf16[144,1024]{1,0:T(8,128)(2,1)S(1)} collective-permute-done((bf16[144,1024]{1,0:T(8,128)(2,1)S(1)}, bf16[144,1024]{1,0:T(8,128)(2,1)S(1)}, u32[]{:S(2)}, u32[]{:S(2)}) %collective-permute-start.6) | collective-permute-done | bytes 294944 | tf_op jit(solution)/shard_map/ppermute | solution.py:503
  25.4 1.5 %collective-permute-start.11 = (bf16[256,512]{1,0:T(8,128)(2,1)S(1)}, bf16[256,512]{1,0:T(8,128)(2,1)S(1)}, u32[]{:S(2)}, u32[]{:S(2)}) collective-permute-start(bf16[256,512]{1,0:T(8,128)(2,1)S(1)} %get-tuple-element.52), channel_id=1, source_target_pairs={{0,8},{8,0},{16,24},{24,16},{1,9},{9,1},{17,25},{25,17},{2,10},{10... | collective-permute-start | bytes 786440 | tf_op jit(solution)/shard_map/ppermute | solution.py:509
  27.0 1.3 %collective-permute-start.13 = (bf16[144,1024]{1,0:T(8,128)(2,1)S(1)}, bf16[144,1024]{1,0:T(8,128)(2,1)S(1)}, u32[]{:S(2)}, u32[]{:S(2)}) collective-permute-start(bf16[144,1024]{1,0:T(8,128)(2,1)S(1)} %pick.6.refs_0_), channel_id=1, source_target_pairs={{4,6},{5,7},{2,0},{3,1},{12,14},{13,15},{10,8},{11,9},{20,22},{21,... | collective-permute-start | bytes 884744 | tf_op jit(solution)/shard_map/ppermute | solution.py:503
  28.7 2.6 %collective-permute-done.4.got = s16[272,512]{1,0:T(8,128)(2,1)S(1)} collective-permute-done((s16[272,512]{1,0:T(8,128)(2,1)S(1)}, s16[272,512]{1,0:T(8,128)(2,1)S(1)}, u32[]{:S(2)}, u32[]{:S(2)}) %collective-permute-start.4) | collective-permute-done | bytes 278560 | tf_op jit(solution)/shard_map/ppermute | solution.py:509
  31.8 4.4 %collective-permute-done.10.refs_5_.refs_7_ = bf16[256,512]{1,0:T(8,128)(2,1)S(1)} collective-permute-done((bf16[256,512]{1,0:T(8,128)(2,1)S(1)}, bf16[256,512]{1,0:T(8,128)(2,1)S(1)}, u32[]{:S(2)}, u32[]{:S(2)}) %collective-permute-start.10) | collective-permute-done | bytes 262176 | tf_op jit(solution)/shard_map/ppermute | solution.py:509
  36.4 1.9 %collective-permute-done.13.refs_1_ = bf16[144,1024]{1,0:T(8,128)(2,1)S(1)} collective-permute-done((bf16[144,1024]{1,0:T(8,128)(2,1)S(1)}, bf16[144,1024]{1,0:T(8,128)(2,1)S(1)}, u32[]{:S(2)}, u32[]{:S(2)}) %collective-permute-start.13) | collective-permute-done | bytes 294944 | tf_op jit(solution)/shard_map/ppermute | solution.py:503
  38.4 1.6 %collective-permute-start.3 = (s16[144,512]{1,0:T(8,128)(2,1)S(1)}, s16[144,512]{1,0:T(8,128)(2,1)S(1)}, u32[]{:S(2)}, u32[]{:S(2)}) collective-permute-start(s16[144,512]{1,0:T(8,128)(2,1)S(1)} %get-tuple-element.44.refs_3_.refs_8_), channel_id=1, source_target_pairs={{0,16},{8,24},{16,0},{24,8},{1,17},{9,25},{17,1},{25,9},{2,18},{10... | collective-permute-start | bytes 442376 | tf_op jit(solution)/shard_map/ppermute | solution.py:509
  40.0 1.5 %collective-permute-start.5 = (s16[144,512]{1,0:T(8,128)(2,1)S(1)}, s16[144,512]{1,0:T(8,128)(2,1)S(1)}, u32[]{:S(2)}, u32[]{:S(2)}) collective-permute-start(s16[144,512]{1,0:T(8,128)(2,1)S(1)} %get-tuple-element.48.refs_4_.refs_9_), channel_id=1, source_target_pairs={{0,8},{8,0},{16,24},{24,16},{1,9},{9,1},{17,25},{25,17},{2,10},{10... | collective-permute-start | bytes 442376 | tf_op jit(solution)/shard_map/ppermute | solution.py:509
  41.5 2.7 %share_0.3 = (s16[528,512]{1,0:T(8,128)(2,1)S(1)}, f32[2,256,512]{2,1,0:T(8,128)S(1)}, f32[256,128]{1,0:T(8,128)S(1)}, f32[3,8,128]{2,1,0:T(8,128)S(1)}, f32[3,8,128]{2,1,0:T(8,128)S(1)}) custom-call(s32[2]{0:T(128)S(1)} %copy-done, bf16[2,2048,1024]{2,1,0:T(8,128)(2,1)S(1)} %load_weight.1.refs_2_.weight, bf16[144,1024]{1,0:T(8,128)(2,1)S(1)} %pick.5.refs_0_, ...), custom_call_target="tpu_custom_call" | custom-call | flops 1073741824 | bytes 9568256 | tf_op jit(solution)/shard_map/share_0/pallas_call | solution.py:369
  44.7 1.2 %collective-permute-done.5.refs_11_.got1 = s16[144,512]{1,0:T(8,128)(2,1)S(1)} collective-permute-done((s16[144,512]{1,0:T(8,128)(2,1)S(1)}, s16[144,512]{1,0:T(8,128)(2,1)S(1)}, u32[]{:S(2)}, u32[]{:S(2)}) %collective-permute-start.5) | collective-permute-done | bytes 147488 | tf_op jit(solution)/shard_map/ppermute | solution.py:509
  45.9 2.7 %share_1.3 = (s16[528,512]{1,0:T(8,128)(2,1)S(1)}, f32[2,256,512]{2,1,0:T(8,128)S(1)}, f32[256,128]{1,0:T(8,128)S(1)}, f32[3,8,128]{2,1,0:T(8,128)S(1)}, f32[3,8,128]{2,1,0:T(8,128)S(1)}) custom-call(s32[2]{0:T(128)S(1)} %copy-done, bf16[2,2048,1024]{2,1,0:T(8,128)(2,1)S(1)} %load_weight.1.refs_2_.weight, bf16[144,1024]{1,0:T(8,128)(2,1)S(1)} %pick.5.refs_0_, ...), custom_call_target="tpu_custom_call" | custom-call | flops 1073741824 | bytes 9568256 | tf_op jit(solution)/shard_map/share_1/pallas_call | solution.py:369
  49.2 1.5 %collective-permute-start.15 = (s16[528,512]{1,0:T(8,128)(2,1)S(1)}, s16[528,512]{1,0:T(8,128)(2,1)S(1)}, u32[]{:S(2)}, u32[]{:S(2)}) collective-permute-start(s16[528,512]{1,0:T(8,128)(2,1)S(1)} %get-tuple-element.58), channel_id=1, source_target_pairs={{0,8},{8,0},{16,24},{24,16},{1,9},{9,1},{17,25},{25,17},{2,10},{10... | collective-permute-start | bytes 1622024 | tf_op jit(solution)/shard_map/ppermute | solution.py:509
  51.7 1.2 %collective-permute-done.16.got = f32[3,8,128]{2,1,0:T(8,128)S(1)} collective-permute-done((f32[3,8,128]{2,1,0:T(8,128)S(1)}, f32[3,8,128]{2,1,0:T(8,128)S(1)}, u32[]{:S(2)}, u32[]{:S(2)}) %collective-permute-start.16) | collective-permute-done | bytes 12320 | tf_op jit(solution)/shard_map/ppermute | solution.py:506
  52.9 4.3 %collective-permute-start.17 = (f32[2,8,128]{2,1,0:T(8,128)S(1)}, f32[2,8,128]{2,1,0:T(8,128)S(1)}, u32[]{:S(2)}, u32[]{:S(2)}) collective-permute-start(f32[2,8,128]{2,1,0:T(8,128)S(1)} %get-tuple-element.63), channel_id=1, source_target_pairs={{0,4},{1,5},{2,6},{3,7},{4,0},{5,1},{6,2},{7,3},{8,12},{9,13},{10,... | collective-permute-start | bytes 24584 | tf_op jit(solution)/shard_map/ppermute | solution.py:503
  57.2 1.6 %collective-permute-done.17.got = f32[2,8,128]{2,1,0:T(8,128)S(1)} collective-permute-done((f32[2,8,128]{2,1,0:T(8,128)S(1)}, f32[2,8,128]{2,1,0:T(8,128)S(1)}, u32[]{:S(2)}, u32[]{:S(2)}) %collective-permute-start.17) | collective-permute-done | bytes 8224 | tf_op jit(solution)/shard_map/ppermute | solution.py:503
  58.8 3.2 %collective-permute-start.18 = (f32[8,128]{1,0:T(8,128)S(1)}, f32[8,128]{1,0:T(8,128)S(1)}, u32[]{:S(2)}, u32[]{:S(2)}) collective-permute-start(f32[8,128]{1,0:T(8,128)S(1)} %get-tuple-element.65), channel_id=1, source_target_pairs={{0,2},{1,3},{2,0},{3,1},{4,6},{5,7},{6,4},{7,5},{8,10},{9,11},{10,... | collective-permute-start | bytes 12296 | tf_op jit(solution)/shard_map/ppermute | solution.py:503
  62.0 1.6 %collective-permute-done.18.refs_1_ = f32[8,128]{1,0:T(8,128)S(1)} collective-permute-done((f32[8,128]{1,0:T(8,128)S(1)}, f32[8,128]{1,0:T(8,128)S(1)}, u32[]{:S(2)}, u32[]{:S(2)}) %collective-permute-start.18) | collective-permute-done | bytes 4128 | tf_op jit(solution)/shard_map/ppermute | solution.py:503
  64.2 1.6 %collective-permute-start.21 = (s16[272,512]{1,0:T(8,128)(2,1)S(1)}, s16[272,512]{1,0:T(8,128)(2,1)S(1)}, u32[]{:S(2)}, u32[]{:S(2)}) collective-permute-start(s16[272,512]{1,0:T(8,128)(2,1)S(1)} %get-tuple-element.71), channel_id=1, source_target_pairs={{0,8},{8,0},{16,24},{24,16},{1,9},{9,1},{17,25},{25,17},{2,10},{10... | collective-permute-start | bytes 835592 | tf_op jit(solution)/shard_map/ppermute | solution.py:509
  66.5 1.6 %collective-permute-start.19 = (s16[272,512]{1,0:T(8,128)(2,1)S(1)}, s16[272,512]{1,0:T(8,128)(2,1)S(1)}, u32[]{:S(2)}, u32[]{:S(2)}) collective-permute-start(s16[272,512]{1,0:T(8,128)(2,1)S(1)} %get-tuple-element.66), channel_id=1, source_target_pairs={{0,16},{8,24},{16,0},{24,8},{1,17},{9,25},{17,1},{25,9},{2,18},{10... | collective-permute-start | bytes 835592 | tf_op jit(solution)/shard_map/ppermute | solution.py:509
  68.5 1.5 %collective-permute-start.23 = (f32[8,128]{1,0:T(8,128)S(1)}, f32[8,128]{1,0:T(8,128)S(1)}, u32[]{:S(2)}, u32[]{:S(2)}) collective-permute-start(f32[8,128]{1,0:T(8,128)S(1)} %add_kernel.1.refs_0_), channel_id=1, source_target_pairs={{0,16},{8,24},{16,0},{24,8},{1,17},{9,25},{17,1},{25,9},{2,18},{10... | collective-permute-start | bytes 12296 | tf_op jit(solution)/shard_map/ppermute | solution.py:509
  70.0 1.5 %collective-permute-start.22 = (f32[8,128]{1,0:T(8,128)S(1)}, f32[8,128]{1,0:T(8,128)S(1)}, u32[]{:S(2)}, u32[]{:S(2)}) collective-permute-start(f32[8,128]{1,0:T(8,128)S(1)} %add_kernel.1.refs_0_), channel_id=1, source_target_pairs={{0,8},{8,0},{16,24},{24,16},{1,9},{9,1},{17,25},{25,17},{2,10},{10... | collective-permute-start | bytes 12296 | tf_op jit(solution)/shard_map/ppermute | solution.py:509
  73.7 1.5 %finish.1 = (f32[2,384,512]{2,1,0:T(8,128)}, f32[8,128]{1,0:T(8,128)}) custom-call(f32[2,128,512]{2,1,0:T(8,128)S(1)} %get-tuple-element.57.first, s16[272,512]{1,0:T(8,128)(2,1)S(1)} %collective-permute-done.19.got0, f32[256,512]{1,0:T(8,128)S(1)} %get-tuple-element.67.rest0, f32[256,128]{1,0:T(8,128)S(1)} %get-tuple-element.68.gates0, ...), custom_call_target="tpu_custom_call" | custom-call | bytes 2916352 | tf_op jit(solution)/shard_map/finish/pallas_call | solution.py:451
  (40 shorter events, 8.7 us)
Async XLA Ops:
  2.0 11.4 %collective-permute-start = (bf16[144,1024]{1,0:T(8,128)(2,1)S(1)}, bf16[144,1024]{1,0:T(8,128)(2,1)S(1)}, u32[]{:S(2)}, u32[]{:S(2)}) collective-permute-start(bf16[144,1024]{1,0:T(8,128)(2,1)S(1)} %get-tuple-element.40.after.refs_0_), channel_id=1, source_target_pairs={{0,2},{1,3},{2,4},{3,5},{4,6},{5,7},{8,10},{9,11},{10,12},{11,13},... | collective-permute-start | bytes 884744 | tf_op jit(solution)/shard_map/ppermute | solution.py:503
  7.0 14.8 %collective-permute-start.9 = (bf16[2,256,512]{2,1,0:T(8,128)(2,1)S(1)}, bf16[2,256,512]{2,1,0:T(8,128)(2,1)S(1)}, u32[]{:S(2)}, u32[]{:S(2)}) collective-permute-start(bf16[2,256,512]{2,1,0:T(8,128)(2,1)S(1)} %get-tuple-element.50.refs_4_), channel_id=1, source_target_pairs={{0,16},{8,24},{16,0},{24,8},{1,17},{9,25},{17,1},{25,9},{2,18},{10... | collective-permute-start | bytes 1572872 | tf_op jit(solution)/shard_map/ppermute | solution.py:509
  8.5 14.8 %collective-permute-start.8 = (bf16[2,256,512]{2,1,0:T(8,128)(2,1)S(1)}, bf16[2,256,512]{2,1,0:T(8,128)(2,1)S(1)}, u32[]{:S(2)}, u32[]{:S(2)}) collective-permute-start(bf16[2,256,512]{2,1,0:T(8,128)(2,1)S(1)} %get-tuple-element.50.refs_4_), channel_id=1, source_target_pairs={{0,8},{8,0},{16,24},{24,16},{1,9},{9,1},{17,25},{25,17},{2,10},{10... | collective-permute-start | bytes 1572872 | tf_op jit(solution)/shard_map/ppermute | solution.py:509
  13.4 2.2 %copy-start = (s32[2]{0:T(128)S(1)}, s32[2]{0:T(128)}, u32[]{:S(2)}) copy-start(s32[2]{0:T(128)} %cap.9) | copy-start | bytes 28
  13.6 2.1 %collective-permute-start.1 = (bf16[144,1024]{1,0:T(8,128)(2,1)S(1)}, bf16[144,1024]{1,0:T(8,128)(2,1)S(1)}, u32[]{:S(2)}, u32[]{:S(2)}) collective-permute-start(bf16[144,1024]{1,0:T(8,128)(2,1)S(1)} %pick.4.refs_0_), channel_id=1, source_target_pairs={{0,1},{1,0},{2,3},{3,2},{4,5},{5,4},{6,7},{7,6},{8,9},{9,8},{10,11... | collective-permute-start | bytes 884744 | tf_op jit(solution)/shard_map/ppermute | solution.py:506
  13.6 11.8 %collective-permute-start.6 = (bf16[144,1024]{1,0:T(8,128)(2,1)S(1)}, bf16[144,1024]{1,0:T(8,128)(2,1)S(1)}, u32[]{:S(2)}, u32[]{:S(2)}) collective-permute-start(bf16[144,1024]{1,0:T(8,128)(2,1)S(1)} %get-tuple-element.40.after.refs_0_), channel_id=1, source_target_pairs={{4,2},{5,3},{2,0},{3,1},{12,10},{13,11},{10,8},{11,9},{20,18},{21,... | collective-permute-start | bytes 884744 | tf_op jit(solution)/shard_map/ppermute | solution.py:503
  14.9 11.9 %collective-permute-start.7 = (bf16[144,1024]{1,0:T(8,128)(2,1)S(1)}, bf16[144,1024]{1,0:T(8,128)(2,1)S(1)}, u32[]{:S(2)}, u32[]{:S(2)}) collective-permute-start(bf16[144,1024]{1,0:T(8,128)(2,1)S(1)} %collective-permute-done.refs_1_.refs_0_), channel_id=1, source_target_pairs={{2,4},{3,5},{4,6},{5,7},{10,12},{11,13},{12,14},{13,15},{18,20},{1... | collective-permute-start | bytes 884744 | tf_op jit(solution)/shard_map/ppermute | solution.py:503
  18.3 9.9 %collective-permute-start.2 = (s16[272,512]{1,0:T(8,128)(2,1)S(1)}, s16[272,512]{1,0:T(8,128)(2,1)S(1)}, u32[]{:S(2)}, u32[]{:S(2)}) collective-permute-start(s16[272,512]{1,0:T(8,128)(2,1)S(1)} %get-tuple-element.42.refs_3_), channel_id=1, source_target_pairs={{0,8},{8,0},{16,24},{24,16},{1,9},{9,1},{17,25},{25,17},{2,10},{10... | collective-permute-start | bytes 835592 | tf_op jit(solution)/shard_map/ppermute | solution.py:509
  21.8 9.6 %collective-permute-start.4 = (s16[272,512]{1,0:T(8,128)(2,1)S(1)}, s16[272,512]{1,0:T(8,128)(2,1)S(1)}, u32[]{:S(2)}, u32[]{:S(2)}) collective-permute-start(s16[272,512]{1,0:T(8,128)(2,1)S(1)} %get-tuple-element.46.refs_4_), channel_id=1, source_target_pairs={{0,16},{8,24},{16,0},{24,8},{1,17},{9,25},{17,1},{25,9},{2,18},{10... | collective-permute-start | bytes 835592 | tf_op jit(solution)/shard_map/ppermute | solution.py:509
  23.4 12.8 %collective-permute-start.10 = (bf16[256,512]{1,0:T(8,128)(2,1)S(1)}, bf16[256,512]{1,0:T(8,128)(2,1)S(1)}, u32[]{:S(2)}, u32[]{:S(2)}) collective-permute-start(bf16[256,512]{1,0:T(8,128)(2,1)S(1)} %get-tuple-element.51), channel_id=1, source_target_pairs={{0,16},{8,24},{16,0},{24,8},{1,17},{9,25},{17,1},{25,9},{2,18},{10... | collective-permute-start | bytes 786440 | tf_op jit(solution)/shard_map/ppermute | solution.py:509
  25.4 10.9 %collective-permute-start.11 = (bf16[256,512]{1,0:T(8,128)(2,1)S(1)}, bf16[256,512]{1,0:T(8,128)(2,1)S(1)}, u32[]{:S(2)}, u32[]{:S(2)}) collective-permute-start(bf16[256,512]{1,0:T(8,128)(2,1)S(1)} %get-tuple-element.52), channel_id=1, source_target_pairs={{0,8},{8,0},{16,24},{24,16},{1,9},{9,1},{17,25},{25,17},{2,10},{10... | collective-permute-start | bytes 786440 | tf_op jit(solution)/shard_map/ppermute | solution.py:509
  27.0 11.3 %collective-permute-start.13 = (bf16[144,1024]{1,0:T(8,128)(2,1)S(1)}, bf16[144,1024]{1,0:T(8,128)(2,1)S(1)}, u32[]{:S(2)}, u32[]{:S(2)}) collective-permute-start(bf16[144,1024]{1,0:T(8,128)(2,1)S(1)} %pick.6.refs_0_), channel_id=1, source_target_pairs={{4,6},{5,7},{2,0},{3,1},{12,14},{13,15},{10,8},{11,9},{20,22},{21,... | collective-permute-start | bytes 884744 | tf_op jit(solution)/shard_map/ppermute | solution.py:503
  36.3 1.9 %collective-permute-start.12 = (bf16[144,1024]{1,0:T(8,128)(2,1)S(1)}, bf16[144,1024]{1,0:T(8,128)(2,1)S(1)}, u32[]{:S(2)}, u32[]{:S(2)}) collective-permute-start(bf16[144,1024]{1,0:T(8,128)(2,1)S(1)} %pick.5.refs_0_), channel_id=1, source_target_pairs={{0,1},{1,0},{2,3},{3,2},{4,5},{5,4},{6,7},{7,6},{8,9},{9,8},{10,11... | collective-permute-start | bytes 884744 | tf_op jit(solution)/shard_map/ppermute | solution.py:506
  38.3 3.2 %collective-permute-start.14 = (bf16[144,1024]{1,0:T(8,128)(2,1)S(1)}, bf16[144,1024]{1,0:T(8,128)(2,1)S(1)}, u32[]{:S(2)}, u32[]{:S(2)}) collective-permute-start(bf16[144,1024]{1,0:T(8,128)(2,1)S(1)} %pick.7.refs_2_), channel_id=1, source_target_pairs={{0,1},{1,0},{2,3},{3,2},{4,5},{5,4},{6,7},{7,6},{8,9},{9,8},{10,11... | collective-permute-start | bytes 884744 | tf_op jit(solution)/shard_map/ppermute | solution.py:506
  38.4 6.3 %collective-permute-start.3 = (s16[144,512]{1,0:T(8,128)(2,1)S(1)}, s16[144,512]{1,0:T(8,128)(2,1)S(1)}, u32[]{:S(2)}, u32[]{:S(2)}) collective-permute-start(s16[144,512]{1,0:T(8,128)(2,1)S(1)} %get-tuple-element.44.refs_3_.refs_8_), channel_id=1, source_target_pairs={{0,16},{8,24},{16,0},{24,8},{1,17},{9,25},{17,1},{25,9},{2,18},{10... | collective-permute-start | bytes 442376 | tf_op jit(solution)/shard_map/ppermute | solution.py:509
  40.0 5.9 %collective-permute-start.5 = (s16[144,512]{1,0:T(8,128)(2,1)S(1)}, s16[144,512]{1,0:T(8,128)(2,1)S(1)}, u32[]{:S(2)}, u32[]{:S(2)}) collective-permute-start(s16[144,512]{1,0:T(8,128)(2,1)S(1)} %get-tuple-element.48.refs_4_.refs_9_), channel_id=1, source_target_pairs={{0,8},{8,0},{16,24},{24,16},{1,9},{9,1},{17,25},{25,17},{2,10},{10... | collective-permute-start | bytes 442376 | tf_op jit(solution)/shard_map/ppermute | solution.py:509
  48.6 15.0 %collective-permute-start.20 = (s16[528,512]{1,0:T(8,128)(2,1)S(1)}, s16[528,512]{1,0:T(8,128)(2,1)S(1)}, u32[]{:S(2)}, u32[]{:S(2)}) collective-permute-start(s16[528,512]{1,0:T(8,128)(2,1)S(1)} %get-tuple-element.69), channel_id=1, source_target_pairs={{0,16},{8,24},{16,0},{24,8},{1,17},{9,25},{17,1},{25,9},{2,18},{10... | collective-permute-start | bytes 1622024 | tf_op jit(solution)/shard_map/ppermute | solution.py:509
  49.2 16.6 %collective-permute-start.15 = (s16[528,512]{1,0:T(8,128)(2,1)S(1)}, s16[528,512]{1,0:T(8,128)(2,1)S(1)}, u32[]{:S(2)}, u32[]{:S(2)}) collective-permute-start(s16[528,512]{1,0:T(8,128)(2,1)S(1)} %get-tuple-element.58), channel_id=1, source_target_pairs={{0,8},{8,0},{16,24},{24,16},{1,9},{9,1},{17,25},{25,17},{2,10},{10... | collective-permute-start | bytes 1622024 | tf_op jit(solution)/shard_map/ppermute | solution.py:509
  51.6 1.2 %collective-permute-start.16 = (f32[3,8,128]{2,1,0:T(8,128)S(1)}, f32[3,8,128]{2,1,0:T(8,128)S(1)}, u32[]{:S(2)}, u32[]{:S(2)}) collective-permute-start(f32[3,8,128]{2,1,0:T(8,128)S(1)} %get-tuple-element.61), channel_id=1, source_target_pairs={{0,1},{1,0},{2,3},{3,2},{4,5},{5,4},{6,7},{7,6},{8,9},{9,8},{10,11... | collective-permute-start | bytes 36872 | tf_op jit(solution)/shard_map/ppermute | solution.py:506
  52.9 5.9 %collective-permute-start.17 = (f32[2,8,128]{2,1,0:T(8,128)S(1)}, f32[2,8,128]{2,1,0:T(8,128)S(1)}, u32[]{:S(2)}, u32[]{:S(2)}) collective-permute-start(f32[2,8,128]{2,1,0:T(8,128)S(1)} %get-tuple-element.63), channel_id=1, source_target_pairs={{0,4},{1,5},{2,6},{3,7},{4,0},{5,1},{6,2},{7,3},{8,12},{9,13},{10,... | collective-permute-start | bytes 24584 | tf_op jit(solution)/shard_map/ppermute | solution.py:503
  58.8 4.8 %collective-permute-start.18 = (f32[8,128]{1,0:T(8,128)S(1)}, f32[8,128]{1,0:T(8,128)S(1)}, u32[]{:S(2)}, u32[]{:S(2)}) collective-permute-start(f32[8,128]{1,0:T(8,128)S(1)} %get-tuple-element.65), channel_id=1, source_target_pairs={{0,2},{1,3},{2,0},{3,1},{4,6},{5,7},{6,4},{7,5},{8,10},{9,11},{10,... | collective-permute-start | bytes 12296 | tf_op jit(solution)/shard_map/ppermute | solution.py:503
  64.2 9.4 %collective-permute-start.21 = (s16[272,512]{1,0:T(8,128)(2,1)S(1)}, s16[272,512]{1,0:T(8,128)(2,1)S(1)}, u32[]{:S(2)}, u32[]{:S(2)}) collective-permute-start(s16[272,512]{1,0:T(8,128)(2,1)S(1)} %get-tuple-element.71), channel_id=1, source_target_pairs={{0,8},{8,0},{16,24},{24,16},{1,9},{9,1},{17,25},{25,17},{2,10},{10... | collective-permute-start | bytes 835592 | tf_op jit(solution)/shard_map/ppermute | solution.py:509
  66.5 7.2 %collective-permute-start.19 = (s16[272,512]{1,0:T(8,128)(2,1)S(1)}, s16[272,512]{1,0:T(8,128)(2,1)S(1)}, u32[]{:S(2)}, u32[]{:S(2)}) collective-permute-start(s16[272,512]{1,0:T(8,128)(2,1)S(1)} %get-tuple-element.66), channel_id=1, source_target_pairs={{0,16},{8,24},{16,0},{24,8},{1,17},{9,25},{17,1},{25,9},{2,18},{10... | collective-permute-start | bytes 835592 | tf_op jit(solution)/shard_map/ppermute | solution.py:509
  68.1 4.6 %collective-permute-start.24 = (f32[8,128]{1,0:T(8,128)S(1)}, f32[8,128]{1,0:T(8,128)S(1)}, u32[]{:S(2)}, u32[]{:S(2)}) collective-permute-start(f32[8,128]{1,0:T(8,128)S(1)} %add_kernel.1.refs_0_), channel_id=1, source_target_pairs={{0,24},{8,16},{16,8},{24,0},{1,25},{9,17},{17,9},{25,1},{2,26},{10... | collective-permute-start | bytes 12296 | tf_op jit(solution)/shard_map/ppermute | solution.py:509
  68.5 4.9 %collective-permute-start.23 = (f32[8,128]{1,0:T(8,128)S(1)}, f32[8,128]{1,0:T(8,128)S(1)}, u32[]{:S(2)}, u32[]{:S(2)}) collective-permute-start(f32[8,128]{1,0:T(8,128)S(1)} %add_kernel.1.refs_0_), channel_id=1, source_target_pairs={{0,16},{8,24},{16,0},{24,8},{1,17},{9,25},{17,1},{25,9},{2,18},{10... | collective-permute-start | bytes 12296 | tf_op jit(solution)/shard_map/ppermute | solution.py:509
  70.0 3.6 %collective-permute-start.22 = (f32[8,128]{1,0:T(8,128)S(1)}, f32[8,128]{1,0:T(8,128)S(1)}, u32[]{:S(2)}, u32[]{:S(2)}) collective-permute-start(f32[8,128]{1,0:T(8,128)S(1)} %add_kernel.1.refs_0_), channel_id=1, source_target_pairs={{0,8},{8,0},{16,24},{24,16},{1,9},{9,1},{17,25},{25,17},{2,10},{10... | collective-permute-start | bytes 12296 | tf_op jit(solution)/shard_map/ppermute | solution.py:509

commit v3 on v1

--- a/solution.py
+++ b/solution.py
@@ -245,10 +245,11 @@
     )(*blocks, *after)
 
 
-def take_kernel(over_x, over_y, one, other, sem):
+def take_kernel(over_x, over_y, block, one, other, again, sem):
     copies = [
         pltpu.make_async_copy(over_x.at[0], one, sem.at[0]),
         pltpu.make_async_copy(over_y.at[1], other, sem.at[1]),
+        pltpu.make_async_copy(block, again, sem.at[2]),
     ]
     for copy in copies:
         copy.start()
@@ -256,18 +257,18 @@
         copy.wait()
 
 
-def take(over_x, over_y):
+def take(over_x, over_y, block):
     out = like(over_x.shape[1:], over_x.dtype)
     return pl.pallas_call(
         take_kernel,
-        in_specs=[VMEM] * 2,
-        out_specs=[VMEM] * 2,
-        out_shape=[out, out],
-        scratch_shapes=[pltpu.SemaphoreType.DMA((2,))],
+        in_specs=[VMEM] * 3,
+        out_specs=[VMEM] * 3,
+        out_shape=[out, out, like(block.shape, block.dtype)],
+        scratch_shapes=[pltpu.SemaphoreType.DMA((3,))],
         compiler_params=pltpu.CompilerParams(vmem_limit_bytes=8 * MIB),
         cost_estimate=cost([out, out]),
         name="take",
-    )(over_x, over_y)
+    )(over_x, over_y, block)
 
 
 def expert_view(info, expert, top):
@@ -512,23 +513,24 @@
     up1 = along(block, [(0, 1), (1, 2), (2, 3)])
     down1 = along(block, [(2, 1), (1, 0)])
     stored = [other_hidden, over(other_hidden, 1), over(other_hidden, 2)]
-    passed = take(stored[1], stored[2])
+    *passed, again = take(stored[1], stored[2], block)
     far_stored = [over(passed[0], 2), over(passed[1], 1)]
     weight = load(block, down_weight)
 
-    (first,) = pick(((0, 0, 0, 1),), (block, up1), (weight,))
+    (first,) = pick(((0, 0, 0, 1),), (block, up1), (weight, down1))
     up2 = along(up1, [(1, 2), (2, 3)])
+    down2 = along(again, [(2, 0)])
     pair = (first, across(first))
     sent, kept = [], []
     for local in range(2):
         send, keep, info = partial_share(
-            local, most, top, (0,), capacity, weight, pair, after=passed if local else ()
+            local, most, top, (0,), capacity, weight, pair, after=far_stored if local else ()
         )
         sent.append(send)
         kept.append(keep)
 
-    second, relay = pick(((1, 0, 0, 2), (1, 1, 2, 2)), (up1, down1, up2), (*sent, *far_stored))
-    third = along(relay, [(2, 3), (1, 0)])
+    up3 = along(up2, [(2, 3)])
+    (second,) = pick(((2, 0, 0, 1),), (up1, up2, down1), (*sent, *far_stored))
     blocks = [second, across(second)]
 
     sums, onward = [], []
@@ -536,7 +538,7 @@
         send, rest = middle(over(sent[local], 1 + local), kept[local])
         onward.append(send)
         sums += [over(send, 2 - local), rest]
-    (third,) = pick(((1, 0, 0, 1),), (relay, third), onward)
+    (third,) = pick(((0, 1, 2, 3),), (down2, down1, up2, up3), ())
     blocks += [third, across(third)]
 
     halves = []

time: 75 us -> 75.5 us (level)
  starting transfers between devices: 28.9 us -> 37.5 us
  waiting for transfers between devices: 24.9 us -> 16.8 us
    ppermute x15, waiting for transfers between devices: 13.8 us -> 5.86 us  [over(): return lax.ppermute(rows, 'dp', [(i, i ^ flip) for i in range(ranks)])]
    ppermute x6 -> x7, starting transfers between devices: 12.8 us -> 18.2 us  [along(): lax.ppermute(rows, 'expert', [(2 * a + c, 2 * b + c) for a, b in pairs fo...]
    ppermute x15, starting transfers between devices: 15.9 us -> 19 us  [over(): return lax.ppermute(rows, 'dp', [(i, i ^ flip) for i in range(ranks)])]
    ppermute x6 -> x7, waiting for transfers between devices: 9.86 us -> 9.77 us  [along(): lax.ppermute(rows, 'expert', [(2 * a + c, 2 * b + c) for a, b in pairs fo...]
  transfers between devices with their start and end apart: 25 -> 26, of which waited for: 14 -> 13; matrix products, arithmetic and copies ran while one was open for 0% -> 0% of each run, Pallas kernels for 19% -> 23%
where the time goes in v3:
time: 75.5 us; the launch traced here: 75.2 us
  starting transfers between devices  37.5 us (50%)
  Pallas kernels  20.1 us (27%)
  waiting for transfers between devices  16.8 us (22%)
  between operations  0.87 us (1%)
    ppermute x15, starting transfers between devices, over(): return lax.ppermute(rows, 'dp', [(i, i ^ flip) for i in range(ranks)])  19 us
    ppermute x7, starting transfers between devices, along(): lax.ppermute(rows, 'expert', [(2 * a + c, 2 * b + c) for a, b in pairs fo...  18.2 us
    pallas_call x4, Pallas kernels, partial_share(): pl.pallas_call(functools.partial(share_kernel, local, most, top, group, e...  10.3 us
    ppermute x7, waiting for transfers between devices, along(): lax.ppermute(rows, 'expert', [(2 * a + c, 2 * b + c) for a, b in pairs fo...  9.77 us
    ppermute x15, waiting for transfers between devices, over(): return lax.ppermute(rows, 'dp', [(i, i ^ flip) for i in range(ranks)])  5.86 us
    pallas_call x1, Pallas kernels, load(): pl.pallas_call(load_kernel, in_specs=[ANY, ANY], out_specs=VMEM, out_shap...  3.39 us
    pallas_call x4, Pallas kernels, middle(): pl.pallas_call(middle_kernel, in_specs=[VMEM, VMEM] + [ANY] * len(after),...  2.17 us
    pallas_call x1, Pallas kernels, finish(): pl.pallas_call(functools.partial(finish_kernel, most), in_specs=[VMEM] *...  1.53 us
  transfers between devices with their start and end apart: 26, of which 13 were waited for; matrix products, arithmetic and copies ran while one was open for 0% of the time, Pallas kernels for 23%

profile of v3, /device:TPU:0, one launch (start us, length us, event | category | flops | bytes accessed | tf_op | source)
XLA Modules:
  0.0 75.2 jit_solution(2168463161213082881)
XLA Ops:
  0.6 1.4 %prepare.1 = (bf16[144,1024]{1,0:T(8,128)(2,1)S(1)}, bf16[2,128,512]{2,1,0:T(8,128)(2,1)S(1)}, bf16[2,256,512]{2,1,0:T(8,128)(2,1)S(1)}) custom-call(bf16[128,1024]{1,0:T(8,128)(2,1)} %rows.1, s32[8,128]{1,0:T(8,128)} %bitcast.4, s32[8,128]{1,0:T(8,128)} %bitcast.5, bf16[8,128]{1,0:T(8,128)(2,1)} %bitcast.6, bf16[2,384,512]{2,1,0:T(8,128)(2,1)} %hidden.1), custom_call_target="tpu_custom_call" | custom-call | bytes 1310720 | tf_op jit(solution)/shard_map/prepare/pallas_call | solution.py:177
  2.0 4.9 %collective-permute-start = (bf16[144,1024]{1,0:T(8,128)(2,1)S(1)}, bf16[144,1024]{1,0:T(8,128)(2,1)S(1)}, u32[]{:S(2)}, u32[]{:S(2)}) collective-permute-start(bf16[144,1024]{1,0:T(8,128)(2,1)S(1)} %get-tuple-element.41.after.refs_0_.block), channel_id=1, source_target_pairs={{0,2},{1,3},{2,4},{3,5},{4,6},{5,7},{8,10},{9,11},{10,12},{11,13},... | collective-permute-start | bytes 884744 | tf_op jit(solution)/shard_map/ppermute | solution.py:504
  7.0 1.6 %collective-permute-start.4 = (bf16[2,256,512]{2,1,0:T(8,128)(2,1)S(1)}, bf16[2,256,512]{2,1,0:T(8,128)(2,1)S(1)}, u32[]{:S(2)}, u32[]{:S(2)}) collective-permute-start(bf16[2,256,512]{2,1,0:T(8,128)(2,1)S(1)} %get-tuple-element.42.refs_4_), channel_id=1, source_target_pairs={{0,16},{8,24},{16,0},{24,8},{1,17},{9,25},{17,1},{25,9},{2,18},{10... | collective-permute-start | bytes 1572872 | tf_op jit(solution)/shard_map/ppermute | solution.py:510
  8.5 1.5 %collective-permute-start.3 = (bf16[2,256,512]{2,1,0:T(8,128)(2,1)S(1)}, bf16[2,256,512]{2,1,0:T(8,128)(2,1)S(1)}, u32[]{:S(2)}, u32[]{:S(2)}) collective-permute-start(bf16[2,256,512]{2,1,0:T(8,128)(2,1)S(1)} %get-tuple-element.42.refs_4_), channel_id=1, source_target_pairs={{0,8},{8,0},{16,24},{24,16},{1,9},{9,1},{17,25},{25,17},{2,10},{10... | collective-permute-start | bytes 1572872 | tf_op jit(solution)/shard_map/ppermute | solution.py:510
  10.0 1.3 %collective-permute-start.1 = (bf16[144,1024]{1,0:T(8,128)(2,1)S(1)}, bf16[144,1024]{1,0:T(8,128)(2,1)S(1)}, u32[]{:S(2)}, u32[]{:S(2)}) collective-permute-start(bf16[144,1024]{1,0:T(8,128)(2,1)S(1)} %get-tuple-element.41.after.refs_0_.block), channel_id=1, source_target_pairs={{4,2},{5,3},{2,0},{3,1},{12,10},{13,11},{10,8},{11,9},{20,18},{21,... | collective-permute-start | bytes 884744 | tf_op jit(solution)/shard_map/ppermute | solution.py:504
  11.3 1.9 %collective-permute-done.refs_1_.refs_0_ = bf16[144,1024]{1,0:T(8,128)(2,1)S(1)} collective-permute-done((bf16[144,1024]{1,0:T(8,128)(2,1)S(1)}, bf16[144,1024]{1,0:T(8,128)(2,1)S(1)}, u32[]{:S(2)}, u32[]{:S(2)}) %collective-permute-start) | collective-permute-done | bytes 294944 | tf_op jit(solution)/shard_map/ppermute | solution.py:504
  13.9 3.4 %load_weight.1.refs_2_.weight = bf16[2,2048,1024]{2,1,0:T(8,128)(2,1)S(1)} custom-call(bf16[144,1024]{1,0:T(8,128)(2,1)S(1)} %get-tuple-element.41.after.refs_0_.block, bf16[2,2048,1024]{2,1,0:T(8,128)(2,1)} %weight.1), custom_call_target="tpu_custom_call" | custom-call | bytes 16777216 | tf_op jit(solution)/shard_map/load_weight/pallas_call | solution.py:205
  17.3 2.5 %collective-permute-done.1.refs_3_.refs_2_.refs_1_ = bf16[144,1024]{1,0:T(8,128)(2,1)S(1)} collective-permute-done((bf16[144,1024]{1,0:T(8,128)(2,1)S(1)}, bf16[144,1024]{1,0:T(8,128)(2,1)S(1)}, u32[]{:S(2)}, u32[]{:S(2)}) %collective-permute-start.1) | collective-permute-done | bytes 294944 | tf_op jit(solution)/shard_map/ppermute | solution.py:504
  20.4 1.2 %collective-permute-done.3.over_x.refs_5_ = bf16[2,256,512]{2,1,0:T(8,128)(2,1)S(1)} collective-permute-done((bf16[2,256,512]{2,1,0:T(8,128)(2,1)S(1)}, bf16[2,256,512]{2,1,0:T(8,128)(2,1)S(1)}, u32[]{:S(2)}, u32[]{:S(2)}) %collective-permute-start.3) | collective-permute-done | bytes 524320 | tf_op jit(solution)/shard_map/ppermute | solution.py:510
  22.3 1.5 %collective-permute-start.6 = (bf16[256,512]{1,0:T(8,128)(2,1)S(1)}, bf16[256,512]{1,0:T(8,128)(2,1)S(1)}, u32[]{:S(2)}, u32[]{:S(2)}) collective-permute-start(bf16[256,512]{1,0:T(8,128)(2,1)S(1)} %get-tuple-element.44), channel_id=1, source_target_pairs={{0,8},{8,0},{16,24},{24,16},{1,9},{9,1},{17,25},{25,17},{2,10},{10... | collective-permute-start | bytes 786440 | tf_op jit(solution)/shard_map/ppermute | solution.py:510
  23.8 1.3 %collective-permute-start.13 = (bf16[144,1024]{1,0:T(8,128)(2,1)S(1)}, bf16[144,1024]{1,0:T(8,128)(2,1)S(1)}, u32[]{:S(2)}, u32[]{:S(2)}) collective-permute-start(bf16[144,1024]{1,0:T(8,128)(2,1)S(1)} %get-tuple-element.54), channel_id=1, source_target_pairs={{4,0},{5,1},{12,8},{13,9},{20,16},{21,17},{28,24},{29,25}} | collective-permute-start | bytes 884744 | tf_op jit(solution)/shard_map/ppermute | solution.py:504
  25.8 2.7 %share_0.2 = (s16[272,512]{1,0:T(8,128)(2,1)S(1)}, f32[2,128,512]{2,1,0:T(8,128)S(1)}, f32[2,16,384]{2,1,0:T(8,128)}) custom-call(s32[2]{0:T(128)S(1)} %copy-done, bf16[2,2048,1024]{2,1,0:T(8,128)(2,1)S(1)} %load_weight.1.refs_2_.weight, bf16[144,1024]{1,0:T(8,128)(2,1)S(1)} %pick.3.refs_0_, bf16[144,1024]{1,0:T(8,128)(2,1)S(1)} %collective-permute-done.2.refs_1_), custom_call_target="tpu_custom_call" | custom-call | flops 536870912 | bytes 8978432 | tf_op jit(solution)/shard_map/share_0/pallas_call | solution.py:370
  29.2 2.2 %share_1.2 = (s16[272,512]{1,0:T(8,128)(2,1)S(1)}, f32[2,128,512]{2,1,0:T(8,128)S(1)}, f32[2,16,384]{2,1,0:T(8,128)S(1)}) custom-call(s32[2]{0:T(128)S(1)} %copy-done, bf16[2,2048,1024]{2,1,0:T(8,128)(2,1)S(1)} %load_weight.1.refs_2_.weight, bf16[144,1024]{1,0:T(8,128)(2,1)S(1)} %pick.3.refs_0_, bf16[144,1024]{1,0:T(8,128)(2,1)S(1)} %collective-permute-done.2.refs_1_, ...), custom_call_target="tpu_custom_call" | custom-call | flops 536870912 | bytes 8978432 | tf_op jit(solution)/shard_map/share_1/pallas_call | solution.py:370
  31.4 1.7 %collective-permute-start.9 = (s16[272,512]{1,0:T(8,128)(2,1)S(1)}, s16[272,512]{1,0:T(8,128)(2,1)S(1)}, u32[]{:S(2)}, u32[]{:S(2)}) collective-permute-start(s16[272,512]{1,0:T(8,128)(2,1)S(1)} %get-tuple-element.50.refs_4_), channel_id=1, source_target_pairs={{0,16},{8,24},{16,0},{24,8},{1,17},{9,25},{17,1},{25,9},{2,18},{10... | collective-permute-start | bytes 835592 | tf_op jit(solution)/shard_map/ppermute | solution.py:510
  33.2 2.1 %collective-permute-done.13.refs_0_ = bf16[144,1024]{1,0:T(8,128)(2,1)S(1)} collective-permute-done((bf16[144,1024]{1,0:T(8,128)(2,1)S(1)}, bf16[144,1024]{1,0:T(8,128)(2,1)S(1)}, u32[]{:S(2)}, u32[]{:S(2)}) %collective-permute-start.13) | collective-permute-done | bytes 294944 | tf_op jit(solution)/shard_map/ppermute | solution.py:504
  36.0 1.1 %collective-permute-start.8 = (s16[144,512]{1,0:T(8,128)(2,1)S(1)}, s16[144,512]{1,0:T(8,128)(2,1)S(1)}, u32[]{:S(2)}, u32[]{:S(2)}) collective-permute-start(s16[144,512]{1,0:T(8,128)(2,1)S(1)} %get-tuple-element.48.refs_8_), channel_id=1, source_target_pairs={{0,16},{8,24},{16,0},{24,8},{1,17},{9,25},{17,1},{25,9},{2,18},{10... | collective-permute-start | bytes 442376 | tf_op jit(solution)/shard_map/ppermute | solution.py:510
  38.5 1.5 %collective-permute-start.10 = (s16[144,512]{1,0:T(8,128)(2,1)S(1)}, s16[144,512]{1,0:T(8,128)(2,1)S(1)}, u32[]{:S(2)}, u32[]{:S(2)}) collective-permute-start(s16[144,512]{1,0:T(8,128)(2,1)S(1)} %get-tuple-element.52.refs_9_), channel_id=1, source_target_pairs={{0,8},{8,0},{16,24},{24,16},{1,9},{9,1},{17,25},{25,17},{2,10},{10... | collective-permute-start | bytes 442376 | tf_op jit(solution)/shard_map/ppermute | solution.py:510
  39.9 2.7 %share_0.3 = (s16[528,512]{1,0:T(8,128)(2,1)S(1)}, f32[2,256,512]{2,1,0:T(8,128)S(1)}, f32[256,128]{1,0:T(8,128)S(1)}, f32[3,8,128]{2,1,0:T(8,128)S(1)}, f32[3,8,128]{2,1,0:T(8,128)S(1)}) custom-call(s32[2]{0:T(128)S(1)} %copy-done, bf16[2,2048,1024]{2,1,0:T(8,128)(2,1)S(1)} %load_weight.1.refs_2_.weight, bf16[144,1024]{1,0:T(8,128)(2,1)S(1)} %pick.4.refs_0_, ...), custom_call_target="tpu_custom_call" | custom-call | flops 1073741824 | bytes 9568256 | tf_op jit(solution)/shard_map/share_0/pallas_call | solution.py:370
  43.3 1.1 %collective-permute-done.10.refs_11_.got1 = s16[144,512]{1,0:T(8,128)(2,1)S(1)} collective-permute-done((s16[144,512]{1,0:T(8,128)(2,1)S(1)}, s16[144,512]{1,0:T(8,128)(2,1)S(1)}, u32[]{:S(2)}, u32[]{:S(2)}) %collective-permute-start.10) | collective-permute-done | bytes 147488 | tf_op jit(solution)/shard_map/ppermute | solution.py:510
  44.5 2.7 %share_1.3 = (s16[528,512]{1,0:T(8,128)(2,1)S(1)}, f32[2,256,512]{2,1,0:T(8,128)S(1)}, f32[256,128]{1,0:T(8,128)S(1)}, f32[3,8,128]{2,1,0:T(8,128)S(1)}, f32[3,8,128]{2,1,0:T(8,128)S(1)}) custom-call(s32[2]{0:T(128)S(1)} %copy-done, bf16[2,2048,1024]{2,1,0:T(8,128)(2,1)S(1)} %load_weight.1.refs_2_.weight, bf16[144,1024]{1,0:T(8,128)(2,1)S(1)} %pick.4.refs_0_, ...), custom_call_target="tpu_custom_call" | custom-call | flops 1073741824 | bytes 9568256 | tf_op jit(solution)/shard_map/share_1/pallas_call | solution.py:370
  47.2 1.8 %collective-permute-start.21 = (s16[528,512]{1,0:T(8,128)(2,1)S(1)}, s16[528,512]{1,0:T(8,128)(2,1)S(1)}, u32[]{:S(2)}, u32[]{:S(2)}) collective-permute-start(s16[528,512]{1,0:T(8,128)(2,1)S(1)} %get-tuple-element.71), channel_id=1, source_target_pairs={{0,16},{8,24},{16,0},{24,8},{1,17},{9,25},{17,1},{25,9},{2,18},{10... | collective-permute-start | bytes 1622024 | tf_op jit(solution)/shard_map/ppermute | solution.py:510
  50.0 1.2 %collective-permute-done.17.got = f32[3,8,128]{2,1,0:T(8,128)S(1)} collective-permute-done((f32[3,8,128]{2,1,0:T(8,128)S(1)}, f32[3,8,128]{2,1,0:T(8,128)S(1)}, u32[]{:S(2)}, u32[]{:S(2)}) %collective-permute-start.17) | collective-permute-done | bytes 12320 | tf_op jit(solution)/shard_map/ppermute | solution.py:507
  51.1 7.3 %collective-permute-start.18 = (f32[2,8,128]{2,1,0:T(8,128)S(1)}, f32[2,8,128]{2,1,0:T(8,128)S(1)}, u32[]{:S(2)}, u32[]{:S(2)}) collective-permute-start(f32[2,8,128]{2,1,0:T(8,128)S(1)} %get-tuple-element.65), channel_id=1, source_target_pairs={{0,4},{1,5},{2,6},{3,7},{4,0},{5,1},{6,2},{7,3},{8,12},{9,13},{10,... | collective-permute-start | bytes 24584 | tf_op jit(solution)/shard_map/ppermute | solution.py:504
  58.4 1.6 %collective-permute-done.18.got = f32[2,8,128]{2,1,0:T(8,128)S(1)} collective-permute-done((f32[2,8,128]{2,1,0:T(8,128)S(1)}, f32[2,8,128]{2,1,0:T(8,128)S(1)}, u32[]{:S(2)}, u32[]{:S(2)}) %collective-permute-start.18) | collective-permute-done | bytes 8224 | tf_op jit(solution)/shard_map/ppermute | solution.py:504
  60.1 2.0 %collective-permute-start.19 = (f32[8,128]{1,0:T(8,128)S(1)}, f32[8,128]{1,0:T(8,128)S(1)}, u32[]{:S(2)}, u32[]{:S(2)}) collective-permute-start(f32[8,128]{1,0:T(8,128)S(1)} %get-tuple-element.67), channel_id=1, source_target_pairs={{0,2},{1,3},{2,0},{3,1},{4,6},{5,7},{6,4},{7,5},{8,10},{9,11},{10,... | collective-permute-start | bytes 12296 | tf_op jit(solution)/shard_map/ppermute | solution.py:504
  62.1 1.6 %collective-permute-done.19.refs_1_ = f32[8,128]{1,0:T(8,128)S(1)} collective-permute-done((f32[8,128]{1,0:T(8,128)S(1)}, f32[8,128]{1,0:T(8,128)S(1)}, u32[]{:S(2)}, u32[]{:S(2)}) %collective-permute-start.19) | collective-permute-done | bytes 4128 | tf_op jit(solution)/shard_map/ppermute | solution.py:504
  64.4 1.5 %collective-permute-start.20 = (s16[272,512]{1,0:T(8,128)(2,1)S(1)}, s16[272,512]{1,0:T(8,128)(2,1)S(1)}, u32[]{:S(2)}, u32[]{:S(2)}) collective-permute-start(s16[272,512]{1,0:T(8,128)(2,1)S(1)} %get-tuple-element.68), channel_id=1, source_target_pairs={{0,16},{8,24},{16,0},{24,8},{1,17},{9,25},{17,1},{25,9},{2,18},{10... | collective-permute-start | bytes 835592 | tf_op jit(solution)/shard_map/ppermute | solution.py:510
  66.5 1.6 %collective-permute-start.22 = (s16[272,512]{1,0:T(8,128)(2,1)S(1)}, s16[272,512]{1,0:T(8,128)(2,1)S(1)}, u32[]{:S(2)}, u32[]{:S(2)}) collective-permute-start(s16[272,512]{1,0:T(8,128)(2,1)S(1)} %get-tuple-element.73), channel_id=1, source_target_pairs={{0,8},{8,0},{16,24},{24,16},{1,9},{9,1},{17,25},{25,17},{2,10},{10... | collective-permute-start | bytes 835592 | tf_op jit(solution)/shard_map/ppermute | solution.py:510
  68.6 1.5 %collective-permute-start.24 = (f32[8,128]{1,0:T(8,128)S(1)}, f32[8,128]{1,0:T(8,128)S(1)}, u32[]{:S(2)}, u32[]{:S(2)}) collective-permute-start(f32[8,128]{1,0:T(8,128)S(1)} %add_kernel.1.refs_0_), channel_id=1, source_target_pairs={{0,16},{8,24},{16,0},{24,8},{1,17},{9,25},{17,1},{25,9},{2,18},{10... | collective-permute-start | bytes 12296 | tf_op jit(solution)/shard_map/ppermute | solution.py:510
  70.1 1.6 %collective-permute-start.23 = (f32[8,128]{1,0:T(8,128)S(1)}, f32[8,128]{1,0:T(8,128)S(1)}, u32[]{:S(2)}, u32[]{:S(2)}) collective-permute-start(f32[8,128]{1,0:T(8,128)S(1)} %add_kernel.1.refs_0_), channel_id=1, source_target_pairs={{0,8},{8,0},{16,24},{24,16},{1,9},{9,1},{17,25},{25,17},{2,10},{10... | collective-permute-start | bytes 12296 | tf_op jit(solution)/shard_map/ppermute | solution.py:510
  71.7 1.5 %collective-permute-done.25.refs_3_ = f32[8,128]{1,0:T(8,128)S(1)} collective-permute-done((f32[8,128]{1,0:T(8,128)S(1)}, f32[8,128]{1,0:T(8,128)S(1)}, u32[]{:S(2)}, u32[]{:S(2)}) %collective-permute-start.25) | collective-permute-done | bytes 4128 | tf_op jit(solution)/shard_map/ppermute | solution.py:510
  73.7 1.5 %finish.1 = (f32[2,384,512]{2,1,0:T(8,128)}, f32[8,128]{1,0:T(8,128)}) custom-call(f32[2,128,512]{2,1,0:T(8,128)S(1)} %get-tuple-element.59.first, s16[272,512]{1,0:T(8,128)(2,1)S(1)} %collective-permute-done.20.got0, f32[256,512]{1,0:T(8,128)S(1)} %get-tuple-element.69.rest0, f32[256,128]{1,0:T(8,128)S(1)} %get-tuple-element.70.gates0, ...), custom_call_target="tpu_custom_call" | custom-call | bytes 2916352 | tf_op jit(solution)/shard_map/finish/pallas_call | solution.py:452
  (41 shorter events, 9.3 us)
Async XLA Ops:
  2.0 11.2 %collective-permute-start = (bf16[144,1024]{1,0:T(8,128)(2,1)S(1)}, bf16[144,1024]{1,0:T(8,128)(2,1)S(1)}, u32[]{:S(2)}, u32[]{:S(2)}) collective-permute-start(bf16[144,1024]{1,0:T(8,128)(2,1)S(1)} %get-tuple-element.41.after.refs_0_.block), channel_id=1, source_target_pairs={{0,2},{1,3},{2,4},{3,5},{4,6},{5,7},{8,10},{9,11},{10,12},{11,13},... | collective-permute-start | bytes 884744 | tf_op jit(solution)/shard_map/ppermute | solution.py:504
  7.0 13.4 %collective-permute-start.4 = (bf16[2,256,512]{2,1,0:T(8,128)(2,1)S(1)}, bf16[2,256,512]{2,1,0:T(8,128)(2,1)S(1)}, u32[]{:S(2)}, u32[]{:S(2)}) collective-permute-start(bf16[2,256,512]{2,1,0:T(8,128)(2,1)S(1)} %get-tuple-element.42.refs_4_), channel_id=1, source_target_pairs={{0,16},{8,24},{16,0},{24,8},{1,17},{9,25},{17,1},{25,9},{2,18},{10... | collective-permute-start | bytes 1572872 | tf_op jit(solution)/shard_map/ppermute | solution.py:510
  8.5 13.1 %collective-permute-start.3 = (bf16[2,256,512]{2,1,0:T(8,128)(2,1)S(1)}, bf16[2,256,512]{2,1,0:T(8,128)(2,1)S(1)}, u32[]{:S(2)}, u32[]{:S(2)}) collective-permute-start(bf16[2,256,512]{2,1,0:T(8,128)(2,1)S(1)} %get-tuple-element.42.refs_4_), channel_id=1, source_target_pairs={{0,8},{8,0},{16,24},{24,16},{1,9},{9,1},{17,25},{25,17},{2,10},{10... | collective-permute-start | bytes 1572872 | tf_op jit(solution)/shard_map/ppermute | solution.py:510
  10.0 9.8 %collective-permute-start.1 = (bf16[144,1024]{1,0:T(8,128)(2,1)S(1)}, bf16[144,1024]{1,0:T(8,128)(2,1)S(1)}, u32[]{:S(2)}, u32[]{:S(2)}) collective-permute-start(bf16[144,1024]{1,0:T(8,128)(2,1)S(1)} %get-tuple-element.41.after.refs_0_.block), channel_id=1, source_target_pairs={{4,2},{5,3},{2,0},{3,1},{12,10},{13,11},{10,8},{11,9},{20,18},{21,... | collective-permute-start | bytes 884744 | tf_op jit(solution)/shard_map/ppermute | solution.py:504
  13.2 11.9 %collective-permute-start.11 = (bf16[144,1024]{1,0:T(8,128)(2,1)S(1)}, bf16[144,1024]{1,0:T(8,128)(2,1)S(1)}, u32[]{:S(2)}, u32[]{:S(2)}) collective-permute-start(bf16[144,1024]{1,0:T(8,128)(2,1)S(1)} %collective-permute-done.refs_1_.refs_0_), channel_id=1, source_target_pairs={{2,4},{3,5},{4,6},{5,7},{10,12},{11,13},{12,14},{13,15},{18,20},{1... | collective-permute-start | bytes 884744 | tf_op jit(solution)/shard_map/ppermute | solution.py:504
  17.3 8.6 %copy-start = (s32[2]{0:T(128)S(1)}, s32[2]{0:T(128)}, u32[]{:S(2)}) copy-start(s32[2]{0:T(128)} %cap.9) | copy-start | bytes 28
  19.9 5.9 %collective-permute-start.2 = (bf16[144,1024]{1,0:T(8,128)(2,1)S(1)}, bf16[144,1024]{1,0:T(8,128)(2,1)S(1)}, u32[]{:S(2)}, u32[]{:S(2)}) collective-permute-start(bf16[144,1024]{1,0:T(8,128)(2,1)S(1)} %pick.3.refs_0_), channel_id=1, source_target_pairs={{0,1},{1,0},{2,3},{3,2},{4,5},{5,4},{6,7},{7,6},{8,9},{9,8},{10,11... | collective-permute-start | bytes 884744 | tf_op jit(solution)/shard_map/ppermute | solution.py:507
  21.8 7.3 %collective-permute-start.5 = (bf16[256,512]{1,0:T(8,128)(2,1)S(1)}, bf16[256,512]{1,0:T(8,128)(2,1)S(1)}, u32[]{:S(2)}, u32[]{:S(2)}) collective-permute-start(bf16[256,512]{1,0:T(8,128)(2,1)S(1)} %get-tuple-element.43), channel_id=1, source_target_pairs={{0,16},{8,24},{16,0},{24,8},{1,17},{9,25},{17,1},{25,9},{2,18},{10... | collective-permute-start | bytes 786440 | tf_op jit(solution)/shard_map/ppermute | solution.py:510
  22.3 6.8 %collective-permute-start.6 = (bf16[256,512]{1,0:T(8,128)(2,1)S(1)}, bf16[256,512]{1,0:T(8,128)(2,1)S(1)}, u32[]{:S(2)}, u32[]{:S(2)}) collective-permute-start(bf16[256,512]{1,0:T(8,128)(2,1)S(1)} %get-tuple-element.44), channel_id=1, source_target_pairs={{0,8},{8,0},{16,24},{24,16},{1,9},{9,1},{17,25},{25,17},{2,10},{10... | collective-permute-start | bytes 786440 | tf_op jit(solution)/shard_map/ppermute | solution.py:510
  23.8 11.5 %collective-permute-start.13 = (bf16[144,1024]{1,0:T(8,128)(2,1)S(1)}, bf16[144,1024]{1,0:T(8,128)(2,1)S(1)}, u32[]{:S(2)}, u32[]{:S(2)}) collective-permute-start(bf16[144,1024]{1,0:T(8,128)(2,1)S(1)} %get-tuple-element.54), channel_id=1, source_target_pairs={{4,0},{5,1},{12,8},{13,9},{20,16},{21,17},{28,24},{29,25}} | collective-permute-start | bytes 884744 | tf_op jit(solution)/shard_map/ppermute | solution.py:504
  25.1 10.2 %collective-permute-start.14 = (bf16[144,1024]{1,0:T(8,128)(2,1)S(1)}, bf16[144,1024]{1,0:T(8,128)(2,1)S(1)}, u32[]{:S(2)}, u32[]{:S(2)}) collective-permute-start(bf16[144,1024]{1,0:T(8,128)(2,1)S(1)} %collective-permute-done.11.refs_1_.refs_2_), channel_id=1, source_target_pairs={{4,6},{5,7},{12,14},{13,15},{20,22},{21,23},{28,30},{29,31}} | collective-permute-start | bytes 884744 | tf_op jit(solution)/shard_map/ppermute | solution.py:504
  28.5 7.0 %collective-permute-start.7 = (s16[272,512]{1,0:T(8,128)(2,1)S(1)}, s16[272,512]{1,0:T(8,128)(2,1)S(1)}, u32[]{:S(2)}, u32[]{:S(2)}) collective-permute-start(s16[272,512]{1,0:T(8,128)(2,1)S(1)} %get-tuple-element.46.refs_3_), channel_id=1, source_target_pairs={{0,8},{8,0},{16,24},{24,16},{1,9},{9,1},{17,25},{25,17},{2,10},{10... | collective-permute-start | bytes 835592 | tf_op jit(solution)/shard_map/ppermute | solution.py:510
  31.4 6.6 %collective-permute-start.9 = (s16[272,512]{1,0:T(8,128)(2,1)S(1)}, s16[272,512]{1,0:T(8,128)(2,1)S(1)}, u32[]{:S(2)}, u32[]{:S(2)}) collective-permute-start(s16[272,512]{1,0:T(8,128)(2,1)S(1)} %get-tuple-element.50.refs_4_), channel_id=1, source_target_pairs={{0,16},{8,24},{16,0},{24,8},{1,17},{9,25},{17,1},{25,9},{2,18},{10... | collective-permute-start | bytes 835592 | tf_op jit(solution)/shard_map/ppermute | solution.py:510
  33.1 6.8 %collective-permute-start.12 = (bf16[144,1024]{1,0:T(8,128)(2,1)S(1)}, bf16[144,1024]{1,0:T(8,128)(2,1)S(1)}, u32[]{:S(2)}, u32[]{:S(2)}) collective-permute-start(bf16[144,1024]{1,0:T(8,128)(2,1)S(1)} %pick.4.refs_0_), channel_id=1, source_target_pairs={{0,1},{1,0},{2,3},{3,2},{4,5},{5,4},{6,7},{7,6},{8,9},{9,8},{10,11... | collective-permute-start | bytes 884744 | tf_op jit(solution)/shard_map/ppermute | solution.py:507
  35.4 4.5 %collective-permute-start.15 = (bf16[144,1024]{1,0:T(8,128)(2,1)S(1)}, bf16[144,1024]{1,0:T(8,128)(2,1)S(1)}, u32[]{:S(2)}, u32[]{:S(2)}) collective-permute-start(bf16[144,1024]{1,0:T(8,128)(2,1)S(1)} %pick.5.refs_2_), channel_id=1, source_target_pairs={{0,1},{1,0},{2,3},{3,2},{4,5},{5,4},{6,7},{7,6},{8,9},{9,8},{10,11... | collective-permute-start | bytes 884744 | tf_op jit(solution)/shard_map/ppermute | solution.py:507
  36.0 7.4 %collective-permute-start.8 = (s16[144,512]{1,0:T(8,128)(2,1)S(1)}, s16[144,512]{1,0:T(8,128)(2,1)S(1)}, u32[]{:S(2)}, u32[]{:S(2)}) collective-permute-start(s16[144,512]{1,0:T(8,128)(2,1)S(1)} %get-tuple-element.48.refs_8_), channel_id=1, source_target_pairs={{0,16},{8,24},{16,0},{24,8},{1,17},{9,25},{17,1},{25,9},{2,18},{10... | collective-permute-start | bytes 442376 | tf_op jit(solution)/shard_map/ppermute | solution.py:510
  38.5 6.0 %collective-permute-start.10 = (s16[144,512]{1,0:T(8,128)(2,1)S(1)}, s16[144,512]{1,0:T(8,128)(2,1)S(1)}, u32[]{:S(2)}, u32[]{:S(2)}) collective-permute-start(s16[144,512]{1,0:T(8,128)(2,1)S(1)} %get-tuple-element.52.refs_9_), channel_id=1, source_target_pairs={{0,8},{8,0},{16,24},{24,16},{1,9},{9,1},{17,25},{25,17},{2,10},{10... | collective-permute-start | bytes 442376 | tf_op jit(solution)/shard_map/ppermute | solution.py:510
  42.6 21.1 %collective-permute-start.16 = (s16[528,512]{1,0:T(8,128)(2,1)S(1)}, s16[528,512]{1,0:T(8,128)(2,1)S(1)}, u32[]{:S(2)}, u32[]{:S(2)}) collective-permute-start(s16[528,512]{1,0:T(8,128)(2,1)S(1)} %get-tuple-element.60), channel_id=1, source_target_pairs={{0,8},{8,0},{16,24},{24,16},{1,9},{9,1},{17,25},{25,17},{2,10},{10... | collective-permute-start | bytes 1622024 | tf_op jit(solution)/shard_map/ppermute | solution.py:510
  47.2 18.7 %collective-permute-start.21 = (s16[528,512]{1,0:T(8,128)(2,1)S(1)}, s16[528,512]{1,0:T(8,128)(2,1)S(1)}, u32[]{:S(2)}, u32[]{:S(2)}) collective-permute-start(s16[528,512]{1,0:T(8,128)(2,1)S(1)} %get-tuple-element.71), channel_id=1, source_target_pairs={{0,16},{8,24},{16,0},{24,8},{1,17},{9,25},{17,1},{25,9},{2,18},{10... | collective-permute-start | bytes 1622024 | tf_op jit(solution)/shard_map/ppermute | solution.py:510
  49.9 1.2 %collective-permute-start.17 = (f32[3,8,128]{2,1,0:T(8,128)S(1)}, f32[3,8,128]{2,1,0:T(8,128)S(1)}, u32[]{:S(2)}, u32[]{:S(2)}) collective-permute-start(f32[3,8,128]{2,1,0:T(8,128)S(1)} %get-tuple-element.63), channel_id=1, source_target_pairs={{0,1},{1,0},{2,3},{3,2},{4,5},{5,4},{6,7},{7,6},{8,9},{9,8},{10,11... | collective-permute-start | bytes 36872 | tf_op jit(solution)/shard_map/ppermute | solution.py:507
  51.1 8.9 %collective-permute-start.18 = (f32[2,8,128]{2,1,0:T(8,128)S(1)}, f32[2,8,128]{2,1,0:T(8,128)S(1)}, u32[]{:S(2)}, u32[]{:S(2)}) collective-permute-start(f32[2,8,128]{2,1,0:T(8,128)S(1)} %get-tuple-element.65), channel_id=1, source_target_pairs={{0,4},{1,5},{2,6},{3,7},{4,0},{5,1},{6,2},{7,3},{8,12},{9,13},{10,... | collective-permute-start | bytes 24584 | tf_op jit(solution)/shard_map/ppermute | solution.py:504
  60.1 3.6 %collective-permute-start.19 = (f32[8,128]{1,0:T(8,128)S(1)}, f32[8,128]{1,0:T(8,128)S(1)}, u32[]{:S(2)}, u32[]{:S(2)}) collective-permute-start(f32[8,128]{1,0:T(8,128)S(1)} %get-tuple-element.67), channel_id=1, source_target_pairs={{0,2},{1,3},{2,0},{3,1},{4,6},{5,7},{6,4},{7,5},{8,10},{9,11},{10,... | collective-permute-start | bytes 12296 | tf_op jit(solution)/shard_map/ppermute | solution.py:504
  64.4 9.4 %collective-permute-start.20 = (s16[272,512]{1,0:T(8,128)(2,1)S(1)}, s16[272,512]{1,0:T(8,128)(2,1)S(1)}, u32[]{:S(2)}, u32[]{:S(2)}) collective-permute-start(s16[272,512]{1,0:T(8,128)(2,1)S(1)} %get-tuple-element.68), channel_id=1, source_target_pairs={{0,16},{8,24},{16,0},{24,8},{1,17},{9,25},{17,1},{25,9},{2,18},{10... | collective-permute-start | bytes 835592 | tf_op jit(solution)/shard_map/ppermute | solution.py:510
  66.5 7.2 %collective-permute-start.22 = (s16[272,512]{1,0:T(8,128)(2,1)S(1)}, s16[272,512]{1,0:T(8,128)(2,1)S(1)}, u32[]{:S(2)}, u32[]{:S(2)}) collective-permute-start(s16[272,512]{1,0:T(8,128)(2,1)S(1)} %get-tuple-element.73), channel_id=1, source_target_pairs={{0,8},{8,0},{16,24},{24,16},{1,9},{9,1},{17,25},{25,17},{2,10},{10... | collective-permute-start | bytes 835592 | tf_op jit(solution)/shard_map/ppermute | solution.py:510
  68.2 5.0 %collective-permute-start.25 = (f32[8,128]{1,0:T(8,128)S(1)}, f32[8,128]{1,0:T(8,128)S(1)}, u32[]{:S(2)}, u32[]{:S(2)}) collective-permute-start(f32[8,128]{1,0:T(8,128)S(1)} %add_kernel.1.refs_0_), channel_id=1, source_target_pairs={{0,24},{8,16},{16,8},{24,0},{1,25},{9,17},{17,9},{25,1},{2,26},{10... | collective-permute-start | bytes 12296 | tf_op jit(solution)/shard_map/ppermute | solution.py:510
  68.6 4.6 %collective-permute-start.24 = (f32[8,128]{1,0:T(8,128)S(1)}, f32[8,128]{1,0:T(8,128)S(1)}, u32[]{:S(2)}, u32[]{:S(2)}) collective-permute-start(f32[8,128]{1,0:T(8,128)S(1)} %add_kernel.1.refs_0_), channel_id=1, source_target_pairs={{0,16},{8,24},{16,0},{24,8},{1,17},{9,25},{17,1},{25,9},{2,18},{10... | collective-permute-start | bytes 12296 | tf_op jit(solution)/shard_map/ppermute | solution.py:510
  70.1 3.6 %collective-permute-start.23 = (f32[8,128]{1,0:T(8,128)S(1)}, f32[8,128]{1,0:T(8,128)S(1)}, u32[]{:S(2)}, u32[]{:S(2)}) collective-permute-start(f32[8,128]{1,0:T(8,128)S(1)} %add_kernel.1.refs_0_), channel_id=1, source_target_pairs={{0,8},{8,0},{16,24},{24,16},{1,9},{9,1},{17,25},{25,17},{2,10},{10... | collective-permute-start | bytes 12296 | tf_op jit(solution)/shard_map/ppermute | solution.py:510

commit v4 on v3

--- a/solution.py
+++ b/solution.py
@@ -436,15 +436,25 @@
 
 
 def finish_kernel(most, first, got0, rest0, gates0, got1, rest1, gates1, *refs):
-    totals, (out, gate_grad) = refs[:-2], refs[-2:]
-    gate_grad[...] = sum((total[...] for total in totals[1:]), totals[0][...])
+    totals, (out, gate_grad, grads, sem) = refs[:-4], refs[-4:]
     z = place()[0]
     spans = [pl.ds(pl.multiple_of(chip_of(z, s) * (2 * most), 2 * most), 2 * most) for s in range(3)]
+    copies = [
+        pltpu.make_async_copy(first.at[local], out.at[local, spans[0]], sem.at[local])
+        for local in range(2)
+    ]
+    for copy in copies:
+        copy.start()
     for local, (got, rest, gates) in enumerate(((got0, rest0, gates0), (got1, rest1, gates1))):
-        out[local, spans[0], :] = first[local]
-        grad = gates[:, :1] * (rest[...] + decode(got, 0, 1))
-        out[local, spans[1], :] = grad[: 2 * most]
-        out[local, spans[2], :] = grad[2 * most :]
+        grads[local] = gates[:, :1] * (rest[...] + decode(got, 0, 1))
+        for step in (1, 2):
+            part = grads.at[local, 2 * most * (step - 1) : 2 * most * step]
+            copy = pltpu.make_async_copy(part, out.at[local, spans[step]], sem.at[2 * step + local])
+            copy.start()
+            copies.append(copy)
+    gate_grad[...] = sum((total[...] for total in totals[1:]), totals[0][...])
+    for copy in copies:
+        copy.wait()
 
 
 def finish(most, first, sums, totals):
@@ -452,29 +462,24 @@
     return pl.pallas_call(
         functools.partial(finish_kernel, most),
         in_specs=[VMEM] * (7 + len(totals)),
-        out_specs=[VMEM, VMEM],
-        out_shape=[like((experts, 3 * rows, width)), like(totals[0].shape)],
+        out_specs=[ANY, VMEM],
+        out_shape=[pltpu.HBM((experts, 3 * rows, width), jnp.float32), like(totals[0].shape)],
+        scratch_shapes=[
+            pltpu.VMEM((experts, 2 * rows, width), jnp.float32),
+            pltpu.SemaphoreType.DMA((6,)),
+        ],
         compiler_params=pltpu.CompilerParams(vmem_limit_bytes=16 * MIB),
         cost_estimate=cost([*sums, first, first]),
         name="finish",
     )(first, *sums, *totals)
 
 
-def chips_kernel(mine, got, stay, away):
+def chips_kernel(mine, got, own, *shifted):
     z = place()[0]
-    low, mid, high = (mine[i] + got[i] for i in range(3))
-    none = jnp.zeros(low.shape, jnp.float32)
-    stay[0] = jnp.where(z < 2, low, high)
-    stay[1] = jnp.where(z < 2, mid, none)
-    away[0] = jnp.where(z < 2, high, low)
-    away[1] = jnp.where(z < 2, none, mid)
-
-
-def chip_kernel(kept, got, stay, away):
-    odd = lax.rem(place()[0], 2) == 1
-    even_part, odd_part = (kept[i] + got[i] for i in range(2))
-    stay[...] = jnp.where(odd, odd_part, even_part)
-    away[...] = jnp.where(odd, even_part, odd_part)
+    for shift, out in enumerate((own, *shifted)):
+        chip = lax.rem(z + shift, len(ORDER))
+        at = jnp.minimum(chip, mine.shape[0] - 1)
+        out[...] = jnp.where(chip == at, mine[at] + got[at], 0.0)
 
 
 def add_kernel(*refs):
@@ -484,16 +489,17 @@
     refs[-1][...] = total
 
 
-def small(kernel, outs, *args):
-    return pl.pallas_call(
-        kernel,
-        in_specs=[VMEM] * len(args),
+def small(kernel, outs, *args, after=()):
+    used = len(args)
+    return pl.pallas_call(
+        lambda *refs: kernel(*refs[:used], *refs[used + len(after) :]),
+        in_specs=[VMEM] * used + [ANY] * len(after),
         out_specs=[VMEM] * len(outs),
         out_shape=outs,
         compiler_params=pltpu.CompilerParams(vmem_limit_bytes=2 * MIB),
         cost_estimate=cost(args),
         name=kernel.__name__,
-    )(*args)
+    )(*args, *after)
 
 
 def blockwise(most, grad_out, routes, slots, gates, capacity, hidden, down_weight):
@@ -552,18 +558,17 @@
     first_grad, mine, theirs = first_finish(most, top, capacity, first_hidden, info, sums, before)
 
     one = like((top, tokens))
-    two = like((2, top, tokens))
-    stay, away = small(chips_kernel, [two, two], mine, across(theirs))
-    stay, away = small(
-        chip_kernel, [one, one], stay, along(away, [(z, z ^ 2) for z in range(peers // 2)])
-    )
-    (total,) = small(add_kernel, [one], stay, along(away, [(z, z ^ 1) for z in range(peers // 2)]))
+    chips = small(chips_kernel, [one] * 4, mine, across(theirs))
+    chips = [chips[0]] + [
+        along(part, [(z, (z + shift) % 4) for z in range(4) if (z + shift) % 4 < 3])
+        for shift, part in enumerate(chips[1:], 1)
+    ]
+    (got0, keep0, gate0), (got1, keep1, gate1) = halves
+    send0, rest0 = middle(got0, keep0, chips[1:])
+    (total,) = small(add_kernel, [one], *chips, after=(send0,))
+    send1, rest1 = middle(got1, keep1, (total,))
+    sums = [over(send0, 2), rest0, gate0, over(send1, 1), rest1, gate1]
     whole = [total] + [over(total, flip) for flip in range(1, ranks)]
-
-    sums = []
-    for local, (got, keep, gate) in enumerate(halves):
-        send, rest = middle(got, keep, (total,))
-        sums += [over(send, 2 - local), rest, gate]
     hidden_grad, gate_grad = finish(most, first_grad, sums, whole)
     return hidden_grad, gate_grad.T
 

time: 75.5 us -> 79.6 us (1.054)
  starting transfers between devices: 37.5 us -> 40 us
  waiting for transfers between devices: 16.8 us -> 17.9 us
    ppermute x7 -> x8, starting transfers between devices: 18.2 us -> 20.6 us  [along(): lax.ppermute(rows, 'expert', [(2 * a + c, 2 * b + c) for a, b in pairs fo...]
    ppermute x7 -> x8, waiting for transfers between devices: 9.77 us -> 10.8 us  [along(): lax.ppermute(rows, 'expert', [(2 * a + c, 2 * b + c) for a, b in pairs fo...]
  transfers between devices with their start and end apart: 26 -> 27, of which waited for: 13 -> 12; matrix products, arithmetic and copies ran while one was open for 0% -> 0% of each run, Pallas kernels for 23% -> 22%
where the time goes in v4:
time: 79.6 us; the launch traced here: 79.3 us
  starting transfers between devices  40 us (50%)
  Pallas kernels  20.5 us (26%)
  waiting for transfers between devices  17.9 us (22%)
  between operations  0.92 us (1%)
    ppermute x8, starting transfers between devices, along(): lax.ppermute(rows, 'expert', [(2 * a + c, 2 * b + c) for a, b in pairs fo...  20.6 us
    ppermute x15, starting transfers between devices, over(): return lax.ppermute(rows, 'dp', [(i, i ^ flip) for i in range(ranks)])  19 us
    ppermute x8, waiting for transfers between devices, along(): lax.ppermute(rows, 'expert', [(2 * a + c, 2 * b + c) for a, b in pairs fo...  10.8 us
    pallas_call x4, Pallas kernels, partial_share(): pl.pallas_call(functools.partial(share_kernel, local, most, top, group, e...  10.3 us
    ppermute x15, waiting for transfers between devices, over(): return lax.ppermute(rows, 'dp', [(i, i ^ flip) for i in range(ranks)])  6.01 us
    pallas_call x1, Pallas kernels, load(): pl.pallas_call(load_kernel, in_specs=[ANY, ANY], out_specs=VMEM, out_shap...  3.39 us
    pallas_call x4, Pallas kernels, middle(): pl.pallas_call(middle_kernel, in_specs=[VMEM, VMEM] + [ANY] * len(after),...  2.17 us
    pallas_call x1, Pallas kernels, finish(): pl.pallas_call(functools.partial(finish_kernel, most), in_specs=[VMEM] *...  1.92 us
  transfers between devices with their start and end apart: 27, of which 12 were waited for; matrix products, arithmetic and copies ran while one was open for 0% of the time, Pallas kernels for 22%

profile of v4, /device:TPU:0, one launch (start us, length us, event | category | flops | bytes accessed | tf_op | source)
XLA Modules:
  0.0 79.3 jit_solution(8701639939823943418)
XLA Ops:
  0.6 1.4 %prepare.1 = (bf16[144,1024]{1,0:T(8,128)(2,1)S(1)}, bf16[2,128,512]{2,1,0:T(8,128)(2,1)S(1)}, bf16[2,256,512]{2,1,0:T(8,128)(2,1)S(1)}) custom-call(bf16[128,1024]{1,0:T(8,128)(2,1)} %rows.1, s32[8,128]{1,0:T(8,128)} %bitcast.4, s32[8,128]{1,0:T(8,128)} %bitcast.5, bf16[8,128]{1,0:T(8,128)(2,1)} %bitcast.6, bf16[2,384,512]{2,1,0:T(8,128)(2,1)} %hidden.1), custom_call_target="tpu_custom_call" | custom-call | bytes 1310720 | tf_op jit(solution)/shard_map/prepare/pallas_call | solution.py:177
  2.0 4.9 %collective-permute-start = (bf16[144,1024]{1,0:T(8,128)(2,1)S(1)}, bf16[144,1024]{1,0:T(8,128)(2,1)S(1)}, u32[]{:S(2)}, u32[]{:S(2)}) collective-permute-start(bf16[144,1024]{1,0:T(8,128)(2,1)S(1)} %get-tuple-element.41.after.refs_0_.block), channel_id=1, source_target_pairs={{0,2},{1,3},{2,4},{3,5},{4,6},{5,7},{8,10},{9,11},{10,12},{11,13},... | collective-permute-start | bytes 884744 | tf_op jit(solution)/shard_map/ppermute | solution.py:510
  7.0 1.6 %collective-permute-start.4 = (bf16[2,256,512]{2,1,0:T(8,128)(2,1)S(1)}, bf16[2,256,512]{2,1,0:T(8,128)(2,1)S(1)}, u32[]{:S(2)}, u32[]{:S(2)}) collective-permute-start(bf16[2,256,512]{2,1,0:T(8,128)(2,1)S(1)} %get-tuple-element.42.refs_4_), channel_id=1, source_target_pairs={{0,16},{8,24},{16,0},{24,8},{1,17},{9,25},{17,1},{25,9},{2,18},{10... | collective-permute-start | bytes 1572872 | tf_op jit(solution)/shard_map/ppermute | solution.py:516
  8.5 1.5 %collective-permute-start.3 = (bf16[2,256,512]{2,1,0:T(8,128)(2,1)S(1)}, bf16[2,256,512]{2,1,0:T(8,128)(2,1)S(1)}, u32[]{:S(2)}, u32[]{:S(2)}) collective-permute-start(bf16[2,256,512]{2,1,0:T(8,128)(2,1)S(1)} %get-tuple-element.42.refs_4_), channel_id=1, source_target_pairs={{0,8},{8,0},{16,24},{24,16},{1,9},{9,1},{17,25},{25,17},{2,10},{10... | collective-permute-start | bytes 1572872 | tf_op jit(solution)/shard_map/ppermute | solution.py:516
  10.0 1.3 %collective-permute-start.1 = (bf16[144,1024]{1,0:T(8,128)(2,1)S(1)}, bf16[144,1024]{1,0:T(8,128)(2,1)S(1)}, u32[]{:S(2)}, u32[]{:S(2)}) collective-permute-start(bf16[144,1024]{1,0:T(8,128)(2,1)S(1)} %get-tuple-element.41.after.refs_0_.block), channel_id=1, source_target_pairs={{4,2},{5,3},{2,0},{3,1},{12,10},{13,11},{10,8},{11,9},{20,18},{21,... | collective-permute-start | bytes 884744 | tf_op jit(solution)/shard_map/ppermute | solution.py:510
  11.3 1.9 %collective-permute-done.refs_1_.refs_0_ = bf16[144,1024]{1,0:T(8,128)(2,1)S(1)} collective-permute-done((bf16[144,1024]{1,0:T(8,128)(2,1)S(1)}, bf16[144,1024]{1,0:T(8,128)(2,1)S(1)}, u32[]{:S(2)}, u32[]{:S(2)}) %collective-permute-start) | collective-permute-done | bytes 294944 | tf_op jit(solution)/shard_map/ppermute | solution.py:510
  13.9 3.4 %load_weight.1.refs_2_.weight = bf16[2,2048,1024]{2,1,0:T(8,128)(2,1)S(1)} custom-call(bf16[144,1024]{1,0:T(8,128)(2,1)S(1)} %get-tuple-element.41.after.refs_0_.block, bf16[2,2048,1024]{2,1,0:T(8,128)(2,1)} %weight.1), custom_call_target="tpu_custom_call" | custom-call | bytes 16777216 | tf_op jit(solution)/shard_map/load_weight/pallas_call | solution.py:205
  17.3 2.5 %collective-permute-done.1.refs_3_.refs_2_.refs_1_ = bf16[144,1024]{1,0:T(8,128)(2,1)S(1)} collective-permute-done((bf16[144,1024]{1,0:T(8,128)(2,1)S(1)}, bf16[144,1024]{1,0:T(8,128)(2,1)S(1)}, u32[]{:S(2)}, u32[]{:S(2)}) %collective-permute-start.1) | collective-permute-done | bytes 294944 | tf_op jit(solution)/shard_map/ppermute | solution.py:510
  20.4 1.2 %collective-permute-done.3.over_x.refs_5_ = bf16[2,256,512]{2,1,0:T(8,128)(2,1)S(1)} collective-permute-done((bf16[2,256,512]{2,1,0:T(8,128)(2,1)S(1)}, bf16[2,256,512]{2,1,0:T(8,128)(2,1)S(1)}, u32[]{:S(2)}, u32[]{:S(2)}) %collective-permute-start.3) | collective-permute-done | bytes 524320 | tf_op jit(solution)/shard_map/ppermute | solution.py:516
  22.3 1.5 %collective-permute-start.6 = (bf16[256,512]{1,0:T(8,128)(2,1)S(1)}, bf16[256,512]{1,0:T(8,128)(2,1)S(1)}, u32[]{:S(2)}, u32[]{:S(2)}) collective-permute-start(bf16[256,512]{1,0:T(8,128)(2,1)S(1)} %get-tuple-element.44), channel_id=1, source_target_pairs={{0,8},{8,0},{16,24},{24,16},{1,9},{9,1},{17,25},{25,17},{2,10},{10... | collective-permute-start | bytes 786440 | tf_op jit(solution)/shard_map/ppermute | solution.py:516
  23.8 1.3 %collective-permute-start.13 = (bf16[144,1024]{1,0:T(8,128)(2,1)S(1)}, bf16[144,1024]{1,0:T(8,128)(2,1)S(1)}, u32[]{:S(2)}, u32[]{:S(2)}) collective-permute-start(bf16[144,1024]{1,0:T(8,128)(2,1)S(1)} %get-tuple-element.54), channel_id=1, source_target_pairs={{4,0},{5,1},{12,8},{13,9},{20,16},{21,17},{28,24},{29,25}} | collective-permute-start | bytes 884744 | tf_op jit(solution)/shard_map/ppermute | solution.py:510
  25.8 2.7 %share_0.2 = (s16[272,512]{1,0:T(8,128)(2,1)S(1)}, f32[2,128,512]{2,1,0:T(8,128)S(1)}, f32[2,16,384]{2,1,0:T(8,128)}) custom-call(s32[2]{0:T(128)S(1)} %copy-done, bf16[2,2048,1024]{2,1,0:T(8,128)(2,1)S(1)} %load_weight.1.refs_2_.weight, bf16[144,1024]{1,0:T(8,128)(2,1)S(1)} %pick.3.refs_0_, bf16[144,1024]{1,0:T(8,128)(2,1)S(1)} %collective-permute-done.2.refs_1_), custom_call_target="tpu_custom_call" | custom-call | flops 536870912 | bytes 8978432 | tf_op jit(solution)/shard_map/share_0/pallas_call | solution.py:370
  29.2 2.2 %share_1.2 = (s16[272,512]{1,0:T(8,128)(2,1)S(1)}, f32[2,128,512]{2,1,0:T(8,128)S(1)}, f32[2,16,384]{2,1,0:T(8,128)S(1)}) custom-call(s32[2]{0:T(128)S(1)} %copy-done, bf16[2,2048,1024]{2,1,0:T(8,128)(2,1)S(1)} %load_weight.1.refs_2_.weight, bf16[144,1024]{1,0:T(8,128)(2,1)S(1)} %pick.3.refs_0_, bf16[144,1024]{1,0:T(8,128)(2,1)S(1)} %collective-permute-done.2.refs_1_, ...), custom_call_target="tpu_custom_call" | custom-call | flops 536870912 | bytes 8978432 | tf_op jit(solution)/shard_map/share_1/pallas_call | solution.py:370
  31.4 1.7 %collective-permute-start.9 = (s16[272,512]{1,0:T(8,128)(2,1)S(1)}, s16[272,512]{1,0:T(8,128)(2,1)S(1)}, u32[]{:S(2)}, u32[]{:S(2)}) collective-permute-start(s16[272,512]{1,0:T(8,128)(2,1)S(1)} %get-tuple-element.50.refs_4_), channel_id=1, source_target_pairs={{0,16},{8,24},{16,0},{24,8},{1,17},{9,25},{17,1},{25,9},{2,18},{10... | collective-permute-start | bytes 835592 | tf_op jit(solution)/shard_map/ppermute | solution.py:516
  33.2 2.1 %collective-permute-done.13.refs_0_ = bf16[144,1024]{1,0:T(8,128)(2,1)S(1)} collective-permute-done((bf16[144,1024]{1,0:T(8,128)(2,1)S(1)}, bf16[144,1024]{1,0:T(8,128)(2,1)S(1)}, u32[]{:S(2)}, u32[]{:S(2)}) %collective-permute-start.13) | collective-permute-done | bytes 294944 | tf_op jit(solution)/shard_map/ppermute | solution.py:510
  38.5 1.5 %collective-permute-start.10 = (s16[144,512]{1,0:T(8,128)(2,1)S(1)}, s16[144,512]{1,0:T(8,128)(2,1)S(1)}, u32[]{:S(2)}, u32[]{:S(2)}) collective-permute-start(s16[144,512]{1,0:T(8,128)(2,1)S(1)} %get-tuple-element.52.refs_9_), channel_id=1, source_target_pairs={{0,8},{8,0},{16,24},{24,16},{1,9},{9,1},{17,25},{25,17},{2,10},{10... | collective-permute-start | bytes 442376 | tf_op jit(solution)/shard_map/ppermute | solution.py:516
  39.9 2.7 %share_0.3 = (s16[528,512]{1,0:T(8,128)(2,1)S(1)}, f32[2,256,512]{2,1,0:T(8,128)S(1)}, f32[256,128]{1,0:T(8,128)S(1)}, f32[3,8,128]{2,1,0:T(8,128)S(1)}, f32[3,8,128]{2,1,0:T(8,128)S(1)}) custom-call(s32[2]{0:T(128)S(1)} %copy-done, bf16[2,2048,1024]{2,1,0:T(8,128)(2,1)S(1)} %load_weight.1.refs_2_.weight, bf16[144,1024]{1,0:T(8,128)(2,1)S(1)} %pick.4.refs_0_, ...), custom_call_target="tpu_custom_call" | custom-call | flops 1073741824 | bytes 9568256 | tf_op jit(solution)/shard_map/share_0/pallas_call | solution.py:370
  43.3 1.1 %collective-permute-done.10.refs_11_.got1 = s16[144,512]{1,0:T(8,128)(2,1)S(1)} collective-permute-done((s16[144,512]{1,0:T(8,128)(2,1)S(1)}, s16[144,512]{1,0:T(8,128)(2,1)S(1)}, u32[]{:S(2)}, u32[]{:S(2)}) %collective-permute-start.10) | collective-permute-done | bytes 147488 | tf_op jit(solution)/shard_map/ppermute | solution.py:516
  44.5 2.7 %share_1.3 = (s16[528,512]{1,0:T(8,128)(2,1)S(1)}, f32[2,256,512]{2,1,0:T(8,128)S(1)}, f32[256,128]{1,0:T(8,128)S(1)}, f32[3,8,128]{2,1,0:T(8,128)S(1)}, f32[3,8,128]{2,1,0:T(8,128)S(1)}) custom-call(s32[2]{0:T(128)S(1)} %copy-done, bf16[2,2048,1024]{2,1,0:T(8,128)(2,1)S(1)} %load_weight.1.refs_2_.weight, bf16[144,1024]{1,0:T(8,128)(2,1)S(1)} %pick.4.refs_0_, ...), custom_call_target="tpu_custom_call" | custom-call | flops 1073741824 | bytes 9568256 | tf_op jit(solution)/shard_map/share_1/pallas_call | solution.py:370
  47.2 1.8 %collective-permute-start.22 = (s16[528,512]{1,0:T(8,128)(2,1)S(1)}, s16[528,512]{1,0:T(8,128)(2,1)S(1)}, u32[]{:S(2)}, u32[]{:S(2)}) collective-permute-start(s16[528,512]{1,0:T(8,128)(2,1)S(1)} %get-tuple-element.70), channel_id=1, source_target_pairs={{0,16},{8,24},{16,0},{24,8},{1,17},{9,25},{17,1},{25,9},{2,18},{10... | collective-permute-start | bytes 1622024 | tf_op jit(solution)/shard_map/ppermute | solution.py:516
  50.0 1.2 %collective-permute-done.17.refs_1_ = f32[3,8,128]{2,1,0:T(8,128)S(1)} collective-permute-done((f32[3,8,128]{2,1,0:T(8,128)S(1)}, f32[3,8,128]{2,1,0:T(8,128)S(1)}, u32[]{:S(2)}, u32[]{:S(2)}) %collective-permute-start.17) | collective-permute-done | bytes 12320 | tf_op jit(solution)/shard_map/ppermute | solution.py:513
  51.2 8.3 %collective-permute-start.18 = (f32[8,128]{1,0:T(8,128)S(1)}, f32[8,128]{1,0:T(8,128)S(1)}, u32[]{:S(2)}, u32[]{:S(2)}) collective-permute-start(f32[8,128]{1,0:T(8,128)S(1)} %get-tuple-element.64), channel_id=1, source_target_pairs={{0,2},{1,3},{2,4},{3,5},{6,0},{7,1},{8,10},{9,11},{10,12},{11,13},... | collective-permute-start | bytes 12296 | tf_op jit(solution)/shard_map/ppermute | solution.py:510
  59.5 2.2 %collective-permute-start.19 = (f32[8,128]{1,0:T(8,128)S(1)}, f32[8,128]{1,0:T(8,128)S(1)}, u32[]{:S(2)}, u32[]{:S(2)}) collective-permute-start(f32[8,128]{1,0:T(8,128)S(1)} %get-tuple-element.65), channel_id=1, source_target_pairs={{0,4},{1,5},{4,0},{5,1},{6,2},{7,3},{8,12},{9,13},{12,8},{13,9},{1... | collective-permute-start | bytes 12296 | tf_op jit(solution)/shard_map/ppermute | solution.py:510
  61.7 1.3 %collective-permute-start.20 = (f32[8,128]{1,0:T(8,128)S(1)}, f32[8,128]{1,0:T(8,128)S(1)}, u32[]{:S(2)}, u32[]{:S(2)}) collective-permute-start(f32[8,128]{1,0:T(8,128)S(1)} %get-tuple-element.66), channel_id=1, source_target_pairs={{2,0},{3,1},{4,2},{5,3},{6,4},{7,5},{10,8},{11,9},{12,10},{13,11},... | collective-permute-start | bytes 12296 | tf_op jit(solution)/shard_map/ppermute | solution.py:510
  63.0 2.9 %collective-permute-done.19.refs_1_.refs_2_ = f32[8,128]{1,0:T(8,128)S(1)} collective-permute-done((f32[8,128]{1,0:T(8,128)S(1)}, f32[8,128]{1,0:T(8,128)S(1)}, u32[]{:S(2)}, u32[]{:S(2)}) %collective-permute-start.19) | collective-permute-done | bytes 4128 | tf_op jit(solution)/shard_map/ppermute | solution.py:510
  65.9 1.3 %collective-permute-done.20.refs_2_.refs_3_ = f32[8,128]{1,0:T(8,128)S(1)} collective-permute-done((f32[8,128]{1,0:T(8,128)S(1)}, f32[8,128]{1,0:T(8,128)S(1)}, u32[]{:S(2)}, u32[]{:S(2)}) %collective-permute-start.20) | collective-permute-done | bytes 4128 | tf_op jit(solution)/shard_map/ppermute | solution.py:510
  67.8 1.5 %collective-permute-start.21 = (s16[272,512]{1,0:T(8,128)(2,1)S(1)}, s16[272,512]{1,0:T(8,128)(2,1)S(1)}, u32[]{:S(2)}, u32[]{:S(2)}) collective-permute-start(s16[272,512]{1,0:T(8,128)(2,1)S(1)} %get-tuple-element.67.refs_4_), channel_id=1, source_target_pairs={{0,16},{8,24},{16,0},{24,8},{1,17},{9,25},{17,1},{25,9},{2,18},{10... | collective-permute-start | bytes 835592 | tf_op jit(solution)/shard_map/ppermute | solution.py:516
  70.0 1.6 %collective-permute-start.23 = (s16[272,512]{1,0:T(8,128)(2,1)S(1)}, s16[272,512]{1,0:T(8,128)(2,1)S(1)}, u32[]{:S(2)}, u32[]{:S(2)}) collective-permute-start(s16[272,512]{1,0:T(8,128)(2,1)S(1)} %get-tuple-element.73), channel_id=1, source_target_pairs={{0,8},{8,0},{16,24},{24,16},{1,9},{9,1},{17,25},{25,17},{2,10},{10... | collective-permute-start | bytes 835592 | tf_op jit(solution)/shard_map/ppermute | solution.py:516
  72.1 1.5 %collective-permute-start.25 = (f32[8,128]{1,0:T(8,128)S(1)}, f32[8,128]{1,0:T(8,128)S(1)}, u32[]{:S(2)}, u32[]{:S(2)}) collective-permute-start(f32[8,128]{1,0:T(8,128)S(1)} %add_kernel.1.refs_0_), channel_id=1, source_target_pairs={{0,16},{8,24},{16,0},{24,8},{1,17},{9,25},{17,1},{25,9},{2,18},{10... | collective-permute-start | bytes 12296 | tf_op jit(solution)/shard_map/ppermute | solution.py:516
  73.6 1.6 %collective-permute-start.24 = (f32[8,128]{1,0:T(8,128)S(1)}, f32[8,128]{1,0:T(8,128)S(1)}, u32[]{:S(2)}, u32[]{:S(2)}) collective-permute-start(f32[8,128]{1,0:T(8,128)S(1)} %add_kernel.1.refs_0_), channel_id=1, source_target_pairs={{0,8},{8,0},{16,24},{24,16},{1,9},{9,1},{17,25},{25,17},{2,10},{10... | collective-permute-start | bytes 12296 | tf_op jit(solution)/shard_map/ppermute | solution.py:516
  75.2 2.2 %collective-permute-done.26.refs_3_ = f32[8,128]{1,0:T(8,128)S(1)} collective-permute-done((f32[8,128]{1,0:T(8,128)S(1)}, f32[8,128]{1,0:T(8,128)S(1)}, u32[]{:S(2)}, u32[]{:S(2)}) %collective-permute-start.26) | collective-permute-done | bytes 4128 | tf_op jit(solution)/shard_map/ppermute | solution.py:516
  77.4 1.9 %finish.1 = (f32[2,384,512]{2,1,0:T(8,128)}, f32[8,128]{1,0:T(8,128)}) custom-call(f32[2,128,512]{2,1,0:T(8,128)S(1)} %get-tuple-element.59.first, s16[272,512]{1,0:T(8,128)(2,1)S(1)} %collective-permute-done.21.got0, f32[256,512]{1,0:T(8,128)S(1)} %get-tuple-element.68.rest0, f32[256,128]{1,0:T(8,128)S(1)} %get-tuple-element.69.gates0, ...), custom_call_target="tpu_custom_call" | custom-call | bytes 2916352 | tf_op jit(solution)/shard_map/finish/pallas_call | solution.py:462
  (42 shorter events, 10.0 us)
Async XLA Ops:
  2.0 11.2 %collective-permute-start = (bf16[144,1024]{1,0:T(8,128)(2,1)S(1)}, bf16[144,1024]{1,0:T(8,128)(2,1)S(1)}, u32[]{:S(2)}, u32[]{:S(2)}) collective-permute-start(bf16[144,1024]{1,0:T(8,128)(2,1)S(1)} %get-tuple-element.41.after.refs_0_.block), channel_id=1, source_target_pairs={{0,2},{1,3},{2,4},{3,5},{4,6},{5,7},{8,10},{9,11},{10,12},{11,13},... | collective-permute-start | bytes 884744 | tf_op jit(solution)/shard_map/ppermute | solution.py:510
  7.0 13.4 %collective-permute-start.4 = (bf16[2,256,512]{2,1,0:T(8,128)(2,1)S(1)}, bf16[2,256,512]{2,1,0:T(8,128)(2,1)S(1)}, u32[]{:S(2)}, u32[]{:S(2)}) collective-permute-start(bf16[2,256,512]{2,1,0:T(8,128)(2,1)S(1)} %get-tuple-element.42.refs_4_), channel_id=1, source_target_pairs={{0,16},{8,24},{16,0},{24,8},{1,17},{9,25},{17,1},{25,9},{2,18},{10... | collective-permute-start | bytes 1572872 | tf_op jit(solution)/shard_map/ppermute | solution.py:516
  8.5 13.1 %collective-permute-start.3 = (bf16[2,256,512]{2,1,0:T(8,128)(2,1)S(1)}, bf16[2,256,512]{2,1,0:T(8,128)(2,1)S(1)}, u32[]{:S(2)}, u32[]{:S(2)}) collective-permute-start(bf16[2,256,512]{2,1,0:T(8,128)(2,1)S(1)} %get-tuple-element.42.refs_4_), channel_id=1, source_target_pairs={{0,8},{8,0},{16,24},{24,16},{1,9},{9,1},{17,25},{25,17},{2,10},{10... | collective-permute-start | bytes 1572872 | tf_op jit(solution)/shard_map/ppermute | solution.py:516
  10.0 9.8 %collective-permute-start.1 = (bf16[144,1024]{1,0:T(8,128)(2,1)S(1)}, bf16[144,1024]{1,0:T(8,128)(2,1)S(1)}, u32[]{:S(2)}, u32[]{:S(2)}) collective-permute-start(bf16[144,1024]{1,0:T(8,128)(2,1)S(1)} %get-tuple-element.41.after.refs_0_.block), channel_id=1, source_target_pairs={{4,2},{5,3},{2,0},{3,1},{12,10},{13,11},{10,8},{11,9},{20,18},{21,... | collective-permute-start | bytes 884744 | tf_op jit(solution)/shard_map/ppermute | solution.py:510
  13.2 11.9 %collective-permute-start.11 = (bf16[144,1024]{1,0:T(8,128)(2,1)S(1)}, bf16[144,1024]{1,0:T(8,128)(2,1)S(1)}, u32[]{:S(2)}, u32[]{:S(2)}) collective-permute-start(bf16[144,1024]{1,0:T(8,128)(2,1)S(1)} %collective-permute-done.refs_1_.refs_0_), channel_id=1, source_target_pairs={{2,4},{3,5},{4,6},{5,7},{10,12},{11,13},{12,14},{13,15},{18,20},{1... | collective-permute-start | bytes 884744 | tf_op jit(solution)/shard_map/ppermute | solution.py:510
  17.3 8.6 %copy-start = (s32[2]{0:T(128)S(1)}, s32[2]{0:T(128)}, u32[]{:S(2)}) copy-start(s32[2]{0:T(128)} %cap.9) | copy-start | bytes 28
  19.9 5.9 %collective-permute-start.2 = (bf16[144,1024]{1,0:T(8,128)(2,1)S(1)}, bf16[144,1024]{1,0:T(8,128)(2,1)S(1)}, u32[]{:S(2)}, u32[]{:S(2)}) collective-permute-start(bf16[144,1024]{1,0:T(8,128)(2,1)S(1)} %pick.3.refs_0_), channel_id=1, source_target_pairs={{0,1},{1,0},{2,3},{3,2},{4,5},{5,4},{6,7},{7,6},{8,9},{9,8},{10,11... | collective-permute-start | bytes 884744 | tf_op jit(solution)/shard_map/ppermute | solution.py:513
  21.8 7.3 %collective-permute-start.5 = (bf16[256,512]{1,0:T(8,128)(2,1)S(1)}, bf16[256,512]{1,0:T(8,128)(2,1)S(1)}, u32[]{:S(2)}, u32[]{:S(2)}) collective-permute-start(bf16[256,512]{1,0:T(8,128)(2,1)S(1)} %get-tuple-element.43), channel_id=1, source_target_pairs={{0,16},{8,24},{16,0},{24,8},{1,17},{9,25},{17,1},{25,9},{2,18},{10... | collective-permute-start | bytes 786440 | tf_op jit(solution)/shard_map/ppermute | solution.py:516
  22.3 6.8 %collective-permute-start.6 = (bf16[256,512]{1,0:T(8,128)(2,1)S(1)}, bf16[256,512]{1,0:T(8,128)(2,1)S(1)}, u32[]{:S(2)}, u32[]{:S(2)}) collective-permute-start(bf16[256,512]{1,0:T(8,128)(2,1)S(1)} %get-tuple-element.44), channel_id=1, source_target_pairs={{0,8},{8,0},{16,24},{24,16},{1,9},{9,1},{17,25},{25,17},{2,10},{10... | collective-permute-start | bytes 786440 | tf_op jit(solution)/shard_map/ppermute | solution.py:516
  23.8 11.5 %collective-permute-start.13 = (bf16[144,1024]{1,0:T(8,128)(2,1)S(1)}, bf16[144,1024]{1,0:T(8,128)(2,1)S(1)}, u32[]{:S(2)}, u32[]{:S(2)}) collective-permute-start(bf16[144,1024]{1,0:T(8,128)(2,1)S(1)} %get-tuple-element.54), channel_id=1, source_target_pairs={{4,0},{5,1},{12,8},{13,9},{20,16},{21,17},{28,24},{29,25}} | collective-permute-start | bytes 884744 | tf_op jit(solution)/shard_map/ppermute | solution.py:510
  25.1 10.2 %collective-permute-start.14 = (bf16[144,1024]{1,0:T(8,128)(2,1)S(1)}, bf16[144,1024]{1,0:T(8,128)(2,1)S(1)}, u32[]{:S(2)}, u32[]{:S(2)}) collective-permute-start(bf16[144,1024]{1,0:T(8,128)(2,1)S(1)} %collective-permute-done.11.refs_1_.refs_2_), channel_id=1, source_target_pairs={{4,6},{5,7},{12,14},{13,15},{20,22},{21,23},{28,30},{29,31}} | collective-permute-start | bytes 884744 | tf_op jit(solution)/shard_map/ppermute | solution.py:510
  28.5 7.0 %collective-permute-start.7 = (s16[272,512]{1,0:T(8,128)(2,1)S(1)}, s16[272,512]{1,0:T(8,128)(2,1)S(1)}, u32[]{:S(2)}, u32[]{:S(2)}) collective-permute-start(s16[272,512]{1,0:T(8,128)(2,1)S(1)} %get-tuple-element.46.refs_3_), channel_id=1, source_target_pairs={{0,8},{8,0},{16,24},{24,16},{1,9},{9,1},{17,25},{25,17},{2,10},{10... | collective-permute-start | bytes 835592 | tf_op jit(solution)/shard_map/ppermute | solution.py:516
  31.4 6.6 %collective-permute-start.9 = (s16[272,512]{1,0:T(8,128)(2,1)S(1)}, s16[272,512]{1,0:T(8,128)(2,1)S(1)}, u32[]{:S(2)}, u32[]{:S(2)}) collective-permute-start(s16[272,512]{1,0:T(8,128)(2,1)S(1)} %get-tuple-element.50.refs_4_), channel_id=1, source_target_pairs={{0,16},{8,24},{16,0},{24,8},{1,17},{9,25},{17,1},{25,9},{2,18},{10... | collective-permute-start | bytes 835592 | tf_op jit(solution)/shard_map/ppermute | solution.py:516
  33.1 6.8 %collective-permute-start.12 = (bf16[144,1024]{1,0:T(8,128)(2,1)S(1)}, bf16[144,1024]{1,0:T(8,128)(2,1)S(1)}, u32[]{:S(2)}, u32[]{:S(2)}) collective-permute-start(bf16[144,1024]{1,0:T(8,128)(2,1)S(1)} %pick.4.refs_0_), channel_id=1, source_target_pairs={{0,1},{1,0},{2,3},{3,2},{4,5},{5,4},{6,7},{7,6},{8,9},{9,8},{10,11... | collective-permute-start | bytes 884744 | tf_op jit(solution)/shard_map/ppermute | solution.py:513
  35.4 4.5 %collective-permute-start.15 = (bf16[144,1024]{1,0:T(8,128)(2,1)S(1)}, bf16[144,1024]{1,0:T(8,128)(2,1)S(1)}, u32[]{:S(2)}, u32[]{:S(2)}) collective-permute-start(bf16[144,1024]{1,0:T(8,128)(2,1)S(1)} %pick.5.refs_2_), channel_id=1, source_target_pairs={{0,1},{1,0},{2,3},{3,2},{4,5},{5,4},{6,7},{7,6},{8,9},{9,8},{10,11... | collective-permute-start | bytes 884744 | tf_op jit(solution)/shard_map/ppermute | solution.py:513
  36.0 7.4 %collective-permute-start.8 = (s16[144,512]{1,0:T(8,128)(2,1)S(1)}, s16[144,512]{1,0:T(8,128)(2,1)S(1)}, u32[]{:S(2)}, u32[]{:S(2)}) collective-permute-start(s16[144,512]{1,0:T(8,128)(2,1)S(1)} %get-tuple-element.48.refs_8_), channel_id=1, source_target_pairs={{0,16},{8,24},{16,0},{24,8},{1,17},{9,25},{17,1},{25,9},{2,18},{10... | collective-permute-start | bytes 442376 | tf_op jit(solution)/shard_map/ppermute | solution.py:516
  38.5 6.0 %collective-permute-start.10 = (s16[144,512]{1,0:T(8,128)(2,1)S(1)}, s16[144,512]{1,0:T(8,128)(2,1)S(1)}, u32[]{:S(2)}, u32[]{:S(2)}) collective-permute-start(s16[144,512]{1,0:T(8,128)(2,1)S(1)} %get-tuple-element.52.refs_9_), channel_id=1, source_target_pairs={{0,8},{8,0},{16,24},{24,16},{1,9},{9,1},{17,25},{25,17},{2,10},{10... | collective-permute-start | bytes 442376 | tf_op jit(solution)/shard_map/ppermute | solution.py:516
  42.6 24.5 %collective-permute-start.16 = (s16[528,512]{1,0:T(8,128)(2,1)S(1)}, s16[528,512]{1,0:T(8,128)(2,1)S(1)}, u32[]{:S(2)}, u32[]{:S(2)}) collective-permute-start(s16[528,512]{1,0:T(8,128)(2,1)S(1)} %get-tuple-element.60), channel_id=1, source_target_pairs={{0,8},{8,0},{16,24},{24,16},{1,9},{9,1},{17,25},{25,17},{2,10},{10... | collective-permute-start | bytes 1622024 | tf_op jit(solution)/shard_map/ppermute | solution.py:516
  47.2 22.2 %collective-permute-start.22 = (s16[528,512]{1,0:T(8,128)(2,1)S(1)}, s16[528,512]{1,0:T(8,128)(2,1)S(1)}, u32[]{:S(2)}, u32[]{:S(2)}) collective-permute-start(s16[528,512]{1,0:T(8,128)(2,1)S(1)} %get-tuple-element.70), channel_id=1, source_target_pairs={{0,16},{8,24},{16,0},{24,8},{1,17},{9,25},{17,1},{25,9},{2,18},{10... | collective-permute-start | bytes 1622024 | tf_op jit(solution)/shard_map/ppermute | solution.py:516
  49.9 1.2 %collective-permute-start.17 = (f32[3,8,128]{2,1,0:T(8,128)S(1)}, f32[3,8,128]{2,1,0:T(8,128)S(1)}, u32[]{:S(2)}, u32[]{:S(2)}) collective-permute-start(f32[3,8,128]{2,1,0:T(8,128)S(1)} %get-tuple-element.63), channel_id=1, source_target_pairs={{0,1},{1,0},{2,3},{3,2},{4,5},{5,4},{6,7},{7,6},{8,9},{9,8},{10,11... | collective-permute-start | bytes 36872 | tf_op jit(solution)/shard_map/ppermute | solution.py:513
  51.2 11.8 %collective-permute-start.18 = (f32[8,128]{1,0:T(8,128)S(1)}, f32[8,128]{1,0:T(8,128)S(1)}, u32[]{:S(2)}, u32[]{:S(2)}) collective-permute-start(f32[8,128]{1,0:T(8,128)S(1)} %get-tuple-element.64), channel_id=1, source_target_pairs={{0,2},{1,3},{2,4},{3,5},{6,0},{7,1},{8,10},{9,11},{10,12},{11,13},... | collective-permute-start | bytes 12296 | tf_op jit(solution)/shard_map/ppermute | solution.py:510
  59.5 6.4 %collective-permute-start.19 = (f32[8,128]{1,0:T(8,128)S(1)}, f32[8,128]{1,0:T(8,128)S(1)}, u32[]{:S(2)}, u32[]{:S(2)}) collective-permute-start(f32[8,128]{1,0:T(8,128)S(1)} %get-tuple-element.65), channel_id=1, source_target_pairs={{0,4},{1,5},{4,0},{5,1},{6,2},{7,3},{8,12},{9,13},{12,8},{13,9},{1... | collective-permute-start | bytes 12296 | tf_op jit(solution)/shard_map/ppermute | solution.py:510
  61.7 5.5 %collective-permute-start.20 = (f32[8,128]{1,0:T(8,128)S(1)}, f32[8,128]{1,0:T(8,128)S(1)}, u32[]{:S(2)}, u32[]{:S(2)}) collective-permute-start(f32[8,128]{1,0:T(8,128)S(1)} %get-tuple-element.66), channel_id=1, source_target_pairs={{2,0},{3,1},{4,2},{5,3},{6,4},{7,5},{10,8},{11,9},{12,10},{13,11},... | collective-permute-start | bytes 12296 | tf_op jit(solution)/shard_map/ppermute | solution.py:510
  67.8 9.5 %collective-permute-start.21 = (s16[272,512]{1,0:T(8,128)(2,1)S(1)}, s16[272,512]{1,0:T(8,128)(2,1)S(1)}, u32[]{:S(2)}, u32[]{:S(2)}) collective-permute-start(s16[272,512]{1,0:T(8,128)(2,1)S(1)} %get-tuple-element.67.refs_4_), channel_id=1, source_target_pairs={{0,16},{8,24},{16,0},{24,8},{1,17},{9,25},{17,1},{25,9},{2,18},{10... | collective-permute-start | bytes 835592 | tf_op jit(solution)/shard_map/ppermute | solution.py:516
  70.0 7.3 %collective-permute-start.23 = (s16[272,512]{1,0:T(8,128)(2,1)S(1)}, s16[272,512]{1,0:T(8,128)(2,1)S(1)}, u32[]{:S(2)}, u32[]{:S(2)}) collective-permute-start(s16[272,512]{1,0:T(8,128)(2,1)S(1)} %get-tuple-element.73), channel_id=1, source_target_pairs={{0,8},{8,0},{16,24},{24,16},{1,9},{9,1},{17,25},{25,17},{2,10},{10... | collective-permute-start | bytes 835592 | tf_op jit(solution)/shard_map/ppermute | solution.py:516
  71.7 5.7 %collective-permute-start.26 = (f32[8,128]{1,0:T(8,128)S(1)}, f32[8,128]{1,0:T(8,128)S(1)}, u32[]{:S(2)}, u32[]{:S(2)}) collective-permute-start(f32[8,128]{1,0:T(8,128)S(1)} %add_kernel.1.refs_0_), channel_id=1, source_target_pairs={{0,24},{8,16},{16,8},{24,0},{1,25},{9,17},{17,9},{25,1},{2,26},{10... | collective-permute-start | bytes 12296 | tf_op jit(solution)/shard_map/ppermute | solution.py:516
  72.1 5.2 %collective-permute-start.25 = (f32[8,128]{1,0:T(8,128)S(1)}, f32[8,128]{1,0:T(8,128)S(1)}, u32[]{:S(2)}, u32[]{:S(2)}) collective-permute-start(f32[8,128]{1,0:T(8,128)S(1)} %add_kernel.1.refs_0_), channel_id=1, source_target_pairs={{0,16},{8,24},{16,0},{24,8},{1,17},{9,25},{17,1},{25,9},{2,18},{10... | collective-permute-start | bytes 12296 | tf_op jit(solution)/shard_map/ppermute | solution.py:516
  73.6 3.8 %collective-permute-start.24 = (f32[8,128]{1,0:T(8,128)S(1)}, f32[8,128]{1,0:T(8,128)S(1)}, u32[]{:S(2)}, u32[]{:S(2)}) collective-permute-start(f32[8,128]{1,0:T(8,128)S(1)} %add_kernel.1.refs_0_), channel_id=1, source_target_pairs={{0,8},{8,0},{16,24},{24,16},{1,9},{9,1},{17,25},{25,17},{2,10},{10... | collective-permute-start | bytes 12296 | tf_op jit(solution)/shard_map/ppermute | solution.py:516

commit v5 on v3

--- a/solution.py
+++ b/solution.py
@@ -484,16 +484,17 @@
     refs[-1][...] = total
 
 
-def small(kernel, outs, *args):
-    return pl.pallas_call(
-        kernel,
-        in_specs=[VMEM] * len(args),
+def small(kernel, outs, *args, after=()):
+    used = len(args)
+    return pl.pallas_call(
+        lambda *refs: kernel(*refs[:used], *refs[used + len(after) :]),
+        in_specs=[VMEM] * used + [ANY] * len(after),
         out_specs=[VMEM] * len(outs),
         out_shape=outs,
         compiler_params=pltpu.CompilerParams(vmem_limit_bytes=2 * MIB),
         cost_estimate=cost(args),
         name=kernel.__name__,
-    )(*args)
+    )(*args, *after)
 
 
 def blockwise(most, grad_out, routes, slots, gates, capacity, hidden, down_weight):
@@ -524,7 +525,7 @@
     sent, kept = [], []
     for local in range(2):
         send, keep, info = partial_share(
-            local, most, top, (0,), capacity, weight, pair, after=far_stored if local else ()
+            local, most, top, (0,), capacity, weight, pair, after=far_stored[:1] if local else ()
         )
         sent.append(send)
         kept.append(keep)
@@ -553,17 +554,17 @@
 
     one = like((top, tokens))
     two = like((2, top, tokens))
+    (got0, keep0, gate0), (got1, keep1, gate1) = halves
     stay, away = small(chips_kernel, [two, two], mine, across(theirs))
-    stay, away = small(
-        chip_kernel, [one, one], stay, along(away, [(z, z ^ 2) for z in range(peers // 2)])
-    )
-    (total,) = small(add_kernel, [one], stay, along(away, [(z, z ^ 1) for z in range(peers // 2)]))
+    came = along(away, [(z, z ^ 2) for z in range(peers // 2)])
+    stay, away = small(chip_kernel, [one, one], stay, came)
+    send0, rest0 = middle(got0, keep0, (away,))
+    (total,) = small(
+        add_kernel, [one], stay, along(away, [(z, z ^ 1) for z in range(peers // 2)]), after=(send0,)
+    )
     whole = [total] + [over(total, flip) for flip in range(1, ranks)]
-
-    sums = []
-    for local, (got, keep, gate) in enumerate(halves):
-        send, rest = middle(got, keep, (total,))
-        sums += [over(send, 2 - local), rest, gate]
+    send1, rest1 = middle(got1, keep1, (total,))
+    sums = [over(send0, 2), rest0, gate0, over(send1, 1), rest1, gate1]
     hidden_grad, gate_grad = finish(most, first_grad, sums, whole)
     return hidden_grad, gate_grad.T
 

time: 75.5 us -> 72.5 us (0.960)
  starting transfers between devices: 37.5 us -> 33 us
  waiting for transfers between devices: 16.8 us -> 18.3 us
    ppermute x15, waiting for transfers between devices: 5.86 us -> 8.62 us  [over(): return lax.ppermute(rows, 'dp', [(i, i ^ flip) for i in range(ranks)])]
    ppermute x7, starting transfers between devices: 18.2 us -> 15.5 us  [along(): lax.ppermute(rows, 'expert', [(2 * a + c, 2 * b + c) for a, b in pairs fo...]
    ppermute x15, starting transfers between devices: 19 us -> 17.2 us  [over(): return lax.ppermute(rows, 'dp', [(i, i ^ flip) for i in range(ranks)])]
    ppermute x7, waiting for transfers between devices: 9.77 us -> 8.52 us  [along(): lax.ppermute(rows, 'expert', [(2 * a + c, 2 * b + c) for a, b in pairs fo...]
  transfers between devices with their start and end apart: 26 -> 26, of which waited for: 13 -> 12; matrix products, arithmetic and copies ran while one was open for 0% -> 0% of each run, Pallas kernels for 23% -> 24%
where the time goes in v5:
time: 72.5 us; the launch traced here: 72.2 us
  starting transfers between devices  33 us (46%)
  Pallas kernels  20 us (28%)
  waiting for transfers between devices  18.3 us (25%)
  between operations  0.86 us (1%)
    ppermute x15, starting transfers between devices, over(): return lax.ppermute(rows, 'dp', [(i, i ^ flip) for i in range(ranks)])  17.2 us
    ppermute x7, starting transfers between devices, along(): lax.ppermute(rows, 'expert', [(2 * a + c, 2 * b + c) for a, b in pairs fo...  15.5 us
    pallas_call x4, Pallas kernels, partial_share(): pl.pallas_call(functools.partial(share_kernel, local, most, top, group, e...  10.3 us
    ppermute x15, waiting for transfers between devices, over(): return lax.ppermute(rows, 'dp', [(i, i ^ flip) for i in range(ranks)])  8.62 us
    ppermute x7, waiting for transfers between devices, along(): lax.ppermute(rows, 'expert', [(2 * a + c, 2 * b + c) for a, b in pairs fo...  8.52 us
    pallas_call x1, Pallas kernels, load(): pl.pallas_call(load_kernel, in_specs=[ANY, ANY], out_specs=VMEM, out_shap...  3.39 us
    pallas_call x4, Pallas kernels, middle(): pl.pallas_call(middle_kernel, in_specs=[VMEM, VMEM] + [ANY] * len(after),...  2.17 us
    pallas_call x1, Pallas kernels, finish(): pl.pallas_call(functools.partial(finish_kernel, most), in_specs=[VMEM] *...  1.52 us
  transfers between devices with their start and end apart: 26, of which 12 were waited for; matrix products, arithmetic and copies ran while one was open for 0% of the time, Pallas kernels for 24%

profile of v5, /device:TPU:0, one launch (start us, length us, event | category | flops | bytes accessed | tf_op | source)
XLA Modules:
  0.0 72.2 jit_solution(10624029284806165287)
XLA Ops:
  0.6 1.4 %prepare.1 = (bf16[144,1024]{1,0:T(8,128)(2,1)S(1)}, bf16[2,128,512]{2,1,0:T(8,128)(2,1)S(1)}, bf16[2,256,512]{2,1,0:T(8,128)(2,1)S(1)}) custom-call(bf16[128,1024]{1,0:T(8,128)(2,1)} %rows.1, s32[8,128]{1,0:T(8,128)} %bitcast.4, s32[8,128]{1,0:T(8,128)} %bitcast.5, bf16[8,128]{1,0:T(8,128)(2,1)} %bitcast.6, bf16[2,384,512]{2,1,0:T(8,128)(2,1)} %hidden.1), custom_call_target="tpu_custom_call" | custom-call | bytes 1310720 | tf_op jit(solution)/shard_map/prepare/pallas_call | solution.py:177
  2.0 4.9 %collective-permute-start = (bf16[144,1024]{1,0:T(8,128)(2,1)S(1)}, bf16[144,1024]{1,0:T(8,128)(2,1)S(1)}, u32[]{:S(2)}, u32[]{:S(2)}) collective-permute-start(bf16[144,1024]{1,0:T(8,128)(2,1)S(1)} %get-tuple-element.41.after.refs_0_.block), channel_id=1, source_target_pairs={{0,2},{1,3},{2,4},{3,5},{4,6},{5,7},{8,10},{9,11},{10,12},{11,13},... | collective-permute-start | bytes 884744 | tf_op jit(solution)/shard_map/ppermute | solution.py:505
  7.0 1.6 %collective-permute-start.4 = (bf16[2,256,512]{2,1,0:T(8,128)(2,1)S(1)}, bf16[2,256,512]{2,1,0:T(8,128)(2,1)S(1)}, u32[]{:S(2)}, u32[]{:S(2)}) collective-permute-start(bf16[2,256,512]{2,1,0:T(8,128)(2,1)S(1)} %get-tuple-element.42.refs_4_), channel_id=1, source_target_pairs={{0,16},{8,24},{16,0},{24,8},{1,17},{9,25},{17,1},{25,9},{2,18},{10... | collective-permute-start | bytes 1572872 | tf_op jit(solution)/shard_map/ppermute | solution.py:511
  8.5 1.5 %collective-permute-start.3 = (bf16[2,256,512]{2,1,0:T(8,128)(2,1)S(1)}, bf16[2,256,512]{2,1,0:T(8,128)(2,1)S(1)}, u32[]{:S(2)}, u32[]{:S(2)}) collective-permute-start(bf16[2,256,512]{2,1,0:T(8,128)(2,1)S(1)} %get-tuple-element.42.refs_4_), channel_id=1, source_target_pairs={{0,8},{8,0},{16,24},{24,16},{1,9},{9,1},{17,25},{25,17},{2,10},{10... | collective-permute-start | bytes 1572872 | tf_op jit(solution)/shard_map/ppermute | solution.py:511
  10.0 1.3 %collective-permute-start.1 = (bf16[144,1024]{1,0:T(8,128)(2,1)S(1)}, bf16[144,1024]{1,0:T(8,128)(2,1)S(1)}, u32[]{:S(2)}, u32[]{:S(2)}) collective-permute-start(bf16[144,1024]{1,0:T(8,128)(2,1)S(1)} %get-tuple-element.41.after.refs_0_.block), channel_id=1, source_target_pairs={{4,2},{5,3},{2,0},{3,1},{12,10},{13,11},{10,8},{11,9},{20,18},{21,... | collective-permute-start | bytes 884744 | tf_op jit(solution)/shard_map/ppermute | solution.py:505
  11.3 1.9 %collective-permute-done.refs_1_.refs_0_ = bf16[144,1024]{1,0:T(8,128)(2,1)S(1)} collective-permute-done((bf16[144,1024]{1,0:T(8,128)(2,1)S(1)}, bf16[144,1024]{1,0:T(8,128)(2,1)S(1)}, u32[]{:S(2)}, u32[]{:S(2)}) %collective-permute-start) | collective-permute-done | bytes 294944 | tf_op jit(solution)/shard_map/ppermute | solution.py:505
  13.9 3.4 %load_weight.1.refs_2_.weight = bf16[2,2048,1024]{2,1,0:T(8,128)(2,1)S(1)} custom-call(bf16[144,1024]{1,0:T(8,128)(2,1)S(1)} %get-tuple-element.41.after.refs_0_.block, bf16[2,2048,1024]{2,1,0:T(8,128)(2,1)} %weight.1), custom_call_target="tpu_custom_call" | custom-call | bytes 16777216 | tf_op jit(solution)/shard_map/load_weight/pallas_call | solution.py:205
  17.3 2.5 %collective-permute-done.1.refs_3_.refs_2_.refs_1_ = bf16[144,1024]{1,0:T(8,128)(2,1)S(1)} collective-permute-done((bf16[144,1024]{1,0:T(8,128)(2,1)S(1)}, bf16[144,1024]{1,0:T(8,128)(2,1)S(1)}, u32[]{:S(2)}, u32[]{:S(2)}) %collective-permute-start.1) | collective-permute-done | bytes 294944 | tf_op jit(solution)/shard_map/ppermute | solution.py:505
  20.4 1.2 %collective-permute-done.3.over_x.refs_5_ = bf16[2,256,512]{2,1,0:T(8,128)(2,1)S(1)} collective-permute-done((bf16[2,256,512]{2,1,0:T(8,128)(2,1)S(1)}, bf16[2,256,512]{2,1,0:T(8,128)(2,1)S(1)}, u32[]{:S(2)}, u32[]{:S(2)}) %collective-permute-start.3) | collective-permute-done | bytes 524320 | tf_op jit(solution)/shard_map/ppermute | solution.py:511
  22.3 1.3 %collective-permute-start.13 = (bf16[144,1024]{1,0:T(8,128)(2,1)S(1)}, bf16[144,1024]{1,0:T(8,128)(2,1)S(1)}, u32[]{:S(2)}, u32[]{:S(2)}) collective-permute-start(bf16[144,1024]{1,0:T(8,128)(2,1)S(1)} %get-tuple-element.54), channel_id=1, source_target_pairs={{4,0},{5,1},{12,8},{13,9},{20,16},{21,17},{28,24},{29,25}} | collective-permute-start | bytes 884744 | tf_op jit(solution)/shard_map/ppermute | solution.py:505
  24.3 1.6 %collective-permute-start.11 = (bf16[256,512]{1,0:T(8,128)(2,1)S(1)}, bf16[256,512]{1,0:T(8,128)(2,1)S(1)}, u32[]{:S(2)}, u32[]{:S(2)}) collective-permute-start(bf16[256,512]{1,0:T(8,128)(2,1)S(1)} %get-tuple-element.53), channel_id=1, source_target_pairs={{0,8},{8,0},{16,24},{24,16},{1,9},{9,1},{17,25},{25,17},{2,10},{10... | collective-permute-start | bytes 786440 | tf_op jit(solution)/shard_map/ppermute | solution.py:511
  25.9 2.7 %share_0.2 = (s16[272,512]{1,0:T(8,128)(2,1)S(1)}, f32[2,128,512]{2,1,0:T(8,128)S(1)}, f32[2,16,384]{2,1,0:T(8,128)}) custom-call(s32[2]{0:T(128)S(1)} %copy-done, bf16[2,2048,1024]{2,1,0:T(8,128)(2,1)S(1)} %load_weight.1.refs_2_.weight, bf16[144,1024]{1,0:T(8,128)(2,1)S(1)} %pick.3.refs_0_, bf16[144,1024]{1,0:T(8,128)(2,1)S(1)} %collective-permute-done.2.refs_1_), custom_call_target="tpu_custom_call" | custom-call | flops 536870912 | bytes 8978432 | tf_op jit(solution)/shard_map/share_0/pallas_call | solution.py:370
  29.1 2.2 %share_1.2 = (s16[272,512]{1,0:T(8,128)(2,1)S(1)}, f32[2,128,512]{2,1,0:T(8,128)S(1)}, f32[2,16,384]{2,1,0:T(8,128)S(1)}) custom-call(s32[2]{0:T(128)S(1)} %copy-done, bf16[2,2048,1024]{2,1,0:T(8,128)(2,1)S(1)} %load_weight.1.refs_2_.weight, bf16[144,1024]{1,0:T(8,128)(2,1)S(1)} %pick.3.refs_0_, bf16[144,1024]{1,0:T(8,128)(2,1)S(1)} %collective-permute-done.2.refs_1_, ...), custom_call_target="tpu_custom_call" | custom-call | flops 536870912 | bytes 8978432 | tf_op jit(solution)/shard_map/share_1/pallas_call | solution.py:370
  31.4 1.6 %collective-permute-start.8 = (s16[272,512]{1,0:T(8,128)(2,1)S(1)}, s16[272,512]{1,0:T(8,128)(2,1)S(1)}, u32[]{:S(2)}, u32[]{:S(2)}) collective-permute-start(s16[272,512]{1,0:T(8,128)(2,1)S(1)} %get-tuple-element.49.refs_4_), channel_id=1, source_target_pairs={{0,16},{8,24},{16,0},{24,8},{1,17},{9,25},{17,1},{25,9},{2,18},{10... | collective-permute-start | bytes 835592 | tf_op jit(solution)/shard_map/ppermute | solution.py:511
  34.3 2.8 %collective-permute-done.6.got = s16[272,512]{1,0:T(8,128)(2,1)S(1)} collective-permute-done((s16[272,512]{1,0:T(8,128)(2,1)S(1)}, s16[272,512]{1,0:T(8,128)(2,1)S(1)}, u32[]{:S(2)}, u32[]{:S(2)}) %collective-permute-start.6) | collective-permute-done | bytes 278560 | tf_op jit(solution)/shard_map/ppermute | solution.py:511
  37.6 1.6 %collective-permute-start.7 = (s16[144,512]{1,0:T(8,128)(2,1)S(1)}, s16[144,512]{1,0:T(8,128)(2,1)S(1)}, u32[]{:S(2)}, u32[]{:S(2)}) collective-permute-start(s16[144,512]{1,0:T(8,128)(2,1)S(1)} %get-tuple-element.47.refs_8_), channel_id=1, source_target_pairs={{0,16},{8,24},{16,0},{24,8},{1,17},{9,25},{17,1},{25,9},{2,18},{10... | collective-permute-start | bytes 442376 | tf_op jit(solution)/shard_map/ppermute | solution.py:511
  39.6 1.2 %collective-permute-start.9 = (s16[144,512]{1,0:T(8,128)(2,1)S(1)}, s16[144,512]{1,0:T(8,128)(2,1)S(1)}, u32[]{:S(2)}, u32[]{:S(2)}) collective-permute-start(s16[144,512]{1,0:T(8,128)(2,1)S(1)} %get-tuple-element.51.refs_9_), channel_id=1, source_target_pairs={{0,8},{8,0},{16,24},{24,16},{1,9},{9,1},{17,25},{25,17},{2,10},{10... | collective-permute-start | bytes 442376 | tf_op jit(solution)/shard_map/ppermute | solution.py:511
  40.8 2.7 %share_0.3 = (s16[528,512]{1,0:T(8,128)(2,1)S(1)}, f32[2,256,512]{2,1,0:T(8,128)S(1)}, f32[256,128]{1,0:T(8,128)S(1)}, f32[3,8,128]{2,1,0:T(8,128)S(1)}, f32[3,8,128]{2,1,0:T(8,128)S(1)}) custom-call(s32[2]{0:T(128)S(1)} %copy-done, bf16[2,2048,1024]{2,1,0:T(8,128)(2,1)S(1)} %load_weight.1.refs_2_.weight, bf16[144,1024]{1,0:T(8,128)(2,1)S(1)} %pick.4.refs_0_, ...), custom_call_target="tpu_custom_call" | custom-call | flops 1073741824 | bytes 9568256 | tf_op jit(solution)/shard_map/share_0/pallas_call | solution.py:370
  43.5 1.0 %collective-permute-start.16 = (s16[528,512]{1,0:T(8,128)(2,1)S(1)}, s16[528,512]{1,0:T(8,128)(2,1)S(1)}, u32[]{:S(2)}, u32[]{:S(2)}) collective-permute-start(s16[528,512]{1,0:T(8,128)(2,1)S(1)} %get-tuple-element.60), channel_id=1, source_target_pairs={{0,8},{8,0},{16,24},{24,16},{1,9},{9,1},{17,25},{25,17},{2,10},{10... | collective-permute-start | bytes 1622024 | tf_op jit(solution)/shard_map/ppermute | solution.py:511
  44.5 1.8 %collective-permute-done.9.refs_11_.got1 = s16[144,512]{1,0:T(8,128)(2,1)S(1)} collective-permute-done((s16[144,512]{1,0:T(8,128)(2,1)S(1)}, s16[144,512]{1,0:T(8,128)(2,1)S(1)}, u32[]{:S(2)}, u32[]{:S(2)}) %collective-permute-start.9) | collective-permute-done | bytes 147488 | tf_op jit(solution)/shard_map/ppermute | solution.py:511
  46.3 2.7 %share_1.3 = (s16[528,512]{1,0:T(8,128)(2,1)S(1)}, f32[2,256,512]{2,1,0:T(8,128)S(1)}, f32[256,128]{1,0:T(8,128)S(1)}, f32[3,8,128]{2,1,0:T(8,128)S(1)}, f32[3,8,128]{2,1,0:T(8,128)S(1)}) custom-call(s32[2]{0:T(128)S(1)} %copy-done, bf16[2,2048,1024]{2,1,0:T(8,128)(2,1)S(1)} %load_weight.1.refs_2_.weight, bf16[144,1024]{1,0:T(8,128)(2,1)S(1)} %pick.4.refs_0_, ...), custom_call_target="tpu_custom_call" | custom-call | flops 1073741824 | bytes 9568256 | tf_op jit(solution)/shard_map/share_1/pallas_call | solution.py:370
  49.3 0.9 %first_finish.1 = (f32[2,128,512]{2,1,0:T(8,128)S(1)}, f32[3,8,128]{2,1,0:T(8,128)S(1)}, f32[3,8,128]{2,1,0:T(8,128)S(1)}) custom-call(s32[2]{0:T(128)S(1)} %copy-done, bf16[2,128,512]{2,1,0:T(8,128)(2,1)S(1)} %get-tuple-element.40.hidden, f32[2,16,384]{2,1,0:T(8,128)S(1)} %get-tuple-element.44.info, ...), custom_call_target="tpu_custom_call" | custom-call | bytes 1081344 | tf_op jit(solution)/shard_map/first_finish/pallas_call | solution.py:427
  50.4 1.2 %collective-permute-done.17.refs_1_ = f32[3,8,128]{2,1,0:T(8,128)S(1)} collective-permute-done((f32[3,8,128]{2,1,0:T(8,128)S(1)}, f32[3,8,128]{2,1,0:T(8,128)S(1)}, u32[]{:S(2)}, u32[]{:S(2)}) %collective-permute-start.17) | collective-permute-done | bytes 12320 | tf_op jit(solution)/shard_map/ppermute | solution.py:508
  51.5 5.7 %collective-permute-start.18 = (f32[2,8,128]{2,1,0:T(8,128)S(1)}, f32[2,8,128]{2,1,0:T(8,128)S(1)}, u32[]{:S(2)}, u32[]{:S(2)}) collective-permute-start(f32[2,8,128]{2,1,0:T(8,128)S(1)} %get-tuple-element.65), channel_id=1, source_target_pairs={{0,4},{1,5},{2,6},{3,7},{4,0},{5,1},{6,2},{7,3},{8,12},{9,13},{10,... | collective-permute-start | bytes 24584 | tf_op jit(solution)/shard_map/ppermute | solution.py:505
  57.2 1.6 %collective-permute-done.18.refs_1_ = f32[2,8,128]{2,1,0:T(8,128)S(1)} collective-permute-done((f32[2,8,128]{2,1,0:T(8,128)S(1)}, f32[2,8,128]{2,1,0:T(8,128)S(1)}, u32[]{:S(2)}, u32[]{:S(2)}) %collective-permute-start.18) | collective-permute-done | bytes 8224 | tf_op jit(solution)/shard_map/ppermute | solution.py:505
  58.8 1.0 %collective-permute-start.21 = (f32[8,128]{1,0:T(8,128)S(1)}, f32[8,128]{1,0:T(8,128)S(1)}, u32[]{:S(2)}, u32[]{:S(2)}) collective-permute-start(f32[8,128]{1,0:T(8,128)S(1)} %get-tuple-element.66.refs_0_), channel_id=1, source_target_pairs={{0,2},{1,3},{2,0},{3,1},{4,6},{5,7},{6,4},{7,5},{8,10},{9,11},{10,... | collective-permute-start | bytes 12296 | tf_op jit(solution)/shard_map/ppermute | solution.py:505
  60.7 1.8 %collective-permute-done.21.refs_1_ = f32[8,128]{1,0:T(8,128)S(1)} collective-permute-done((f32[8,128]{1,0:T(8,128)S(1)}, f32[8,128]{1,0:T(8,128)S(1)}, u32[]{:S(2)}, u32[]{:S(2)}) %collective-permute-start.21) | collective-permute-done | bytes 4128 | tf_op jit(solution)/shard_map/ppermute | solution.py:505
  63.1 2.1 %collective-permute-start.22 = (s16[272,512]{1,0:T(8,128)(2,1)S(1)}, s16[272,512]{1,0:T(8,128)(2,1)S(1)}, u32[]{:S(2)}, u32[]{:S(2)}) collective-permute-start(s16[272,512]{1,0:T(8,128)(2,1)S(1)} %get-tuple-element.73), channel_id=1, source_target_pairs={{0,8},{8,0},{16,24},{24,16},{1,9},{9,1},{17,25},{25,17},{2,10},{10... | collective-permute-start | bytes 835592 | tf_op jit(solution)/shard_map/ppermute | solution.py:511
  65.7 1.0 %collective-permute-start.24 = (f32[8,128]{1,0:T(8,128)S(1)}, f32[8,128]{1,0:T(8,128)S(1)}, u32[]{:S(2)}, u32[]{:S(2)}) collective-permute-start(f32[8,128]{1,0:T(8,128)S(1)} %add_kernel.1.refs_0_), channel_id=1, source_target_pairs={{0,16},{8,24},{16,0},{24,8},{1,17},{9,25},{17,1},{25,9},{2,18},{10... | collective-permute-start | bytes 12296 | tf_op jit(solution)/shard_map/ppermute | solution.py:511
  66.7 1.9 %collective-permute-start.23 = (f32[8,128]{1,0:T(8,128)S(1)}, f32[8,128]{1,0:T(8,128)S(1)}, u32[]{:S(2)}, u32[]{:S(2)}) collective-permute-start(f32[8,128]{1,0:T(8,128)S(1)} %add_kernel.1.refs_0_), channel_id=1, source_target_pairs={{0,8},{8,0},{16,24},{24,16},{1,9},{9,1},{17,25},{25,17},{2,10},{10... | collective-permute-start | bytes 12296 | tf_op jit(solution)/shard_map/ppermute | solution.py:511
  68.7 2.0 %collective-permute-done.25.refs_3_ = f32[8,128]{1,0:T(8,128)S(1)} collective-permute-done((f32[8,128]{1,0:T(8,128)S(1)}, f32[8,128]{1,0:T(8,128)S(1)}, u32[]{:S(2)}, u32[]{:S(2)}) %collective-permute-start.25) | collective-permute-done | bytes 4128 | tf_op jit(solution)/shard_map/ppermute | solution.py:511
  70.7 1.5 %finish.1 = (f32[2,384,512]{2,1,0:T(8,128)}, f32[8,128]{1,0:T(8,128)}) custom-call(f32[2,128,512]{2,1,0:T(8,128)S(1)} %get-tuple-element.59.first, s16[272,512]{1,0:T(8,128)(2,1)S(1)} %collective-permute-done.19.got0, f32[256,512]{1,0:T(8,128)S(1)} %get-tuple-element.68.rest0, f32[256,128]{1,0:T(8,128)S(1)} %get-tuple-element.69.gates0, ...), custom_call_target="tpu_custom_call" | custom-call | bytes 2916352 | tf_op jit(solution)/shard_map/finish/pallas_call | solution.py:452
  (41 shorter events, 7.9 us)
Async XLA Ops:
  2.0 11.2 %collective-permute-start = (bf16[144,1024]{1,0:T(8,128)(2,1)S(1)}, bf16[144,1024]{1,0:T(8,128)(2,1)S(1)}, u32[]{:S(2)}, u32[]{:S(2)}) collective-permute-start(bf16[144,1024]{1,0:T(8,128)(2,1)S(1)} %get-tuple-element.41.after.refs_0_.block), channel_id=1, source_target_pairs={{0,2},{1,3},{2,4},{3,5},{4,6},{5,7},{8,10},{9,11},{10,12},{11,13},... | collective-permute-start | bytes 884744 | tf_op jit(solution)/shard_map/ppermute | solution.py:505
  7.0 13.4 %collective-permute-start.4 = (bf16[2,256,512]{2,1,0:T(8,128)(2,1)S(1)}, bf16[2,256,512]{2,1,0:T(8,128)(2,1)S(1)}, u32[]{:S(2)}, u32[]{:S(2)}) collective-permute-start(bf16[2,256,512]{2,1,0:T(8,128)(2,1)S(1)} %get-tuple-element.42.refs_4_), channel_id=1, source_target_pairs={{0,16},{8,24},{16,0},{24,8},{1,17},{9,25},{17,1},{25,9},{2,18},{10... | collective-permute-start | bytes 1572872 | tf_op jit(solution)/shard_map/ppermute | solution.py:511
  8.5 13.1 %collective-permute-start.3 = (bf16[2,256,512]{2,1,0:T(8,128)(2,1)S(1)}, bf16[2,256,512]{2,1,0:T(8,128)(2,1)S(1)}, u32[]{:S(2)}, u32[]{:S(2)}) collective-permute-start(bf16[2,256,512]{2,1,0:T(8,128)(2,1)S(1)} %get-tuple-element.42.refs_4_), channel_id=1, source_target_pairs={{0,8},{8,0},{16,24},{24,16},{1,9},{9,1},{17,25},{25,17},{2,10},{10... | collective-permute-start | bytes 1572872 | tf_op jit(solution)/shard_map/ppermute | solution.py:511
  10.0 9.8 %collective-permute-start.1 = (bf16[144,1024]{1,0:T(8,128)(2,1)S(1)}, bf16[144,1024]{1,0:T(8,128)(2,1)S(1)}, u32[]{:S(2)}, u32[]{:S(2)}) collective-permute-start(bf16[144,1024]{1,0:T(8,128)(2,1)S(1)} %get-tuple-element.41.after.refs_0_.block), channel_id=1, source_target_pairs={{4,2},{5,3},{2,0},{3,1},{12,10},{13,11},{10,8},{11,9},{20,18},{21,... | collective-permute-start | bytes 884744 | tf_op jit(solution)/shard_map/ppermute | solution.py:505
  13.2 10.5 %collective-permute-start.10 = (bf16[144,1024]{1,0:T(8,128)(2,1)S(1)}, bf16[144,1024]{1,0:T(8,128)(2,1)S(1)}, u32[]{:S(2)}, u32[]{:S(2)}) collective-permute-start(bf16[144,1024]{1,0:T(8,128)(2,1)S(1)} %collective-permute-done.refs_1_.refs_0_), channel_id=1, source_target_pairs={{2,4},{3,5},{4,6},{5,7},{10,12},{11,13},{12,14},{13,15},{18,20},{1... | collective-permute-start | bytes 884744 | tf_op jit(solution)/shard_map/ppermute | solution.py:505
  17.3 8.6 %copy-start = (s32[2]{0:T(128)S(1)}, s32[2]{0:T(128)}, u32[]{:S(2)}) copy-start(s32[2]{0:T(128)} %cap.9) | copy-start | bytes 28
  19.9 6.0 %collective-permute-start.2 = (bf16[144,1024]{1,0:T(8,128)(2,1)S(1)}, bf16[144,1024]{1,0:T(8,128)(2,1)S(1)}, u32[]{:S(2)}, u32[]{:S(2)}) collective-permute-start(bf16[144,1024]{1,0:T(8,128)(2,1)S(1)} %pick.3.refs_0_), channel_id=1, source_target_pairs={{0,1},{1,0},{2,3},{3,2},{4,5},{5,4},{6,7},{7,6},{8,9},{9,8},{10,11... | collective-permute-start | bytes 884744 | tf_op jit(solution)/shard_map/ppermute | solution.py:508
  21.8 7.3 %collective-permute-start.5 = (bf16[256,512]{1,0:T(8,128)(2,1)S(1)}, bf16[256,512]{1,0:T(8,128)(2,1)S(1)}, u32[]{:S(2)}, u32[]{:S(2)}) collective-permute-start(bf16[256,512]{1,0:T(8,128)(2,1)S(1)} %get-tuple-element.43), channel_id=1, source_target_pairs={{0,16},{8,24},{16,0},{24,8},{1,17},{9,25},{17,1},{25,9},{2,18},{10... | collective-permute-start | bytes 786440 | tf_op jit(solution)/shard_map/ppermute | solution.py:511
  22.3 11.8 %collective-permute-start.13 = (bf16[144,1024]{1,0:T(8,128)(2,1)S(1)}, bf16[144,1024]{1,0:T(8,128)(2,1)S(1)}, u32[]{:S(2)}, u32[]{:S(2)}) collective-permute-start(bf16[144,1024]{1,0:T(8,128)(2,1)S(1)} %get-tuple-element.54), channel_id=1, source_target_pairs={{4,0},{5,1},{12,8},{13,9},{20,16},{21,17},{28,24},{29,25}} | collective-permute-start | bytes 884744 | tf_op jit(solution)/shard_map/ppermute | solution.py:505
  23.6 10.5 %collective-permute-start.14 = (bf16[144,1024]{1,0:T(8,128)(2,1)S(1)}, bf16[144,1024]{1,0:T(8,128)(2,1)S(1)}, u32[]{:S(2)}, u32[]{:S(2)}) collective-permute-start(bf16[144,1024]{1,0:T(8,128)(2,1)S(1)} %collective-permute-done.10.refs_1_.refs_2_), channel_id=1, source_target_pairs={{4,6},{5,7},{12,14},{13,15},{20,22},{21,23},{28,30},{29,31}} | collective-permute-start | bytes 884744 | tf_op jit(solution)/shard_map/ppermute | solution.py:505
  24.3 8.9 %collective-permute-start.11 = (bf16[256,512]{1,0:T(8,128)(2,1)S(1)}, bf16[256,512]{1,0:T(8,128)(2,1)S(1)}, u32[]{:S(2)}, u32[]{:S(2)}) collective-permute-start(bf16[256,512]{1,0:T(8,128)(2,1)S(1)} %get-tuple-element.53), channel_id=1, source_target_pairs={{0,8},{8,0},{16,24},{24,16},{1,9},{9,1},{17,25},{25,17},{2,10},{10... | collective-permute-start | bytes 786440 | tf_op jit(solution)/shard_map/ppermute | solution.py:511
  28.6 8.6 %collective-permute-start.6 = (s16[272,512]{1,0:T(8,128)(2,1)S(1)}, s16[272,512]{1,0:T(8,128)(2,1)S(1)}, u32[]{:S(2)}, u32[]{:S(2)}) collective-permute-start(s16[272,512]{1,0:T(8,128)(2,1)S(1)} %get-tuple-element.45.refs_3_), channel_id=1, source_target_pairs={{0,8},{8,0},{16,24},{24,16},{1,9},{9,1},{17,25},{25,17},{2,10},{10... | collective-permute-start | bytes 835592 | tf_op jit(solution)/shard_map/ppermute | solution.py:511
  31.4 7.8 %collective-permute-start.8 = (s16[272,512]{1,0:T(8,128)(2,1)S(1)}, s16[272,512]{1,0:T(8,128)(2,1)S(1)}, u32[]{:S(2)}, u32[]{:S(2)}) collective-permute-start(s16[272,512]{1,0:T(8,128)(2,1)S(1)} %get-tuple-element.49.refs_4_), channel_id=1, source_target_pairs={{0,16},{8,24},{16,0},{24,8},{1,17},{9,25},{17,1},{25,9},{2,18},{10... | collective-permute-start | bytes 835592 | tf_op jit(solution)/shard_map/ppermute | solution.py:511
  33.4 7.4 %collective-permute-start.12 = (bf16[144,1024]{1,0:T(8,128)(2,1)S(1)}, bf16[144,1024]{1,0:T(8,128)(2,1)S(1)}, u32[]{:S(2)}, u32[]{:S(2)}) collective-permute-start(bf16[144,1024]{1,0:T(8,128)(2,1)S(1)} %pick.4.refs_0_), channel_id=1, source_target_pairs={{0,1},{1,0},{2,3},{3,2},{4,5},{5,4},{6,7},{7,6},{8,9},{9,8},{10,11... | collective-permute-start | bytes 884744 | tf_op jit(solution)/shard_map/ppermute | solution.py:508
  34.2 6.5 %collective-permute-start.15 = (bf16[144,1024]{1,0:T(8,128)(2,1)S(1)}, bf16[144,1024]{1,0:T(8,128)(2,1)S(1)}, u32[]{:S(2)}, u32[]{:S(2)}) collective-permute-start(bf16[144,1024]{1,0:T(8,128)(2,1)S(1)} %pick.5.refs_2_), channel_id=1, source_target_pairs={{0,1},{1,0},{2,3},{3,2},{4,5},{5,4},{6,7},{7,6},{8,9},{9,8},{10,11... | collective-permute-start | bytes 884744 | tf_op jit(solution)/shard_map/ppermute | solution.py:508
  37.6 6.9 %collective-permute-start.7 = (s16[144,512]{1,0:T(8,128)(2,1)S(1)}, s16[144,512]{1,0:T(8,128)(2,1)S(1)}, u32[]{:S(2)}, u32[]{:S(2)}) collective-permute-start(s16[144,512]{1,0:T(8,128)(2,1)S(1)} %get-tuple-element.47.refs_8_), channel_id=1, source_target_pairs={{0,16},{8,24},{16,0},{24,8},{1,17},{9,25},{17,1},{25,9},{2,18},{10... | collective-permute-start | bytes 442376 | tf_op jit(solution)/shard_map/ppermute | solution.py:511
  39.6 6.7 %collective-permute-start.9 = (s16[144,512]{1,0:T(8,128)(2,1)S(1)}, s16[144,512]{1,0:T(8,128)(2,1)S(1)}, u32[]{:S(2)}, u32[]{:S(2)}) collective-permute-start(s16[144,512]{1,0:T(8,128)(2,1)S(1)} %get-tuple-element.51.refs_9_), channel_id=1, source_target_pairs={{0,8},{8,0},{16,24},{24,16},{1,9},{9,1},{17,25},{25,17},{2,10},{10... | collective-permute-start | bytes 442376 | tf_op jit(solution)/shard_map/ppermute | solution.py:511
  43.5 16.4 %collective-permute-start.16 = (s16[528,512]{1,0:T(8,128)(2,1)S(1)}, s16[528,512]{1,0:T(8,128)(2,1)S(1)}, u32[]{:S(2)}, u32[]{:S(2)}) collective-permute-start(s16[528,512]{1,0:T(8,128)(2,1)S(1)} %get-tuple-element.60), channel_id=1, source_target_pairs={{0,8},{8,0},{16,24},{24,16},{1,9},{9,1},{17,25},{25,17},{2,10},{10... | collective-permute-start | bytes 1622024 | tf_op jit(solution)/shard_map/ppermute | solution.py:511
  49.0 13.5 %collective-permute-start.20 = (s16[528,512]{1,0:T(8,128)(2,1)S(1)}, s16[528,512]{1,0:T(8,128)(2,1)S(1)}, u32[]{:S(2)}, u32[]{:S(2)}) collective-permute-start(s16[528,512]{1,0:T(8,128)(2,1)S(1)} %get-tuple-element.70), channel_id=1, source_target_pairs={{0,16},{8,24},{16,0},{24,8},{1,17},{9,25},{17,1},{25,9},{2,18},{10... | collective-permute-start | bytes 1622024 | tf_op jit(solution)/shard_map/ppermute | solution.py:511
  50.3 1.2 %collective-permute-start.17 = (f32[3,8,128]{2,1,0:T(8,128)S(1)}, f32[3,8,128]{2,1,0:T(8,128)S(1)}, u32[]{:S(2)}, u32[]{:S(2)}) collective-permute-start(f32[3,8,128]{2,1,0:T(8,128)S(1)} %get-tuple-element.63), channel_id=1, source_target_pairs={{0,1},{1,0},{2,3},{3,2},{4,5},{5,4},{6,7},{7,6},{8,9},{9,8},{10,11... | collective-permute-start | bytes 36872 | tf_op jit(solution)/shard_map/ppermute | solution.py:508
  51.5 7.3 %collective-permute-start.18 = (f32[2,8,128]{2,1,0:T(8,128)S(1)}, f32[2,8,128]{2,1,0:T(8,128)S(1)}, u32[]{:S(2)}, u32[]{:S(2)}) collective-permute-start(f32[2,8,128]{2,1,0:T(8,128)S(1)} %get-tuple-element.65), channel_id=1, source_target_pairs={{0,4},{1,5},{2,6},{3,7},{4,0},{5,1},{6,2},{7,3},{8,12},{9,13},{10,... | collective-permute-start | bytes 24584 | tf_op jit(solution)/shard_map/ppermute | solution.py:505
  58.8 3.6 %collective-permute-start.21 = (f32[8,128]{1,0:T(8,128)S(1)}, f32[8,128]{1,0:T(8,128)S(1)}, u32[]{:S(2)}, u32[]{:S(2)}) collective-permute-start(f32[8,128]{1,0:T(8,128)S(1)} %get-tuple-element.66.refs_0_), channel_id=1, source_target_pairs={{0,2},{1,3},{2,0},{3,1},{4,6},{5,7},{6,4},{7,5},{8,10},{9,11},{10,... | collective-permute-start | bytes 12296 | tf_op jit(solution)/shard_map/ppermute | solution.py:505
  60.5 10.2 %collective-permute-start.19 = (s16[272,512]{1,0:T(8,128)(2,1)S(1)}, s16[272,512]{1,0:T(8,128)(2,1)S(1)}, u32[]{:S(2)}, u32[]{:S(2)}) collective-permute-start(s16[272,512]{1,0:T(8,128)(2,1)S(1)} %get-tuple-element.67.refs_2_), channel_id=1, source_target_pairs={{0,16},{8,24},{16,0},{24,8},{1,17},{9,25},{17,1},{25,9},{2,18},{10... | collective-permute-start | bytes 835592 | tf_op jit(solution)/shard_map/ppermute | solution.py:511
  63.1 7.6 %collective-permute-start.22 = (s16[272,512]{1,0:T(8,128)(2,1)S(1)}, s16[272,512]{1,0:T(8,128)(2,1)S(1)}, u32[]{:S(2)}, u32[]{:S(2)}) collective-permute-start(s16[272,512]{1,0:T(8,128)(2,1)S(1)} %get-tuple-element.73), channel_id=1, source_target_pairs={{0,8},{8,0},{16,24},{24,16},{1,9},{9,1},{17,25},{25,17},{2,10},{10... | collective-permute-start | bytes 835592 | tf_op jit(solution)/shard_map/ppermute | solution.py:511
  65.2 5.5 %collective-permute-start.25 = (f32[8,128]{1,0:T(8,128)S(1)}, f32[8,128]{1,0:T(8,128)S(1)}, u32[]{:S(2)}, u32[]{:S(2)}) collective-permute-start(f32[8,128]{1,0:T(8,128)S(1)} %add_kernel.1.refs_0_), channel_id=1, source_target_pairs={{0,24},{8,16},{16,8},{24,0},{1,25},{9,17},{17,9},{25,1},{2,26},{10... | collective-permute-start | bytes 12296 | tf_op jit(solution)/shard_map/ppermute | solution.py:511
  65.7 4.9 %collective-permute-start.24 = (f32[8,128]{1,0:T(8,128)S(1)}, f32[8,128]{1,0:T(8,128)S(1)}, u32[]{:S(2)}, u32[]{:S(2)}) collective-permute-start(f32[8,128]{1,0:T(8,128)S(1)} %add_kernel.1.refs_0_), channel_id=1, source_target_pairs={{0,16},{8,24},{16,0},{24,8},{1,17},{9,25},{17,1},{25,9},{2,18},{10... | collective-permute-start | bytes 12296 | tf_op jit(solution)/shard_map/ppermute | solution.py:511
  66.7 3.9 %collective-permute-start.23 = (f32[8,128]{1,0:T(8,128)S(1)}, f32[8,128]{1,0:T(8,128)S(1)}, u32[]{:S(2)}, u32[]{:S(2)}) collective-permute-start(f32[8,128]{1,0:T(8,128)S(1)} %add_kernel.1.refs_0_), channel_id=1, source_target_pairs={{0,8},{8,0},{16,24},{24,16},{1,9},{9,1},{17,25},{25,17},{2,10},{10... | collective-permute-start | bytes 12296 | tf_op jit(solution)/shard_map/ppermute | solution.py:511

commit v6 on v5

--- a/solution.py
+++ b/solution.py
@@ -542,14 +542,14 @@
     (third,) = pick(((0, 1, 2, 3),), (down2, down1, up2, up3), ())
     blocks += [third, across(third)]
 
-    halves = []
+    halves = [None, None]
     before = []
-    for local in range(2):
+    for local in (1, 0):
         send, keep, gate, *before = partial_share(
             local, most, top, (1, 2), capacity, weight, blocks, [*stored, far_stored[local]], before,
-            (sums[0], sums[2]) if local else onward,
+            onward if local else (sums[0], sums[2]),
         )
-        halves.append((over(send, 1 + local), keep, gate))
+        halves[local] = (over(send, 1 + local), keep, gate)
     first_grad, mine, theirs = first_finish(most, top, capacity, first_hidden, info, sums, before)
 
     one = like((top, tokens))
@@ -558,12 +558,12 @@
     stay, away = small(chips_kernel, [two, two], mine, across(theirs))
     came = along(away, [(z, z ^ 2) for z in range(peers // 2)])
     stay, away = small(chip_kernel, [one, one], stay, came)
-    send0, rest0 = middle(got0, keep0, (away,))
+    send1, rest1 = middle(got1, keep1, (away,))
     (total,) = small(
-        add_kernel, [one], stay, along(away, [(z, z ^ 1) for z in range(peers // 2)]), after=(send0,)
+        add_kernel, [one], stay, along(away, [(z, z ^ 1) for z in range(peers // 2)]), after=(send1,)
     )
     whole = [total] + [over(total, flip) for flip in range(1, ranks)]
-    send1, rest1 = middle(got1, keep1, (total,))
+    send0, rest0 = middle(got0, keep0, (total,))
     sums = [over(send0, 2), rest0, gate0, over(send1, 1), rest1, gate1]
     hidden_grad, gate_grad = finish(most, first_grad, sums, whole)
     return hidden_grad, gate_grad.T

time: 72.5 us -> 71.6 us (0.988)
  waiting for transfers between devices: 18.3 us -> 15.7 us
  starting transfers between devices: 33 us -> 34.5 us
    ppermute x7, waiting for transfers between devices: 8.52 us -> 6.92 us  [along(): lax.ppermute(rows, 'expert', [(2 * a + c, 2 * b + c) for a, b in pairs fo...]
    ppermute x15, starting transfers between devices: 17.2 us -> 18.7 us  [over(): return lax.ppermute(rows, 'dp', [(i, i ^ flip) for i in range(ranks)])]
    ppermute x15, waiting for transfers between devices: 8.62 us -> 7.59 us  [over(): return lax.ppermute(rows, 'dp', [(i, i ^ flip) for i in range(ranks)])]
  transfers between devices with their start and end apart: 26 -> 26, of which waited for: 12 -> 14; matrix products, arithmetic and copies ran while one was open for 0% -> 0% of each run, Pallas kernels for 24% -> 24%
where the time goes in v6:
time: 71.6 us; the launch traced here: 71.1 us
  starting transfers between devices  34.5 us (48%)
  Pallas kernels  20.1 us (28%)
  waiting for transfers between devices  15.7 us (22%)
  between operations  0.85 us (1%)
    ppermute x15, starting transfers between devices, over(): return lax.ppermute(rows, 'dp', [(i, i ^ flip) for i in range(ranks)])  18.7 us
    ppermute x7, starting transfers between devices, along(): lax.ppermute(rows, 'expert', [(2 * a + c, 2 * b + c) for a, b in pairs fo...  15.5 us
    pallas_call x4, Pallas kernels, partial_share(): pl.pallas_call(functools.partial(share_kernel, local, most, top, group, e...  10.3 us
    ppermute x15, waiting for transfers between devices, over(): return lax.ppermute(rows, 'dp', [(i, i ^ flip) for i in range(ranks)])  7.59 us
    ppermute x7, waiting for transfers between devices, along(): lax.ppermute(rows, 'expert', [(2 * a + c, 2 * b + c) for a, b in pairs fo...  6.92 us
    pallas_call x1, Pallas kernels, load(): pl.pallas_call(load_kernel, in_specs=[ANY, ANY], out_specs=VMEM, out_shap...  3.39 us
    pallas_call x4, Pallas kernels, middle(): pl.pallas_call(middle_kernel, in_specs=[VMEM, VMEM] + [ANY] * len(after),...  2.17 us
    pallas_call x1, Pallas kernels, finish(): pl.pallas_call(functools.partial(finish_kernel, most), in_specs=[VMEM] *...  1.52 us
  transfers between devices with their start and end apart: 26, of which 14 were waited for; matrix products, arithmetic and copies ran while one was open for 0% of the time, Pallas kernels for 24%

profile of v6, /device:TPU:0, one launch (start us, length us, event | category | flops | bytes accessed | tf_op | source)
XLA Modules:
  0.0 71.1 jit_solution(587040153113089550)
XLA Ops:
  0.6 1.4 %prepare.1 = (bf16[144,1024]{1,0:T(8,128)(2,1)S(1)}, bf16[2,128,512]{2,1,0:T(8,128)(2,1)S(1)}, bf16[2,256,512]{2,1,0:T(8,128)(2,1)S(1)}) custom-call(bf16[128,1024]{1,0:T(8,128)(2,1)} %rows.1, s32[8,128]{1,0:T(8,128)} %bitcast.4, s32[8,128]{1,0:T(8,128)} %bitcast.5, bf16[8,128]{1,0:T(8,128)(2,1)} %bitcast.6, bf16[2,384,512]{2,1,0:T(8,128)(2,1)} %hidden.1), custom_call_target="tpu_custom_call" | custom-call | bytes 1310720 | tf_op jit(solution)/shard_map/prepare/pallas_call | solution.py:177
  2.0 4.9 %collective-permute-start = (bf16[144,1024]{1,0:T(8,128)(2,1)S(1)}, bf16[144,1024]{1,0:T(8,128)(2,1)S(1)}, u32[]{:S(2)}, u32[]{:S(2)}) collective-permute-start(bf16[144,1024]{1,0:T(8,128)(2,1)S(1)} %get-tuple-element.41.after.refs_0_.block), channel_id=1, source_target_pairs={{0,2},{1,3},{2,4},{3,5},{4,6},{5,7},{8,10},{9,11},{10,12},{11,13},... | collective-permute-start | bytes 884744 | tf_op jit(solution)/shard_map/ppermute | solution.py:505
  7.0 1.6 %collective-permute-start.4 = (bf16[2,256,512]{2,1,0:T(8,128)(2,1)S(1)}, bf16[2,256,512]{2,1,0:T(8,128)(2,1)S(1)}, u32[]{:S(2)}, u32[]{:S(2)}) collective-permute-start(bf16[2,256,512]{2,1,0:T(8,128)(2,1)S(1)} %get-tuple-element.42.refs_4_), channel_id=1, source_target_pairs={{0,16},{8,24},{16,0},{24,8},{1,17},{9,25},{17,1},{25,9},{2,18},{10... | collective-permute-start | bytes 1572872 | tf_op jit(solution)/shard_map/ppermute | solution.py:511
  8.5 1.5 %collective-permute-start.3 = (bf16[2,256,512]{2,1,0:T(8,128)(2,1)S(1)}, bf16[2,256,512]{2,1,0:T(8,128)(2,1)S(1)}, u32[]{:S(2)}, u32[]{:S(2)}) collective-permute-start(bf16[2,256,512]{2,1,0:T(8,128)(2,1)S(1)} %get-tuple-element.42.refs_4_), channel_id=1, source_target_pairs={{0,8},{8,0},{16,24},{24,16},{1,9},{9,1},{17,25},{25,17},{2,10},{10... | collective-permute-start | bytes 1572872 | tf_op jit(solution)/shard_map/ppermute | solution.py:511
  10.0 1.3 %collective-permute-start.1 = (bf16[144,1024]{1,0:T(8,128)(2,1)S(1)}, bf16[144,1024]{1,0:T(8,128)(2,1)S(1)}, u32[]{:S(2)}, u32[]{:S(2)}) collective-permute-start(bf16[144,1024]{1,0:T(8,128)(2,1)S(1)} %get-tuple-element.41.after.refs_0_.block), channel_id=1, source_target_pairs={{4,2},{5,3},{2,0},{3,1},{12,10},{13,11},{10,8},{11,9},{20,18},{21,... | collective-permute-start | bytes 884744 | tf_op jit(solution)/shard_map/ppermute | solution.py:505
  11.3 1.9 %collective-permute-done.refs_1_.refs_0_ = bf16[144,1024]{1,0:T(8,128)(2,1)S(1)} collective-permute-done((bf16[144,1024]{1,0:T(8,128)(2,1)S(1)}, bf16[144,1024]{1,0:T(8,128)(2,1)S(1)}, u32[]{:S(2)}, u32[]{:S(2)}) %collective-permute-start) | collective-permute-done | bytes 294944 | tf_op jit(solution)/shard_map/ppermute | solution.py:505
  13.9 3.4 %load_weight.1.refs_2_.weight = bf16[2,2048,1024]{2,1,0:T(8,128)(2,1)S(1)} custom-call(bf16[144,1024]{1,0:T(8,128)(2,1)S(1)} %get-tuple-element.41.after.refs_0_.block, bf16[2,2048,1024]{2,1,0:T(8,128)(2,1)} %weight.1), custom_call_target="tpu_custom_call" | custom-call | bytes 16777216 | tf_op jit(solution)/shard_map/load_weight/pallas_call | solution.py:205
  17.3 2.5 %collective-permute-done.1.refs_3_.refs_2_.refs_1_ = bf16[144,1024]{1,0:T(8,128)(2,1)S(1)} collective-permute-done((bf16[144,1024]{1,0:T(8,128)(2,1)S(1)}, bf16[144,1024]{1,0:T(8,128)(2,1)S(1)}, u32[]{:S(2)}, u32[]{:S(2)}) %collective-permute-start.1) | collective-permute-done | bytes 294944 | tf_op jit(solution)/shard_map/ppermute | solution.py:505
  20.4 1.2 %collective-permute-done.3.over_x.refs_5_ = bf16[2,256,512]{2,1,0:T(8,128)(2,1)S(1)} collective-permute-done((bf16[2,256,512]{2,1,0:T(8,128)(2,1)S(1)}, bf16[2,256,512]{2,1,0:T(8,128)(2,1)S(1)}, u32[]{:S(2)}, u32[]{:S(2)}) %collective-permute-start.3) | collective-permute-done | bytes 524320 | tf_op jit(solution)/shard_map/ppermute | solution.py:511
  22.3 1.3 %collective-permute-start.13 = (bf16[144,1024]{1,0:T(8,128)(2,1)S(1)}, bf16[144,1024]{1,0:T(8,128)(2,1)S(1)}, u32[]{:S(2)}, u32[]{:S(2)}) collective-permute-start(bf16[144,1024]{1,0:T(8,128)(2,1)S(1)} %get-tuple-element.54), channel_id=1, source_target_pairs={{4,0},{5,1},{12,8},{13,9},{20,16},{21,17},{28,24},{29,25}} | collective-permute-start | bytes 884744 | tf_op jit(solution)/shard_map/ppermute | solution.py:505
  24.3 1.6 %collective-permute-start.11 = (bf16[256,512]{1,0:T(8,128)(2,1)S(1)}, bf16[256,512]{1,0:T(8,128)(2,1)S(1)}, u32[]{:S(2)}, u32[]{:S(2)}) collective-permute-start(bf16[256,512]{1,0:T(8,128)(2,1)S(1)} %get-tuple-element.53), channel_id=1, source_target_pairs={{0,8},{8,0},{16,24},{24,16},{1,9},{9,1},{17,25},{25,17},{2,10},{10... | collective-permute-start | bytes 786440 | tf_op jit(solution)/shard_map/ppermute | solution.py:511
  25.9 2.7 %share_0.2 = (s16[272,512]{1,0:T(8,128)(2,1)S(1)}, f32[2,128,512]{2,1,0:T(8,128)S(1)}, f32[2,16,384]{2,1,0:T(8,128)}) custom-call(s32[2]{0:T(128)S(1)} %copy-done, bf16[2,2048,1024]{2,1,0:T(8,128)(2,1)S(1)} %load_weight.1.refs_2_.weight, bf16[144,1024]{1,0:T(8,128)(2,1)S(1)} %pick.3.refs_0_, bf16[144,1024]{1,0:T(8,128)(2,1)S(1)} %collective-permute-done.2.refs_1_), custom_call_target="tpu_custom_call" | custom-call | flops 536870912 | bytes 8978432 | tf_op jit(solution)/shard_map/share_0/pallas_call | solution.py:370
  29.1 2.2 %share_1.2 = (s16[272,512]{1,0:T(8,128)(2,1)S(1)}, f32[2,128,512]{2,1,0:T(8,128)S(1)}, f32[2,16,384]{2,1,0:T(8,128)S(1)}) custom-call(s32[2]{0:T(128)S(1)} %copy-done, bf16[2,2048,1024]{2,1,0:T(8,128)(2,1)S(1)} %load_weight.1.refs_2_.weight, bf16[144,1024]{1,0:T(8,128)(2,1)S(1)} %pick.3.refs_0_, bf16[144,1024]{1,0:T(8,128)(2,1)S(1)} %collective-permute-done.2.refs_1_, ...), custom_call_target="tpu_custom_call" | custom-call | flops 536870912 | bytes 8978432 | tf_op jit(solution)/shard_map/share_1/pallas_call | solution.py:370
  31.4 1.6 %collective-permute-start.8 = (s16[272,512]{1,0:T(8,128)(2,1)S(1)}, s16[272,512]{1,0:T(8,128)(2,1)S(1)}, u32[]{:S(2)}, u32[]{:S(2)}) collective-permute-start(s16[272,512]{1,0:T(8,128)(2,1)S(1)} %get-tuple-element.49.refs_4_), channel_id=1, source_target_pairs={{0,16},{8,24},{16,0},{24,8},{1,17},{9,25},{17,1},{25,9},{2,18},{10... | collective-permute-start | bytes 835592 | tf_op jit(solution)/shard_map/ppermute | solution.py:511
  34.3 2.8 %collective-permute-done.6.got = s16[272,512]{1,0:T(8,128)(2,1)S(1)} collective-permute-done((s16[272,512]{1,0:T(8,128)(2,1)S(1)}, s16[272,512]{1,0:T(8,128)(2,1)S(1)}, u32[]{:S(2)}, u32[]{:S(2)}) %collective-permute-start.6) | collective-permute-done | bytes 278560 | tf_op jit(solution)/shard_map/ppermute | solution.py:511
  37.6 1.6 %collective-permute-start.7 = (s16[144,512]{1,0:T(8,128)(2,1)S(1)}, s16[144,512]{1,0:T(8,128)(2,1)S(1)}, u32[]{:S(2)}, u32[]{:S(2)}) collective-permute-start(s16[144,512]{1,0:T(8,128)(2,1)S(1)} %get-tuple-element.47.refs_8_), channel_id=1, source_target_pairs={{0,16},{8,24},{16,0},{24,8},{1,17},{9,25},{17,1},{25,9},{2,18},{10... | collective-permute-start | bytes 442376 | tf_op jit(solution)/shard_map/ppermute | solution.py:511
  39.6 1.2 %collective-permute-start.9 = (s16[144,512]{1,0:T(8,128)(2,1)S(1)}, s16[144,512]{1,0:T(8,128)(2,1)S(1)}, u32[]{:S(2)}, u32[]{:S(2)}) collective-permute-start(s16[144,512]{1,0:T(8,128)(2,1)S(1)} %get-tuple-element.51.refs_9_), channel_id=1, source_target_pairs={{0,8},{8,0},{16,24},{24,16},{1,9},{9,1},{17,25},{25,17},{2,10},{10... | collective-permute-start | bytes 442376 | tf_op jit(solution)/shard_map/ppermute | solution.py:511
  40.8 2.7 %share_1.3 = (s16[528,512]{1,0:T(8,128)(2,1)S(1)}, f32[2,256,512]{2,1,0:T(8,128)S(1)}, f32[256,128]{1,0:T(8,128)S(1)}, f32[3,8,128]{2,1,0:T(8,128)S(1)}, f32[3,8,128]{2,1,0:T(8,128)S(1)}) custom-call(s32[2]{0:T(128)S(1)} %copy-done, bf16[2,2048,1024]{2,1,0:T(8,128)(2,1)S(1)} %load_weight.1.refs_2_.weight, bf16[144,1024]{1,0:T(8,128)(2,1)S(1)} %pick.4.refs_0_, ...), custom_call_target="tpu_custom_call" | custom-call | flops 1073741824 | bytes 9568256 | tf_op jit(solution)/shard_map/share_1/pallas_call | solution.py:370
  43.5 1.1 %collective-permute-start.20 = (s16[528,512]{1,0:T(8,128)(2,1)S(1)}, s16[528,512]{1,0:T(8,128)(2,1)S(1)}, u32[]{:S(2)}, u32[]{:S(2)}) collective-permute-start(s16[528,512]{1,0:T(8,128)(2,1)S(1)} %get-tuple-element.68), channel_id=1, source_target_pairs={{0,16},{8,24},{16,0},{24,8},{1,17},{9,25},{17,1},{25,9},{2,18},{10... | collective-permute-start | bytes 1622024 | tf_op jit(solution)/shard_map/ppermute | solution.py:511
  44.8 2.7 %share_0.3 = (s16[528,512]{1,0:T(8,128)(2,1)S(1)}, f32[2,256,512]{2,1,0:T(8,128)S(1)}, f32[256,128]{1,0:T(8,128)S(1)}, f32[3,8,128]{2,1,0:T(8,128)S(1)}, f32[3,8,128]{2,1,0:T(8,128)S(1)}) custom-call(s32[2]{0:T(128)S(1)} %copy-done, bf16[2,2048,1024]{2,1,0:T(8,128)(2,1)S(1)} %load_weight.1.refs_2_.weight, bf16[144,1024]{1,0:T(8,128)(2,1)S(1)} %pick.4.refs_0_, ...), custom_call_target="tpu_custom_call" | custom-call | flops 1073741824 | bytes 9568256 | tf_op jit(solution)/shard_map/share_0/pallas_call | solution.py:370
  47.5 1.1 %collective-permute-start.16 = (s16[528,512]{1,0:T(8,128)(2,1)S(1)}, s16[528,512]{1,0:T(8,128)(2,1)S(1)}, u32[]{:S(2)}, u32[]{:S(2)}) collective-permute-start(s16[528,512]{1,0:T(8,128)(2,1)S(1)} %get-tuple-element.60), channel_id=1, source_target_pairs={{0,8},{8,0},{16,24},{24,16},{1,9},{9,1},{17,25},{25,17},{2,10},{10... | collective-permute-start | bytes 1622024 | tf_op jit(solution)/shard_map/ppermute | solution.py:511
  49.7 1.2 %collective-permute-done.17.refs_1_ = f32[3,8,128]{2,1,0:T(8,128)S(1)} collective-permute-done((f32[3,8,128]{2,1,0:T(8,128)S(1)}, f32[3,8,128]{2,1,0:T(8,128)S(1)}, u32[]{:S(2)}, u32[]{:S(2)}) %collective-permute-start.17) | collective-permute-done | bytes 12320 | tf_op jit(solution)/shard_map/ppermute | solution.py:508
  50.9 5.3 %collective-permute-start.18 = (f32[2,8,128]{2,1,0:T(8,128)S(1)}, f32[2,8,128]{2,1,0:T(8,128)S(1)}, u32[]{:S(2)}, u32[]{:S(2)}) collective-permute-start(f32[2,8,128]{2,1,0:T(8,128)S(1)} %get-tuple-element.65), channel_id=1, source_target_pairs={{0,4},{1,5},{2,6},{3,7},{4,0},{5,1},{6,2},{7,3},{8,12},{9,13},{10,... | collective-permute-start | bytes 24584 | tf_op jit(solution)/shard_map/ppermute | solution.py:505
  56.2 1.7 %collective-permute-done.18.refs_1_ = f32[2,8,128]{2,1,0:T(8,128)S(1)} collective-permute-done((f32[2,8,128]{2,1,0:T(8,128)S(1)}, f32[2,8,128]{2,1,0:T(8,128)S(1)}, u32[]{:S(2)}, u32[]{:S(2)}) %collective-permute-start.18) | collective-permute-done | bytes 8224 | tf_op jit(solution)/shard_map/ppermute | solution.py:505
  57.9 1.3 %collective-permute-start.19 = (f32[8,128]{1,0:T(8,128)S(1)}, f32[8,128]{1,0:T(8,128)S(1)}, u32[]{:S(2)}, u32[]{:S(2)}) collective-permute-start(f32[8,128]{1,0:T(8,128)S(1)} %get-tuple-element.67.refs_0_), channel_id=1, source_target_pairs={{0,2},{1,3},{2,0},{3,1},{4,6},{5,7},{6,4},{7,5},{8,10},{9,11},{10,... | collective-permute-start | bytes 12296 | tf_op jit(solution)/shard_map/ppermute | solution.py:505
  59.9 1.6 %collective-permute-start.22 = (s16[272,512]{1,0:T(8,128)(2,1)S(1)}, s16[272,512]{1,0:T(8,128)(2,1)S(1)}, u32[]{:S(2)}, u32[]{:S(2)}) collective-permute-start(s16[272,512]{1,0:T(8,128)(2,1)S(1)} %get-tuple-element.70.refs_2_), channel_id=1, source_target_pairs={{0,8},{8,0},{16,24},{24,16},{1,9},{9,1},{17,25},{25,17},{2,10},{10... | collective-permute-start | bytes 835592 | tf_op jit(solution)/shard_map/ppermute | solution.py:511
  62.2 1.4 %collective-permute-start.21 = (s16[272,512]{1,0:T(8,128)(2,1)S(1)}, s16[272,512]{1,0:T(8,128)(2,1)S(1)}, u32[]{:S(2)}, u32[]{:S(2)}) collective-permute-start(s16[272,512]{1,0:T(8,128)(2,1)S(1)} %get-tuple-element.71), channel_id=1, source_target_pairs={{0,16},{8,24},{16,0},{24,8},{1,17},{9,25},{17,1},{25,9},{2,18},{10... | collective-permute-start | bytes 835592 | tf_op jit(solution)/shard_map/ppermute | solution.py:511
  63.6 1.1 %collective-permute-start.25 = (f32[8,128]{1,0:T(8,128)S(1)}, f32[8,128]{1,0:T(8,128)S(1)}, u32[]{:S(2)}, u32[]{:S(2)}) collective-permute-start(f32[8,128]{1,0:T(8,128)S(1)} %add_kernel.1.refs_0_), channel_id=1, source_target_pairs={{0,24},{8,16},{16,8},{24,0},{1,25},{9,17},{17,9},{25,1},{2,26},{10... | collective-permute-start | bytes 12296 | tf_op jit(solution)/shard_map/ppermute | solution.py:511
  64.8 1.2 %collective-permute-start.24 = (f32[8,128]{1,0:T(8,128)S(1)}, f32[8,128]{1,0:T(8,128)S(1)}, u32[]{:S(2)}, u32[]{:S(2)}) collective-permute-start(f32[8,128]{1,0:T(8,128)S(1)} %add_kernel.1.refs_0_), channel_id=1, source_target_pairs={{0,16},{8,24},{16,0},{24,8},{1,17},{9,25},{17,1},{25,9},{2,18},{10... | collective-permute-start | bytes 12296 | tf_op jit(solution)/shard_map/ppermute | solution.py:511
  66.0 1.1 %collective-permute-start.23 = (f32[8,128]{1,0:T(8,128)S(1)}, f32[8,128]{1,0:T(8,128)S(1)}, u32[]{:S(2)}, u32[]{:S(2)}) collective-permute-start(f32[8,128]{1,0:T(8,128)S(1)} %add_kernel.1.refs_0_), channel_id=1, source_target_pairs={{0,8},{8,0},{16,24},{24,16},{1,9},{9,1},{17,25},{25,17},{2,10},{10... | collective-permute-start | bytes 12296 | tf_op jit(solution)/shard_map/ppermute | solution.py:511
  67.1 1.6 %collective-permute-done.25.refs_3_ = f32[8,128]{1,0:T(8,128)S(1)} collective-permute-done((f32[8,128]{1,0:T(8,128)S(1)}, f32[8,128]{1,0:T(8,128)S(1)}, u32[]{:S(2)}, u32[]{:S(2)}) %collective-permute-start.25) | collective-permute-done | bytes 4128 | tf_op jit(solution)/shard_map/ppermute | solution.py:511
  69.6 1.5 %finish.1 = (f32[2,384,512]{2,1,0:T(8,128)}, f32[8,128]{1,0:T(8,128)}) custom-call(f32[2,128,512]{2,1,0:T(8,128)S(1)} %get-tuple-element.59.first, s16[272,512]{1,0:T(8,128)(2,1)S(1)} %collective-permute-done.21.got0, f32[256,512]{1,0:T(8,128)S(1)} %get-tuple-element.72.rest0, f32[256,128]{1,0:T(8,128)S(1)} %get-tuple-element.73.gates0, ...), custom_call_target="tpu_custom_call" | custom-call | bytes 2916352 | tf_op jit(solution)/shard_map/finish/pallas_call | solution.py:452
  (41 shorter events, 9.0 us)
Async XLA Ops:
  2.0 11.2 %collective-permute-start = (bf16[144,1024]{1,0:T(8,128)(2,1)S(1)}, bf16[144,1024]{1,0:T(8,128)(2,1)S(1)}, u32[]{:S(2)}, u32[]{:S(2)}) collective-permute-start(bf16[144,1024]{1,0:T(8,128)(2,1)S(1)} %get-tuple-element.41.after.refs_0_.block), channel_id=1, source_target_pairs={{0,2},{1,3},{2,4},{3,5},{4,6},{5,7},{8,10},{9,11},{10,12},{11,13},... | collective-permute-start | bytes 884744 | tf_op jit(solution)/shard_map/ppermute | solution.py:505
  7.0 13.4 %collective-permute-start.4 = (bf16[2,256,512]{2,1,0:T(8,128)(2,1)S(1)}, bf16[2,256,512]{2,1,0:T(8,128)(2,1)S(1)}, u32[]{:S(2)}, u32[]{:S(2)}) collective-permute-start(bf16[2,256,512]{2,1,0:T(8,128)(2,1)S(1)} %get-tuple-element.42.refs_4_), channel_id=1, source_target_pairs={{0,16},{8,24},{16,0},{24,8},{1,17},{9,25},{17,1},{25,9},{2,18},{10... | collective-permute-start | bytes 1572872 | tf_op jit(solution)/shard_map/ppermute | solution.py:511
  8.5 13.1 %collective-permute-start.3 = (bf16[2,256,512]{2,1,0:T(8,128)(2,1)S(1)}, bf16[2,256,512]{2,1,0:T(8,128)(2,1)S(1)}, u32[]{:S(2)}, u32[]{:S(2)}) collective-permute-start(bf16[2,256,512]{2,1,0:T(8,128)(2,1)S(1)} %get-tuple-element.42.refs_4_), channel_id=1, source_target_pairs={{0,8},{8,0},{16,24},{24,16},{1,9},{9,1},{17,25},{25,17},{2,10},{10... | collective-permute-start | bytes 1572872 | tf_op jit(solution)/shard_map/ppermute | solution.py:511
  10.0 9.8 %collective-permute-start.1 = (bf16[144,1024]{1,0:T(8,128)(2,1)S(1)}, bf16[144,1024]{1,0:T(8,128)(2,1)S(1)}, u32[]{:S(2)}, u32[]{:S(2)}) collective-permute-start(bf16[144,1024]{1,0:T(8,128)(2,1)S(1)} %get-tuple-element.41.after.refs_0_.block), channel_id=1, source_target_pairs={{4,2},{5,3},{2,0},{3,1},{12,10},{13,11},{10,8},{11,9},{20,18},{21,... | collective-permute-start | bytes 884744 | tf_op jit(solution)/shard_map/ppermute | solution.py:505
  13.2 10.5 %collective-permute-start.10 = (bf16[144,1024]{1,0:T(8,128)(2,1)S(1)}, bf16[144,1024]{1,0:T(8,128)(2,1)S(1)}, u32[]{:S(2)}, u32[]{:S(2)}) collective-permute-start(bf16[144,1024]{1,0:T(8,128)(2,1)S(1)} %collective-permute-done.refs_1_.refs_0_), channel_id=1, source_target_pairs={{2,4},{3,5},{4,6},{5,7},{10,12},{11,13},{12,14},{13,15},{18,20},{1... | collective-permute-start | bytes 884744 | tf_op jit(solution)/shard_map/ppermute | solution.py:505
  17.3 8.6 %copy-start = (s32[2]{0:T(128)S(1)}, s32[2]{0:T(128)}, u32[]{:S(2)}) copy-start(s32[2]{0:T(128)} %cap.9) | copy-start | bytes 28
  19.9 6.0 %collective-permute-start.2 = (bf16[144,1024]{1,0:T(8,128)(2,1)S(1)}, bf16[144,1024]{1,0:T(8,128)(2,1)S(1)}, u32[]{:S(2)}, u32[]{:S(2)}) collective-permute-start(bf16[144,1024]{1,0:T(8,128)(2,1)S(1)} %pick.3.refs_0_), channel_id=1, source_target_pairs={{0,1},{1,0},{2,3},{3,2},{4,5},{5,4},{6,7},{7,6},{8,9},{9,8},{10,11... | collective-permute-start | bytes 884744 | tf_op jit(solution)/shard_map/ppermute | solution.py:508
  21.8 7.3 %collective-permute-start.5 = (bf16[256,512]{1,0:T(8,128)(2,1)S(1)}, bf16[256,512]{1,0:T(8,128)(2,1)S(1)}, u32[]{:S(2)}, u32[]{:S(2)}) collective-permute-start(bf16[256,512]{1,0:T(8,128)(2,1)S(1)} %get-tuple-element.43), channel_id=1, source_target_pairs={{0,16},{8,24},{16,0},{24,8},{1,17},{9,25},{17,1},{25,9},{2,18},{10... | collective-permute-start | bytes 786440 | tf_op jit(solution)/shard_map/ppermute | solution.py:511
  22.3 11.8 %collective-permute-start.13 = (bf16[144,1024]{1,0:T(8,128)(2,1)S(1)}, bf16[144,1024]{1,0:T(8,128)(2,1)S(1)}, u32[]{:S(2)}, u32[]{:S(2)}) collective-permute-start(bf16[144,1024]{1,0:T(8,128)(2,1)S(1)} %get-tuple-element.54), channel_id=1, source_target_pairs={{4,0},{5,1},{12,8},{13,9},{20,16},{21,17},{28,24},{29,25}} | collective-permute-start | bytes 884744 | tf_op jit(solution)/shard_map/ppermute | solution.py:505
  23.6 10.5 %collective-permute-start.14 = (bf16[144,1024]{1,0:T(8,128)(2,1)S(1)}, bf16[144,1024]{1,0:T(8,128)(2,1)S(1)}, u32[]{:S(2)}, u32[]{:S(2)}) collective-permute-start(bf16[144,1024]{1,0:T(8,128)(2,1)S(1)} %collective-permute-done.10.refs_1_.refs_2_), channel_id=1, source_target_pairs={{4,6},{5,7},{12,14},{13,15},{20,22},{21,23},{28,30},{29,31}} | collective-permute-start | bytes 884744 | tf_op jit(solution)/shard_map/ppermute | solution.py:505
  24.3 8.9 %collective-permute-start.11 = (bf16[256,512]{1,0:T(8,128)(2,1)S(1)}, bf16[256,512]{1,0:T(8,128)(2,1)S(1)}, u32[]{:S(2)}, u32[]{:S(2)}) collective-permute-start(bf16[256,512]{1,0:T(8,128)(2,1)S(1)} %get-tuple-element.53), channel_id=1, source_target_pairs={{0,8},{8,0},{16,24},{24,16},{1,9},{9,1},{17,25},{25,17},{2,10},{10... | collective-permute-start | bytes 786440 | tf_op jit(solution)/shard_map/ppermute | solution.py:511
  28.6 8.6 %collective-permute-start.6 = (s16[272,512]{1,0:T(8,128)(2,1)S(1)}, s16[272,512]{1,0:T(8,128)(2,1)S(1)}, u32[]{:S(2)}, u32[]{:S(2)}) collective-permute-start(s16[272,512]{1,0:T(8,128)(2,1)S(1)} %get-tuple-element.45.refs_3_), channel_id=1, source_target_pairs={{0,8},{8,0},{16,24},{24,16},{1,9},{9,1},{17,25},{25,17},{2,10},{10... | collective-permute-start | bytes 835592 | tf_op jit(solution)/shard_map/ppermute | solution.py:511
  31.4 7.8 %collective-permute-start.8 = (s16[272,512]{1,0:T(8,128)(2,1)S(1)}, s16[272,512]{1,0:T(8,128)(2,1)S(1)}, u32[]{:S(2)}, u32[]{:S(2)}) collective-permute-start(s16[272,512]{1,0:T(8,128)(2,1)S(1)} %get-tuple-element.49.refs_4_), channel_id=1, source_target_pairs={{0,16},{8,24},{16,0},{24,8},{1,17},{9,25},{17,1},{25,9},{2,18},{10... | collective-permute-start | bytes 835592 | tf_op jit(solution)/shard_map/ppermute | solution.py:511
  33.4 7.4 %collective-permute-start.12 = (bf16[144,1024]{1,0:T(8,128)(2,1)S(1)}, bf16[144,1024]{1,0:T(8,128)(2,1)S(1)}, u32[]{:S(2)}, u32[]{:S(2)}) collective-permute-start(bf16[144,1024]{1,0:T(8,128)(2,1)S(1)} %pick.4.refs_0_), channel_id=1, source_target_pairs={{0,1},{1,0},{2,3},{3,2},{4,5},{5,4},{6,7},{7,6},{8,9},{9,8},{10,11... | collective-permute-start | bytes 884744 | tf_op jit(solution)/shard_map/ppermute | solution.py:508
  34.2 6.5 %collective-permute-start.15 = (bf16[144,1024]{1,0:T(8,128)(2,1)S(1)}, bf16[144,1024]{1,0:T(8,128)(2,1)S(1)}, u32[]{:S(2)}, u32[]{:S(2)}) collective-permute-start(bf16[144,1024]{1,0:T(8,128)(2,1)S(1)} %pick.5.refs_2_), channel_id=1, source_target_pairs={{0,1},{1,0},{2,3},{3,2},{4,5},{5,4},{6,7},{7,6},{8,9},{9,8},{10,11... | collective-permute-start | bytes 884744 | tf_op jit(solution)/shard_map/ppermute | solution.py:508
  37.6 7.0 %collective-permute-start.7 = (s16[144,512]{1,0:T(8,128)(2,1)S(1)}, s16[144,512]{1,0:T(8,128)(2,1)S(1)}, u32[]{:S(2)}, u32[]{:S(2)}) collective-permute-start(s16[144,512]{1,0:T(8,128)(2,1)S(1)} %get-tuple-element.47.refs_8_), channel_id=1, source_target_pairs={{0,16},{8,24},{16,0},{24,8},{1,17},{9,25},{17,1},{25,9},{2,18},{10... | collective-permute-start | bytes 442376 | tf_op jit(solution)/shard_map/ppermute | solution.py:511
  39.6 5.2 %collective-permute-start.9 = (s16[144,512]{1,0:T(8,128)(2,1)S(1)}, s16[144,512]{1,0:T(8,128)(2,1)S(1)}, u32[]{:S(2)}, u32[]{:S(2)}) collective-permute-start(s16[144,512]{1,0:T(8,128)(2,1)S(1)} %get-tuple-element.51.refs_9_), channel_id=1, source_target_pairs={{0,8},{8,0},{16,24},{24,16},{1,9},{9,1},{17,25},{25,17},{2,10},{10... | collective-permute-start | bytes 442376 | tf_op jit(solution)/shard_map/ppermute | solution.py:511
  43.5 15.7 %collective-permute-start.20 = (s16[528,512]{1,0:T(8,128)(2,1)S(1)}, s16[528,512]{1,0:T(8,128)(2,1)S(1)}, u32[]{:S(2)}, u32[]{:S(2)}) collective-permute-start(s16[528,512]{1,0:T(8,128)(2,1)S(1)} %get-tuple-element.68), channel_id=1, source_target_pairs={{0,16},{8,24},{16,0},{24,8},{1,17},{9,25},{17,1},{25,9},{2,18},{10... | collective-permute-start | bytes 1622024 | tf_op jit(solution)/shard_map/ppermute | solution.py:511
  47.5 14.0 %collective-permute-start.16 = (s16[528,512]{1,0:T(8,128)(2,1)S(1)}, s16[528,512]{1,0:T(8,128)(2,1)S(1)}, u32[]{:S(2)}, u32[]{:S(2)}) collective-permute-start(s16[528,512]{1,0:T(8,128)(2,1)S(1)} %get-tuple-element.60), channel_id=1, source_target_pairs={{0,8},{8,0},{16,24},{24,16},{1,9},{9,1},{17,25},{25,17},{2,10},{10... | collective-permute-start | bytes 1622024 | tf_op jit(solution)/shard_map/ppermute | solution.py:511
  49.6 1.2 %collective-permute-start.17 = (f32[3,8,128]{2,1,0:T(8,128)S(1)}, f32[3,8,128]{2,1,0:T(8,128)S(1)}, u32[]{:S(2)}, u32[]{:S(2)}) collective-permute-start(f32[3,8,128]{2,1,0:T(8,128)S(1)} %get-tuple-element.63), channel_id=1, source_target_pairs={{0,1},{1,0},{2,3},{3,2},{4,5},{5,4},{6,7},{7,6},{8,9},{9,8},{10,11... | collective-permute-start | bytes 36872 | tf_op jit(solution)/shard_map/ppermute | solution.py:508
  50.9 7.0 %collective-permute-start.18 = (f32[2,8,128]{2,1,0:T(8,128)S(1)}, f32[2,8,128]{2,1,0:T(8,128)S(1)}, u32[]{:S(2)}, u32[]{:S(2)}) collective-permute-start(f32[2,8,128]{2,1,0:T(8,128)S(1)} %get-tuple-element.65), channel_id=1, source_target_pairs={{0,4},{1,5},{2,6},{3,7},{4,0},{5,1},{6,2},{7,3},{8,12},{9,13},{10,... | collective-permute-start | bytes 24584 | tf_op jit(solution)/shard_map/ppermute | solution.py:505
  57.9 3.6 %collective-permute-start.19 = (f32[8,128]{1,0:T(8,128)S(1)}, f32[8,128]{1,0:T(8,128)S(1)}, u32[]{:S(2)}, u32[]{:S(2)}) collective-permute-start(f32[8,128]{1,0:T(8,128)S(1)} %get-tuple-element.67.refs_0_), channel_id=1, source_target_pairs={{0,2},{1,3},{2,0},{3,1},{4,6},{5,7},{6,4},{7,5},{8,10},{9,11},{10,... | collective-permute-start | bytes 12296 | tf_op jit(solution)/shard_map/ppermute | solution.py:505
  59.9 9.7 %collective-permute-start.22 = (s16[272,512]{1,0:T(8,128)(2,1)S(1)}, s16[272,512]{1,0:T(8,128)(2,1)S(1)}, u32[]{:S(2)}, u32[]{:S(2)}) collective-permute-start(s16[272,512]{1,0:T(8,128)(2,1)S(1)} %get-tuple-element.70.refs_2_), channel_id=1, source_target_pairs={{0,8},{8,0},{16,24},{24,16},{1,9},{9,1},{17,25},{25,17},{2,10},{10... | collective-permute-start | bytes 835592 | tf_op jit(solution)/shard_map/ppermute | solution.py:511
  62.2 7.4 %collective-permute-start.21 = (s16[272,512]{1,0:T(8,128)(2,1)S(1)}, s16[272,512]{1,0:T(8,128)(2,1)S(1)}, u32[]{:S(2)}, u32[]{:S(2)}) collective-permute-start(s16[272,512]{1,0:T(8,128)(2,1)S(1)} %get-tuple-element.71), channel_id=1, source_target_pairs={{0,16},{8,24},{16,0},{24,8},{1,17},{9,25},{17,1},{25,9},{2,18},{10... | collective-permute-start | bytes 835592 | tf_op jit(solution)/shard_map/ppermute | solution.py:511
  63.6 5.1 %collective-permute-start.25 = (f32[8,128]{1,0:T(8,128)S(1)}, f32[8,128]{1,0:T(8,128)S(1)}, u32[]{:S(2)}, u32[]{:S(2)}) collective-permute-start(f32[8,128]{1,0:T(8,128)S(1)} %add_kernel.1.refs_0_), channel_id=1, source_target_pairs={{0,24},{8,16},{16,8},{24,0},{1,25},{9,17},{17,9},{25,1},{2,26},{10... | collective-permute-start | bytes 12296 | tf_op jit(solution)/shard_map/ppermute | solution.py:511
  64.8 4.6 %collective-permute-start.24 = (f32[8,128]{1,0:T(8,128)S(1)}, f32[8,128]{1,0:T(8,128)S(1)}, u32[]{:S(2)}, u32[]{:S(2)}) collective-permute-start(f32[8,128]{1,0:T(8,128)S(1)} %add_kernel.1.refs_0_), channel_id=1, source_target_pairs={{0,16},{8,24},{16,0},{24,8},{1,17},{9,25},{17,1},{25,9},{2,18},{10... | collective-permute-start | bytes 12296 | tf_op jit(solution)/shard_map/ppermute | solution.py:511
  66.0 3.6 %collective-permute-start.23 = (f32[8,128]{1,0:T(8,128)S(1)}, f32[8,128]{1,0:T(8,128)S(1)}, u32[]{:S(2)}, u32[]{:S(2)}) collective-permute-start(f32[8,128]{1,0:T(8,128)S(1)} %add_kernel.1.refs_0_), channel_id=1, source_target_pairs={{0,8},{8,0},{16,24},{24,16},{1,9},{9,1},{17,25},{25,17},{2,10},{10... | collective-permute-start | bytes 12296 | tf_op jit(solution)/shard_map/ppermute | solution.py:511

commit v7 on v6

--- a/solution.py
+++ b/solution.py
@@ -125,7 +125,7 @@
 def encode(values):
     peak = jnp.maximum(jnp.max(jnp.abs(values), keepdims=True), 1e-30)
     power = jnp.floor(jnp.log2(peak)) + 1.0
-    scaled = values * (jnp.exp2(-power) * (STEPS * STEPS))
+    scaled = (values * jnp.exp2(-power)) * (STEPS * STEPS)
     code = jnp.round(scaled * lax.rsqrt(jnp.abs(scaled) + 1e-20))
     return code.astype(jnp.int32).astype(jnp.int16), power
 
@@ -140,8 +140,8 @@
     lane = part * (coded.shape[1] // parts)
     power = coded[parts * rows :, lane : lane + 128].astype(jnp.int32).astype(jnp.float32)
     code = coded[part * rows : (part + 1) * rows, :].astype(jnp.int32).astype(jnp.float32)
-    scale = jnp.exp2(jnp.max(power, keepdims=True)) * (1.0 / (STEPS * STEPS))
-    return code * jnp.abs(code) * scale
+    scale = jnp.exp2(jnp.max(power, keepdims=True))
+    return (code * jnp.abs(code) * (1.0 / (STEPS * STEPS))) * scale
 
 
 def prepare_kernel(

time: 71.6 us -> 71.8 us (level)
  transfers between devices with their start and end apart: 26 -> 26, of which waited for: 14 -> 13; matrix products, arithmetic and copies ran while one was open for 0% -> 0% of each run, Pallas kernels for 24% -> 25%
where the time goes in v7:
time: 71.8 us; the launch traced here: 71.5 us
  starting transfers between devices  34.6 us (48%)
  Pallas kernels  20.6 us (29%)
  waiting for transfers between devices  15.5 us (22%)
  between operations  0.85 us (1%)
    ppermute x15, starting transfers between devices, over(): return lax.ppermute(rows, 'dp', [(i, i ^ flip) for i in range(ranks)])  18.7 us
    ppermute x7, starting transfers between devices, along(): lax.ppermute(rows, 'expert', [(2 * a + c, 2 * b + c) for a, b in pairs fo...  15.5 us
    pallas_call x4, Pallas kernels, partial_share(): pl.pallas_call(functools.partial(share_kernel, local, most, top, group, e...  10.6 us
    ppermute x15, waiting for transfers between devices, over(): return lax.ppermute(rows, 'dp', [(i, i ^ flip) for i in range(ranks)])  7.41 us
    ppermute x7, waiting for transfers between devices, along(): lax.ppermute(rows, 'expert', [(2 * a + c, 2 * b + c) for a, b in pairs fo...  6.91 us
    pallas_call x1, Pallas kernels, load(): pl.pallas_call(load_kernel, in_specs=[ANY, ANY], out_specs=VMEM, out_shap...  3.39 us
    pallas_call x4, Pallas kernels, middle(): pl.pallas_call(middle_kernel, in_specs=[VMEM, VMEM] + [ANY] * len(after),...  2.45 us
    pallas_call x1, Pallas kernels, finish(): pl.pallas_call(functools.partial(finish_kernel, most), in_specs=[VMEM] *...  1.54 us
  transfers between devices with their start and end apart: 26, of which 13 were waited for; matrix products, arithmetic and copies ran while one was open for 0% of the time, Pallas kernels for 25%

profile of v7, /device:TPU:0, one launch (start us, length us, event | category | flops | bytes accessed | tf_op | source)
XLA Modules:
  0.0 71.5 jit_solution(13536431029496462658)
XLA Ops:
  0.6 1.4 %prepare.1 = (bf16[144,1024]{1,0:T(8,128)(2,1)S(1)}, bf16[2,128,512]{2,1,0:T(8,128)(2,1)S(1)}, bf16[2,256,512]{2,1,0:T(8,128)(2,1)S(1)}) custom-call(bf16[128,1024]{1,0:T(8,128)(2,1)} %rows.1, s32[8,128]{1,0:T(8,128)} %bitcast.4, s32[8,128]{1,0:T(8,128)} %bitcast.5, bf16[8,128]{1,0:T(8,128)(2,1)} %bitcast.6, bf16[2,384,512]{2,1,0:T(8,128)(2,1)} %hidden.1), custom_call_target="tpu_custom_call" | custom-call | bytes 1310720 | tf_op jit(solution)/shard_map/prepare/pallas_call | solution.py:177
  2.0 4.9 %collective-permute-start = (bf16[144,1024]{1,0:T(8,128)(2,1)S(1)}, bf16[144,1024]{1,0:T(8,128)(2,1)S(1)}, u32[]{:S(2)}, u32[]{:S(2)}) collective-permute-start(bf16[144,1024]{1,0:T(8,128)(2,1)S(1)} %get-tuple-element.41.after.refs_0_.block), channel_id=1, source_target_pairs={{0,2},{1,3},{2,4},{3,5},{4,6},{5,7},{8,10},{9,11},{10,12},{11,13},... | collective-permute-start | bytes 884744 | tf_op jit(solution)/shard_map/ppermute | solution.py:505
  7.0 1.6 %collective-permute-start.4 = (bf16[2,256,512]{2,1,0:T(8,128)(2,1)S(1)}, bf16[2,256,512]{2,1,0:T(8,128)(2,1)S(1)}, u32[]{:S(2)}, u32[]{:S(2)}) collective-permute-start(bf16[2,256,512]{2,1,0:T(8,128)(2,1)S(1)} %get-tuple-element.42.refs_4_), channel_id=1, source_target_pairs={{0,16},{8,24},{16,0},{24,8},{1,17},{9,25},{17,1},{25,9},{2,18},{10... | collective-permute-start | bytes 1572872 | tf_op jit(solution)/shard_map/ppermute | solution.py:511
  8.5 1.5 %collective-permute-start.3 = (bf16[2,256,512]{2,1,0:T(8,128)(2,1)S(1)}, bf16[2,256,512]{2,1,0:T(8,128)(2,1)S(1)}, u32[]{:S(2)}, u32[]{:S(2)}) collective-permute-start(bf16[2,256,512]{2,1,0:T(8,128)(2,1)S(1)} %get-tuple-element.42.refs_4_), channel_id=1, source_target_pairs={{0,8},{8,0},{16,24},{24,16},{1,9},{9,1},{17,25},{25,17},{2,10},{10... | collective-permute-start | bytes 1572872 | tf_op jit(solution)/shard_map/ppermute | solution.py:511
  10.0 1.3 %collective-permute-start.1 = (bf16[144,1024]{1,0:T(8,128)(2,1)S(1)}, bf16[144,1024]{1,0:T(8,128)(2,1)S(1)}, u32[]{:S(2)}, u32[]{:S(2)}) collective-permute-start(bf16[144,1024]{1,0:T(8,128)(2,1)S(1)} %get-tuple-element.41.after.refs_0_.block), channel_id=1, source_target_pairs={{4,2},{5,3},{2,0},{3,1},{12,10},{13,11},{10,8},{11,9},{20,18},{21,... | collective-permute-start | bytes 884744 | tf_op jit(solution)/shard_map/ppermute | solution.py:505
  11.3 1.9 %collective-permute-done.refs_1_.refs_0_ = bf16[144,1024]{1,0:T(8,128)(2,1)S(1)} collective-permute-done((bf16[144,1024]{1,0:T(8,128)(2,1)S(1)}, bf16[144,1024]{1,0:T(8,128)(2,1)S(1)}, u32[]{:S(2)}, u32[]{:S(2)}) %collective-permute-start) | collective-permute-done | bytes 294944 | tf_op jit(solution)/shard_map/ppermute | solution.py:505
  13.9 3.4 %load_weight.1.refs_2_.weight = bf16[2,2048,1024]{2,1,0:T(8,128)(2,1)S(1)} custom-call(bf16[144,1024]{1,0:T(8,128)(2,1)S(1)} %get-tuple-element.41.after.refs_0_.block, bf16[2,2048,1024]{2,1,0:T(8,128)(2,1)} %weight.1), custom_call_target="tpu_custom_call" | custom-call | bytes 16777216 | tf_op jit(solution)/shard_map/load_weight/pallas_call | solution.py:205
  17.3 2.5 %collective-permute-done.1.refs_3_.refs_2_.refs_1_ = bf16[144,1024]{1,0:T(8,128)(2,1)S(1)} collective-permute-done((bf16[144,1024]{1,0:T(8,128)(2,1)S(1)}, bf16[144,1024]{1,0:T(8,128)(2,1)S(1)}, u32[]{:S(2)}, u32[]{:S(2)}) %collective-permute-start.1) | collective-permute-done | bytes 294944 | tf_op jit(solution)/shard_map/ppermute | solution.py:505
  20.4 1.2 %collective-permute-done.3.over_x.refs_5_ = bf16[2,256,512]{2,1,0:T(8,128)(2,1)S(1)} collective-permute-done((bf16[2,256,512]{2,1,0:T(8,128)(2,1)S(1)}, bf16[2,256,512]{2,1,0:T(8,128)(2,1)S(1)}, u32[]{:S(2)}, u32[]{:S(2)}) %collective-permute-start.3) | collective-permute-done | bytes 524320 | tf_op jit(solution)/shard_map/ppermute | solution.py:511
  22.3 1.3 %collective-permute-start.13 = (bf16[144,1024]{1,0:T(8,128)(2,1)S(1)}, bf16[144,1024]{1,0:T(8,128)(2,1)S(1)}, u32[]{:S(2)}, u32[]{:S(2)}) collective-permute-start(bf16[144,1024]{1,0:T(8,128)(2,1)S(1)} %get-tuple-element.54), channel_id=1, source_target_pairs={{4,0},{5,1},{12,8},{13,9},{20,16},{21,17},{28,24},{29,25}} | collective-permute-start | bytes 884744 | tf_op jit(solution)/shard_map/ppermute | solution.py:505
  24.3 1.6 %collective-permute-start.11 = (bf16[256,512]{1,0:T(8,128)(2,1)S(1)}, bf16[256,512]{1,0:T(8,128)(2,1)S(1)}, u32[]{:S(2)}, u32[]{:S(2)}) collective-permute-start(bf16[256,512]{1,0:T(8,128)(2,1)S(1)} %get-tuple-element.53), channel_id=1, source_target_pairs={{0,8},{8,0},{16,24},{24,16},{1,9},{9,1},{17,25},{25,17},{2,10},{10... | collective-permute-start | bytes 786440 | tf_op jit(solution)/shard_map/ppermute | solution.py:511
  25.9 2.7 %share_0.2 = (s16[272,512]{1,0:T(8,128)(2,1)S(1)}, f32[2,128,512]{2,1,0:T(8,128)S(1)}, f32[2,16,384]{2,1,0:T(8,128)}) custom-call(s32[2]{0:T(128)S(1)} %copy-done, bf16[2,2048,1024]{2,1,0:T(8,128)(2,1)S(1)} %load_weight.1.refs_2_.weight, bf16[144,1024]{1,0:T(8,128)(2,1)S(1)} %pick.3.refs_0_, bf16[144,1024]{1,0:T(8,128)(2,1)S(1)} %collective-permute-done.2.refs_1_), custom_call_target="tpu_custom_call" | custom-call | flops 536870912 | bytes 8978432 | tf_op jit(solution)/shard_map/share_0/pallas_call | solution.py:370
  29.2 2.3 %share_1.2 = (s16[272,512]{1,0:T(8,128)(2,1)S(1)}, f32[2,128,512]{2,1,0:T(8,128)S(1)}, f32[2,16,384]{2,1,0:T(8,128)S(1)}) custom-call(s32[2]{0:T(128)S(1)} %copy-done, bf16[2,2048,1024]{2,1,0:T(8,128)(2,1)S(1)} %load_weight.1.refs_2_.weight, bf16[144,1024]{1,0:T(8,128)(2,1)S(1)} %pick.3.refs_0_, bf16[144,1024]{1,0:T(8,128)(2,1)S(1)} %collective-permute-done.2.refs_1_, ...), custom_call_target="tpu_custom_call" | custom-call | flops 536870912 | bytes 8978432 | tf_op jit(solution)/shard_map/share_1/pallas_call | solution.py:370
  31.5 1.6 %collective-permute-start.8 = (s16[272,512]{1,0:T(8,128)(2,1)S(1)}, s16[272,512]{1,0:T(8,128)(2,1)S(1)}, u32[]{:S(2)}, u32[]{:S(2)}) collective-permute-start(s16[272,512]{1,0:T(8,128)(2,1)S(1)} %get-tuple-element.49.refs_4_), channel_id=1, source_target_pairs={{0,16},{8,24},{16,0},{24,8},{1,17},{9,25},{17,1},{25,9},{2,18},{10... | collective-permute-start | bytes 835592 | tf_op jit(solution)/shard_map/ppermute | solution.py:511
  34.3 2.8 %collective-permute-done.6.got = s16[272,512]{1,0:T(8,128)(2,1)S(1)} collective-permute-done((s16[272,512]{1,0:T(8,128)(2,1)S(1)}, s16[272,512]{1,0:T(8,128)(2,1)S(1)}, u32[]{:S(2)}, u32[]{:S(2)}) %collective-permute-start.6) | collective-permute-done | bytes 278560 | tf_op jit(solution)/shard_map/ppermute | solution.py:511
  37.6 1.6 %collective-permute-start.7 = (s16[144,512]{1,0:T(8,128)(2,1)S(1)}, s16[144,512]{1,0:T(8,128)(2,1)S(1)}, u32[]{:S(2)}, u32[]{:S(2)}) collective-permute-start(s16[144,512]{1,0:T(8,128)(2,1)S(1)} %get-tuple-element.47.refs_8_), channel_id=1, source_target_pairs={{0,16},{8,24},{16,0},{24,8},{1,17},{9,25},{17,1},{25,9},{2,18},{10... | collective-permute-start | bytes 442376 | tf_op jit(solution)/shard_map/ppermute | solution.py:511
  39.7 1.2 %collective-permute-start.9 = (s16[144,512]{1,0:T(8,128)(2,1)S(1)}, s16[144,512]{1,0:T(8,128)(2,1)S(1)}, u32[]{:S(2)}, u32[]{:S(2)}) collective-permute-start(s16[144,512]{1,0:T(8,128)(2,1)S(1)} %get-tuple-element.51.refs_9_), channel_id=1, source_target_pairs={{0,8},{8,0},{16,24},{24,16},{1,9},{9,1},{17,25},{25,17},{2,10},{10... | collective-permute-start | bytes 442376 | tf_op jit(solution)/shard_map/ppermute | solution.py:511
  40.9 2.8 %share_1.3 = (s16[528,512]{1,0:T(8,128)(2,1)S(1)}, f32[2,256,512]{2,1,0:T(8,128)S(1)}, f32[256,128]{1,0:T(8,128)S(1)}, f32[3,8,128]{2,1,0:T(8,128)S(1)}, f32[3,8,128]{2,1,0:T(8,128)S(1)}) custom-call(s32[2]{0:T(128)S(1)} %copy-done, bf16[2,2048,1024]{2,1,0:T(8,128)(2,1)S(1)} %load_weight.1.refs_2_.weight, bf16[144,1024]{1,0:T(8,128)(2,1)S(1)} %pick.4.refs_0_, ...), custom_call_target="tpu_custom_call" | custom-call | flops 1073741824 | bytes 9568256 | tf_op jit(solution)/shard_map/share_1/pallas_call | solution.py:370
  43.6 1.1 %collective-permute-start.20 = (s16[528,512]{1,0:T(8,128)(2,1)S(1)}, s16[528,512]{1,0:T(8,128)(2,1)S(1)}, u32[]{:S(2)}, u32[]{:S(2)}) collective-permute-start(s16[528,512]{1,0:T(8,128)(2,1)S(1)} %get-tuple-element.68), channel_id=1, source_target_pairs={{0,16},{8,24},{16,0},{24,8},{1,17},{9,25},{17,1},{25,9},{2,18},{10... | collective-permute-start | bytes 1622024 | tf_op jit(solution)/shard_map/ppermute | solution.py:511
  44.9 2.8 %share_0.3 = (s16[528,512]{1,0:T(8,128)(2,1)S(1)}, f32[2,256,512]{2,1,0:T(8,128)S(1)}, f32[256,128]{1,0:T(8,128)S(1)}, f32[3,8,128]{2,1,0:T(8,128)S(1)}, f32[3,8,128]{2,1,0:T(8,128)S(1)}) custom-call(s32[2]{0:T(128)S(1)} %copy-done, bf16[2,2048,1024]{2,1,0:T(8,128)(2,1)S(1)} %load_weight.1.refs_2_.weight, bf16[144,1024]{1,0:T(8,128)(2,1)S(1)} %pick.4.refs_0_, ...), custom_call_target="tpu_custom_call" | custom-call | flops 1073741824 | bytes 9568256 | tf_op jit(solution)/shard_map/share_0/pallas_call | solution.py:370
  47.7 1.1 %collective-permute-start.16 = (s16[528,512]{1,0:T(8,128)(2,1)S(1)}, s16[528,512]{1,0:T(8,128)(2,1)S(1)}, u32[]{:S(2)}, u32[]{:S(2)}) collective-permute-start(s16[528,512]{1,0:T(8,128)(2,1)S(1)} %get-tuple-element.60), channel_id=1, source_target_pairs={{0,8},{8,0},{16,24},{24,16},{1,9},{9,1},{17,25},{25,17},{2,10},{10... | collective-permute-start | bytes 1622024 | tf_op jit(solution)/shard_map/ppermute | solution.py:511
  49.9 1.2 %collective-permute-done.17.refs_1_ = f32[3,8,128]{2,1,0:T(8,128)S(1)} collective-permute-done((f32[3,8,128]{2,1,0:T(8,128)S(1)}, f32[3,8,128]{2,1,0:T(8,128)S(1)}, u32[]{:S(2)}, u32[]{:S(2)}) %collective-permute-start.17) | collective-permute-done | bytes 12320 | tf_op jit(solution)/shard_map/ppermute | solution.py:508
  51.0 5.4 %collective-permute-start.18 = (f32[2,8,128]{2,1,0:T(8,128)S(1)}, f32[2,8,128]{2,1,0:T(8,128)S(1)}, u32[]{:S(2)}, u32[]{:S(2)}) collective-permute-start(f32[2,8,128]{2,1,0:T(8,128)S(1)} %get-tuple-element.65), channel_id=1, source_target_pairs={{0,4},{1,5},{2,6},{3,7},{4,0},{5,1},{6,2},{7,3},{8,12},{9,13},{10,... | collective-permute-start | bytes 24584 | tf_op jit(solution)/shard_map/ppermute | solution.py:505
  56.4 1.7 %collective-permute-done.18.refs_1_ = f32[2,8,128]{2,1,0:T(8,128)S(1)} collective-permute-done((f32[2,8,128]{2,1,0:T(8,128)S(1)}, f32[2,8,128]{2,1,0:T(8,128)S(1)}, u32[]{:S(2)}, u32[]{:S(2)}) %collective-permute-start.18) | collective-permute-done | bytes 8224 | tf_op jit(solution)/shard_map/ppermute | solution.py:505
  58.2 1.3 %collective-permute-start.19 = (f32[8,128]{1,0:T(8,128)S(1)}, f32[8,128]{1,0:T(8,128)S(1)}, u32[]{:S(2)}, u32[]{:S(2)}) collective-permute-start(f32[8,128]{1,0:T(8,128)S(1)} %get-tuple-element.67.refs_0_), channel_id=1, source_target_pairs={{0,2},{1,3},{2,0},{3,1},{4,6},{5,7},{6,4},{7,5},{8,10},{9,11},{10,... | collective-permute-start | bytes 12296 | tf_op jit(solution)/shard_map/ppermute | solution.py:505
  60.2 1.6 %collective-permute-start.22 = (s16[272,512]{1,0:T(8,128)(2,1)S(1)}, s16[272,512]{1,0:T(8,128)(2,1)S(1)}, u32[]{:S(2)}, u32[]{:S(2)}) collective-permute-start(s16[272,512]{1,0:T(8,128)(2,1)S(1)} %get-tuple-element.70.refs_2_), channel_id=1, source_target_pairs={{0,8},{8,0},{16,24},{24,16},{1,9},{9,1},{17,25},{25,17},{2,10},{10... | collective-permute-start | bytes 835592 | tf_op jit(solution)/shard_map/ppermute | solution.py:511
  62.5 1.4 %collective-permute-start.21 = (s16[272,512]{1,0:T(8,128)(2,1)S(1)}, s16[272,512]{1,0:T(8,128)(2,1)S(1)}, u32[]{:S(2)}, u32[]{:S(2)}) collective-permute-start(s16[272,512]{1,0:T(8,128)(2,1)S(1)} %get-tuple-element.71), channel_id=1, source_target_pairs={{0,16},{8,24},{16,0},{24,8},{1,17},{9,25},{17,1},{25,9},{2,18},{10... | collective-permute-start | bytes 835592 | tf_op jit(solution)/shard_map/ppermute | solution.py:511
  63.9 1.2 %collective-permute-start.25 = (f32[8,128]{1,0:T(8,128)S(1)}, f32[8,128]{1,0:T(8,128)S(1)}, u32[]{:S(2)}, u32[]{:S(2)}) collective-permute-start(f32[8,128]{1,0:T(8,128)S(1)} %add_kernel.1.refs_0_), channel_id=1, source_target_pairs={{0,24},{8,16},{16,8},{24,0},{1,25},{9,17},{17,9},{25,1},{2,26},{10... | collective-permute-start | bytes 12296 | tf_op jit(solution)/shard_map/ppermute | solution.py:511
  65.1 1.2 %collective-permute-start.24 = (f32[8,128]{1,0:T(8,128)S(1)}, f32[8,128]{1,0:T(8,128)S(1)}, u32[]{:S(2)}, u32[]{:S(2)}) collective-permute-start(f32[8,128]{1,0:T(8,128)S(1)} %add_kernel.1.refs_0_), channel_id=1, source_target_pairs={{0,16},{8,24},{16,0},{24,8},{1,17},{9,25},{17,1},{25,9},{2,18},{10... | collective-permute-start | bytes 12296 | tf_op jit(solution)/shard_map/ppermute | solution.py:511
  66.4 1.1 %collective-permute-start.23 = (f32[8,128]{1,0:T(8,128)S(1)}, f32[8,128]{1,0:T(8,128)S(1)}, u32[]{:S(2)}, u32[]{:S(2)}) collective-permute-start(f32[8,128]{1,0:T(8,128)S(1)} %add_kernel.1.refs_0_), channel_id=1, source_target_pairs={{0,8},{8,0},{16,24},{24,16},{1,9},{9,1},{17,25},{25,17},{2,10},{10... | collective-permute-start | bytes 12296 | tf_op jit(solution)/shard_map/ppermute | solution.py:511
  67.4 1.6 %collective-permute-done.25.refs_3_ = f32[8,128]{1,0:T(8,128)S(1)} collective-permute-done((f32[8,128]{1,0:T(8,128)S(1)}, f32[8,128]{1,0:T(8,128)S(1)}, u32[]{:S(2)}, u32[]{:S(2)}) %collective-permute-start.25) | collective-permute-done | bytes 4128 | tf_op jit(solution)/shard_map/ppermute | solution.py:511
  70.0 1.5 %finish.1 = (f32[2,384,512]{2,1,0:T(8,128)}, f32[8,128]{1,0:T(8,128)}) custom-call(f32[2,128,512]{2,1,0:T(8,128)S(1)} %get-tuple-element.59.first, s16[272,512]{1,0:T(8,128)(2,1)S(1)} %collective-permute-done.21.got0, f32[256,512]{1,0:T(8,128)S(1)} %get-tuple-element.72.rest0, f32[256,128]{1,0:T(8,128)S(1)} %get-tuple-element.73.gates0, ...), custom_call_target="tpu_custom_call" | custom-call | bytes 2916352 | tf_op jit(solution)/shard_map/finish/pallas_call | solution.py:452
  (41 shorter events, 9.1 us)
Async XLA Ops:
  2.0 11.2 %collective-permute-start = (bf16[144,1024]{1,0:T(8,128)(2,1)S(1)}, bf16[144,1024]{1,0:T(8,128)(2,1)S(1)}, u32[]{:S(2)}, u32[]{:S(2)}) collective-permute-start(bf16[144,1024]{1,0:T(8,128)(2,1)S(1)} %get-tuple-element.41.after.refs_0_.block), channel_id=1, source_target_pairs={{0,2},{1,3},{2,4},{3,5},{4,6},{5,7},{8,10},{9,11},{10,12},{11,13},... | collective-permute-start | bytes 884744 | tf_op jit(solution)/shard_map/ppermute | solution.py:505
  7.0 13.4 %collective-permute-start.4 = (bf16[2,256,512]{2,1,0:T(8,128)(2,1)S(1)}, bf16[2,256,512]{2,1,0:T(8,128)(2,1)S(1)}, u32[]{:S(2)}, u32[]{:S(2)}) collective-permute-start(bf16[2,256,512]{2,1,0:T(8,128)(2,1)S(1)} %get-tuple-element.42.refs_4_), channel_id=1, source_target_pairs={{0,16},{8,24},{16,0},{24,8},{1,17},{9,25},{17,1},{25,9},{2,18},{10... | collective-permute-start | bytes 1572872 | tf_op jit(solution)/shard_map/ppermute | solution.py:511
  8.5 13.1 %collective-permute-start.3 = (bf16[2,256,512]{2,1,0:T(8,128)(2,1)S(1)}, bf16[2,256,512]{2,1,0:T(8,128)(2,1)S(1)}, u32[]{:S(2)}, u32[]{:S(2)}) collective-permute-start(bf16[2,256,512]{2,1,0:T(8,128)(2,1)S(1)} %get-tuple-element.42.refs_4_), channel_id=1, source_target_pairs={{0,8},{8,0},{16,24},{24,16},{1,9},{9,1},{17,25},{25,17},{2,10},{10... | collective-permute-start | bytes 1572872 | tf_op jit(solution)/shard_map/ppermute | solution.py:511
  10.0 9.8 %collective-permute-start.1 = (bf16[144,1024]{1,0:T(8,128)(2,1)S(1)}, bf16[144,1024]{1,0:T(8,128)(2,1)S(1)}, u32[]{:S(2)}, u32[]{:S(2)}) collective-permute-start(bf16[144,1024]{1,0:T(8,128)(2,1)S(1)} %get-tuple-element.41.after.refs_0_.block), channel_id=1, source_target_pairs={{4,2},{5,3},{2,0},{3,1},{12,10},{13,11},{10,8},{11,9},{20,18},{21,... | collective-permute-start | bytes 884744 | tf_op jit(solution)/shard_map/ppermute | solution.py:505
  13.2 10.5 %collective-permute-start.10 = (bf16[144,1024]{1,0:T(8,128)(2,1)S(1)}, bf16[144,1024]{1,0:T(8,128)(2,1)S(1)}, u32[]{:S(2)}, u32[]{:S(2)}) collective-permute-start(bf16[144,1024]{1,0:T(8,128)(2,1)S(1)} %collective-permute-done.refs_1_.refs_0_), channel_id=1, source_target_pairs={{2,4},{3,5},{4,6},{5,7},{10,12},{11,13},{12,14},{13,15},{18,20},{1... | collective-permute-start | bytes 884744 | tf_op jit(solution)/shard_map/ppermute | solution.py:505
  17.3 8.6 %copy-start = (s32[2]{0:T(128)S(1)}, s32[2]{0:T(128)}, u32[]{:S(2)}) copy-start(s32[2]{0:T(128)} %cap.9) | copy-start | bytes 28
  19.9 6.0 %collective-permute-start.2 = (bf16[144,1024]{1,0:T(8,128)(2,1)S(1)}, bf16[144,1024]{1,0:T(8,128)(2,1)S(1)}, u32[]{:S(2)}, u32[]{:S(2)}) collective-permute-start(bf16[144,1024]{1,0:T(8,128)(2,1)S(1)} %pick.3.refs_0_), channel_id=1, source_target_pairs={{0,1},{1,0},{2,3},{3,2},{4,5},{5,4},{6,7},{7,6},{8,9},{9,8},{10,11... | collective-permute-start | bytes 884744 | tf_op jit(solution)/shard_map/ppermute | solution.py:508
  21.8 7.4 %collective-permute-start.5 = (bf16[256,512]{1,0:T(8,128)(2,1)S(1)}, bf16[256,512]{1,0:T(8,128)(2,1)S(1)}, u32[]{:S(2)}, u32[]{:S(2)}) collective-permute-start(bf16[256,512]{1,0:T(8,128)(2,1)S(1)} %get-tuple-element.43), channel_id=1, source_target_pairs={{0,16},{8,24},{16,0},{24,8},{1,17},{9,25},{17,1},{25,9},{2,18},{10... | collective-permute-start | bytes 786440 | tf_op jit(solution)/shard_map/ppermute | solution.py:511
  22.3 11.8 %collective-permute-start.13 = (bf16[144,1024]{1,0:T(8,128)(2,1)S(1)}, bf16[144,1024]{1,0:T(8,128)(2,1)S(1)}, u32[]{:S(2)}, u32[]{:S(2)}) collective-permute-start(bf16[144,1024]{1,0:T(8,128)(2,1)S(1)} %get-tuple-element.54), channel_id=1, source_target_pairs={{4,0},{5,1},{12,8},{13,9},{20,16},{21,17},{28,24},{29,25}} | collective-permute-start | bytes 884744 | tf_op jit(solution)/shard_map/ppermute | solution.py:505
  23.6 10.5 %collective-permute-start.14 = (bf16[144,1024]{1,0:T(8,128)(2,1)S(1)}, bf16[144,1024]{1,0:T(8,128)(2,1)S(1)}, u32[]{:S(2)}, u32[]{:S(2)}) collective-permute-start(bf16[144,1024]{1,0:T(8,128)(2,1)S(1)} %collective-permute-done.10.refs_1_.refs_2_), channel_id=1, source_target_pairs={{4,6},{5,7},{12,14},{13,15},{20,22},{21,23},{28,30},{29,31}} | collective-permute-start | bytes 884744 | tf_op jit(solution)/shard_map/ppermute | solution.py:505
  24.3 8.9 %collective-permute-start.11 = (bf16[256,512]{1,0:T(8,128)(2,1)S(1)}, bf16[256,512]{1,0:T(8,128)(2,1)S(1)}, u32[]{:S(2)}, u32[]{:S(2)}) collective-permute-start(bf16[256,512]{1,0:T(8,128)(2,1)S(1)} %get-tuple-element.53), channel_id=1, source_target_pairs={{0,8},{8,0},{16,24},{24,16},{1,9},{9,1},{17,25},{25,17},{2,10},{10... | collective-permute-start | bytes 786440 | tf_op jit(solution)/shard_map/ppermute | solution.py:511
  28.6 8.5 %collective-permute-start.6 = (s16[272,512]{1,0:T(8,128)(2,1)S(1)}, s16[272,512]{1,0:T(8,128)(2,1)S(1)}, u32[]{:S(2)}, u32[]{:S(2)}) collective-permute-start(s16[272,512]{1,0:T(8,128)(2,1)S(1)} %get-tuple-element.45.refs_3_), channel_id=1, source_target_pairs={{0,8},{8,0},{16,24},{24,16},{1,9},{9,1},{17,25},{25,17},{2,10},{10... | collective-permute-start | bytes 835592 | tf_op jit(solution)/shard_map/ppermute | solution.py:511
  31.5 7.8 %collective-permute-start.8 = (s16[272,512]{1,0:T(8,128)(2,1)S(1)}, s16[272,512]{1,0:T(8,128)(2,1)S(1)}, u32[]{:S(2)}, u32[]{:S(2)}) collective-permute-start(s16[272,512]{1,0:T(8,128)(2,1)S(1)} %get-tuple-element.49.refs_4_), channel_id=1, source_target_pairs={{0,16},{8,24},{16,0},{24,8},{1,17},{9,25},{17,1},{25,9},{2,18},{10... | collective-permute-start | bytes 835592 | tf_op jit(solution)/shard_map/ppermute | solution.py:511
  33.3 7.5 %collective-permute-start.12 = (bf16[144,1024]{1,0:T(8,128)(2,1)S(1)}, bf16[144,1024]{1,0:T(8,128)(2,1)S(1)}, u32[]{:S(2)}, u32[]{:S(2)}) collective-permute-start(bf16[144,1024]{1,0:T(8,128)(2,1)S(1)} %pick.4.refs_0_), channel_id=1, source_target_pairs={{0,1},{1,0},{2,3},{3,2},{4,5},{5,4},{6,7},{7,6},{8,9},{9,8},{10,11... | collective-permute-start | bytes 884744 | tf_op jit(solution)/shard_map/ppermute | solution.py:508
  34.2 6.6 %collective-permute-start.15 = (bf16[144,1024]{1,0:T(8,128)(2,1)S(1)}, bf16[144,1024]{1,0:T(8,128)(2,1)S(1)}, u32[]{:S(2)}, u32[]{:S(2)}) collective-permute-start(bf16[144,1024]{1,0:T(8,128)(2,1)S(1)} %pick.5.refs_2_), channel_id=1, source_target_pairs={{0,1},{1,0},{2,3},{3,2},{4,5},{5,4},{6,7},{7,6},{8,9},{9,8},{10,11... | collective-permute-start | bytes 884744 | tf_op jit(solution)/shard_map/ppermute | solution.py:508
  37.6 7.1 %collective-permute-start.7 = (s16[144,512]{1,0:T(8,128)(2,1)S(1)}, s16[144,512]{1,0:T(8,128)(2,1)S(1)}, u32[]{:S(2)}, u32[]{:S(2)}) collective-permute-start(s16[144,512]{1,0:T(8,128)(2,1)S(1)} %get-tuple-element.47.refs_8_), channel_id=1, source_target_pairs={{0,16},{8,24},{16,0},{24,8},{1,17},{9,25},{17,1},{25,9},{2,18},{10... | collective-permute-start | bytes 442376 | tf_op jit(solution)/shard_map/ppermute | solution.py:511
  39.7 5.2 %collective-permute-start.9 = (s16[144,512]{1,0:T(8,128)(2,1)S(1)}, s16[144,512]{1,0:T(8,128)(2,1)S(1)}, u32[]{:S(2)}, u32[]{:S(2)}) collective-permute-start(s16[144,512]{1,0:T(8,128)(2,1)S(1)} %get-tuple-element.51.refs_9_), channel_id=1, source_target_pairs={{0,8},{8,0},{16,24},{24,16},{1,9},{9,1},{17,25},{25,17},{2,10},{10... | collective-permute-start | bytes 442376 | tf_op jit(solution)/shard_map/ppermute | solution.py:511
  43.6 15.8 %collective-permute-start.20 = (s16[528,512]{1,0:T(8,128)(2,1)S(1)}, s16[528,512]{1,0:T(8,128)(2,1)S(1)}, u32[]{:S(2)}, u32[]{:S(2)}) collective-permute-start(s16[528,512]{1,0:T(8,128)(2,1)S(1)} %get-tuple-element.68), channel_id=1, source_target_pairs={{0,16},{8,24},{16,0},{24,8},{1,17},{9,25},{17,1},{25,9},{2,18},{10... | collective-permute-start | bytes 1622024 | tf_op jit(solution)/shard_map/ppermute | solution.py:511
  47.7 14.1 %collective-permute-start.16 = (s16[528,512]{1,0:T(8,128)(2,1)S(1)}, s16[528,512]{1,0:T(8,128)(2,1)S(1)}, u32[]{:S(2)}, u32[]{:S(2)}) collective-permute-start(s16[528,512]{1,0:T(8,128)(2,1)S(1)} %get-tuple-element.60), channel_id=1, source_target_pairs={{0,8},{8,0},{16,24},{24,16},{1,9},{9,1},{17,25},{25,17},{2,10},{10... | collective-permute-start | bytes 1622024 | tf_op jit(solution)/shard_map/ppermute | solution.py:511
  49.8 1.2 %collective-permute-start.17 = (f32[3,8,128]{2,1,0:T(8,128)S(1)}, f32[3,8,128]{2,1,0:T(8,128)S(1)}, u32[]{:S(2)}, u32[]{:S(2)}) collective-permute-start(f32[3,8,128]{2,1,0:T(8,128)S(1)} %get-tuple-element.63), channel_id=1, source_target_pairs={{0,1},{1,0},{2,3},{3,2},{4,5},{5,4},{6,7},{7,6},{8,9},{9,8},{10,11... | collective-permute-start | bytes 36872 | tf_op jit(solution)/shard_map/ppermute | solution.py:508
  51.0 7.1 %collective-permute-start.18 = (f32[2,8,128]{2,1,0:T(8,128)S(1)}, f32[2,8,128]{2,1,0:T(8,128)S(1)}, u32[]{:S(2)}, u32[]{:S(2)}) collective-permute-start(f32[2,8,128]{2,1,0:T(8,128)S(1)} %get-tuple-element.65), channel_id=1, source_target_pairs={{0,4},{1,5},{2,6},{3,7},{4,0},{5,1},{6,2},{7,3},{8,12},{9,13},{10,... | collective-permute-start | bytes 24584 | tf_op jit(solution)/shard_map/ppermute | solution.py:505
  58.2 3.6 %collective-permute-start.19 = (f32[8,128]{1,0:T(8,128)S(1)}, f32[8,128]{1,0:T(8,128)S(1)}, u32[]{:S(2)}, u32[]{:S(2)}) collective-permute-start(f32[8,128]{1,0:T(8,128)S(1)} %get-tuple-element.67.refs_0_), channel_id=1, source_target_pairs={{0,2},{1,3},{2,0},{3,1},{4,6},{5,7},{6,4},{7,5},{8,10},{9,11},{10,... | collective-permute-start | bytes 12296 | tf_op jit(solution)/shard_map/ppermute | solution.py:505
  60.2 9.8 %collective-permute-start.22 = (s16[272,512]{1,0:T(8,128)(2,1)S(1)}, s16[272,512]{1,0:T(8,128)(2,1)S(1)}, u32[]{:S(2)}, u32[]{:S(2)}) collective-permute-start(s16[272,512]{1,0:T(8,128)(2,1)S(1)} %get-tuple-element.70.refs_2_), channel_id=1, source_target_pairs={{0,8},{8,0},{16,24},{24,16},{1,9},{9,1},{17,25},{25,17},{2,10},{10... | collective-permute-start | bytes 835592 | tf_op jit(solution)/shard_map/ppermute | solution.py:511
  62.5 7.4 %collective-permute-start.21 = (s16[272,512]{1,0:T(8,128)(2,1)S(1)}, s16[272,512]{1,0:T(8,128)(2,1)S(1)}, u32[]{:S(2)}, u32[]{:S(2)}) collective-permute-start(s16[272,512]{1,0:T(8,128)(2,1)S(1)} %get-tuple-element.71), channel_id=1, source_target_pairs={{0,16},{8,24},{16,0},{24,8},{1,17},{9,25},{17,1},{25,9},{2,18},{10... | collective-permute-start | bytes 835592 | tf_op jit(solution)/shard_map/ppermute | solution.py:511
  63.9 5.1 %collective-permute-start.25 = (f32[8,128]{1,0:T(8,128)S(1)}, f32[8,128]{1,0:T(8,128)S(1)}, u32[]{:S(2)}, u32[]{:S(2)}) collective-permute-start(f32[8,128]{1,0:T(8,128)S(1)} %add_kernel.1.refs_0_), channel_id=1, source_target_pairs={{0,24},{8,16},{16,8},{24,0},{1,25},{9,17},{17,9},{25,1},{2,26},{10... | collective-permute-start | bytes 12296 | tf_op jit(solution)/shard_map/ppermute | solution.py:511
  65.1 4.7 %collective-permute-start.24 = (f32[8,128]{1,0:T(8,128)S(1)}, f32[8,128]{1,0:T(8,128)S(1)}, u32[]{:S(2)}, u32[]{:S(2)}) collective-permute-start(f32[8,128]{1,0:T(8,128)S(1)} %add_kernel.1.refs_0_), channel_id=1, source_target_pairs={{0,16},{8,24},{16,0},{24,8},{1,17},{9,25},{17,1},{25,9},{2,18},{10... | collective-permute-start | bytes 12296 | tf_op jit(solution)/shard_map/ppermute | solution.py:511
  66.4 3.6 %collective-permute-start.23 = (f32[8,128]{1,0:T(8,128)S(1)}, f32[8,128]{1,0:T(8,128)S(1)}, u32[]{:S(2)}, u32[]{:S(2)}) collective-permute-start(f32[8,128]{1,0:T(8,128)S(1)} %add_kernel.1.refs_0_), channel_id=1, source_target_pairs={{0,8},{8,0},{16,24},{24,16},{1,9},{9,1},{17,25},{25,17},{2,10},{10... | collective-permute-start | bytes 12296 | tf_op jit(solution)/shard_map/ppermute | solution.py:511

commit v8 on v7

--- a/solution.py
+++ b/solution.py
@@ -547,7 +547,7 @@
     for local in (1, 0):
         send, keep, gate, *before = partial_share(
             local, most, top, (1, 2), capacity, weight, blocks, [*stored, far_stored[local]], before,
-            onward if local else (sums[0], sums[2]),
+            () if local else (sums[0], sums[2]),
         )
         halves[local] = (over(send, 1 + local), keep, gate)
     first_grad, mine, theirs = first_finish(most, top, capacity, first_hidden, info, sums, before)

time: 71.8 us -> 71.8 us (level)
  no operation moved by 1% of the time
where the time goes in v8:
time: 71.8 us; the launch traced here: 71.5 us
  starting transfers between devices  34.6 us (48%)
  Pallas kernels  20.6 us (29%)
  waiting for transfers between devices  15.5 us (22%)
  between operations  0.85 us (1%)
    ppermute x15, starting transfers between devices, over(): return lax.ppermute(rows, 'dp', [(i, i ^ flip) for i in range(ranks)])  18.7 us
    ppermute x7, starting transfers between devices, along(): lax.ppermute(rows, 'expert', [(2 * a + c, 2 * b + c) for a, b in pairs fo...  15.5 us
    pallas_call x4, Pallas kernels, partial_share(): pl.pallas_call(functools.partial(share_kernel, local, most, top, group, e...  10.6 us
    ppermute x15, waiting for transfers between devices, over(): return lax.ppermute(rows, 'dp', [(i, i ^ flip) for i in range(ranks)])  7.41 us
    ppermute x7, waiting for transfers between devices, along(): lax.ppermute(rows, 'expert', [(2 * a + c, 2 * b + c) for a, b in pairs fo...  6.91 us
    pallas_call x1, Pallas kernels, load(): pl.pallas_call(load_kernel, in_specs=[ANY, ANY], out_specs=VMEM, out_shap...  3.39 us
    pallas_call x4, Pallas kernels, middle(): pl.pallas_call(middle_kernel, in_specs=[VMEM, VMEM] + [ANY] * len(after),...  2.45 us
    pallas_call x1, Pallas kernels, finish(): pl.pallas_call(functools.partial(finish_kernel, most), in_specs=[VMEM] *...  1.54 us
  transfers between devices with their start and end apart: 26, of which 13 were waited for; matrix products, arithmetic and copies ran while one was open for 0% of the time, Pallas kernels for 25%

profile of v8, /device:TPU:0, one launch (start us, length us, event | category | flops | bytes accessed | tf_op | source)
XLA Modules:
  0.0 71.5 jit_solution(10353105683420222581)
XLA Ops:
  0.6 1.4 %prepare.1 = (bf16[144,1024]{1,0:T(8,128)(2,1)S(1)}, bf16[2,128,512]{2,1,0:T(8,128)(2,1)S(1)}, bf16[2,256,512]{2,1,0:T(8,128)(2,1)S(1)}) custom-call(bf16[128,1024]{1,0:T(8,128)(2,1)} %rows.1, s32[8,128]{1,0:T(8,128)} %bitcast.4, s32[8,128]{1,0:T(8,128)} %bitcast.5, bf16[8,128]{1,0:T(8,128)(2,1)} %bitcast.6, bf16[2,384,512]{2,1,0:T(8,128)(2,1)} %hidden.1), custom_call_target="tpu_custom_call" | custom-call | bytes 1310720 | tf_op jit(solution)/shard_map/prepare/pallas_call | solution.py:177
  2.0 4.9 %collective-permute-start = (bf16[144,1024]{1,0:T(8,128)(2,1)S(1)}, bf16[144,1024]{1,0:T(8,128)(2,1)S(1)}, u32[]{:S(2)}, u32[]{:S(2)}) collective-permute-start(bf16[144,1024]{1,0:T(8,128)(2,1)S(1)} %get-tuple-element.41.after.refs_0_.block), channel_id=1, source_target_pairs={{0,2},{1,3},{2,4},{3,5},{4,6},{5,7},{8,10},{9,11},{10,12},{11,13},... | collective-permute-start | bytes 884744 | tf_op jit(solution)/shard_map/ppermute | solution.py:505
  7.0 1.6 %collective-permute-start.4 = (bf16[2,256,512]{2,1,0:T(8,128)(2,1)S(1)}, bf16[2,256,512]{2,1,0:T(8,128)(2,1)S(1)}, u32[]{:S(2)}, u32[]{:S(2)}) collective-permute-start(bf16[2,256,512]{2,1,0:T(8,128)(2,1)S(1)} %get-tuple-element.42.refs_4_), channel_id=1, source_target_pairs={{0,16},{8,24},{16,0},{24,8},{1,17},{9,25},{17,1},{25,9},{2,18},{10... | collective-permute-start | bytes 1572872 | tf_op jit(solution)/shard_map/ppermute | solution.py:511
  8.5 1.5 %collective-permute-start.3 = (bf16[2,256,512]{2,1,0:T(8,128)(2,1)S(1)}, bf16[2,256,512]{2,1,0:T(8,128)(2,1)S(1)}, u32[]{:S(2)}, u32[]{:S(2)}) collective-permute-start(bf16[2,256,512]{2,1,0:T(8,128)(2,1)S(1)} %get-tuple-element.42.refs_4_), channel_id=1, source_target_pairs={{0,8},{8,0},{16,24},{24,16},{1,9},{9,1},{17,25},{25,17},{2,10},{10... | collective-permute-start | bytes 1572872 | tf_op jit(solution)/shard_map/ppermute | solution.py:511
  10.0 1.3 %collective-permute-start.1 = (bf16[144,1024]{1,0:T(8,128)(2,1)S(1)}, bf16[144,1024]{1,0:T(8,128)(2,1)S(1)}, u32[]{:S(2)}, u32[]{:S(2)}) collective-permute-start(bf16[144,1024]{1,0:T(8,128)(2,1)S(1)} %get-tuple-element.41.after.refs_0_.block), channel_id=1, source_target_pairs={{4,2},{5,3},{2,0},{3,1},{12,10},{13,11},{10,8},{11,9},{20,18},{21,... | collective-permute-start | bytes 884744 | tf_op jit(solution)/shard_map/ppermute | solution.py:505
  11.3 1.9 %collective-permute-done.refs_1_.refs_0_ = bf16[144,1024]{1,0:T(8,128)(2,1)S(1)} collective-permute-done((bf16[144,1024]{1,0:T(8,128)(2,1)S(1)}, bf16[144,1024]{1,0:T(8,128)(2,1)S(1)}, u32[]{:S(2)}, u32[]{:S(2)}) %collective-permute-start) | collective-permute-done | bytes 294944 | tf_op jit(solution)/shard_map/ppermute | solution.py:505
  13.9 3.4 %load_weight.1.refs_2_.weight = bf16[2,2048,1024]{2,1,0:T(8,128)(2,1)S(1)} custom-call(bf16[144,1024]{1,0:T(8,128)(2,1)S(1)} %get-tuple-element.41.after.refs_0_.block, bf16[2,2048,1024]{2,1,0:T(8,128)(2,1)} %weight.1), custom_call_target="tpu_custom_call" | custom-call | bytes 16777216 | tf_op jit(solution)/shard_map/load_weight/pallas_call | solution.py:205
  17.3 2.5 %collective-permute-done.1.refs_3_.refs_2_.refs_1_ = bf16[144,1024]{1,0:T(8,128)(2,1)S(1)} collective-permute-done((bf16[144,1024]{1,0:T(8,128)(2,1)S(1)}, bf16[144,1024]{1,0:T(8,128)(2,1)S(1)}, u32[]{:S(2)}, u32[]{:S(2)}) %collective-permute-start.1) | collective-permute-done | bytes 294944 | tf_op jit(solution)/shard_map/ppermute | solution.py:505
  20.4 1.2 %collective-permute-done.3.over_x.refs_5_ = bf16[2,256,512]{2,1,0:T(8,128)(2,1)S(1)} collective-permute-done((bf16[2,256,512]{2,1,0:T(8,128)(2,1)S(1)}, bf16[2,256,512]{2,1,0:T(8,128)(2,1)S(1)}, u32[]{:S(2)}, u32[]{:S(2)}) %collective-permute-start.3) | collective-permute-done | bytes 524320 | tf_op jit(solution)/shard_map/ppermute | solution.py:511
  22.3 1.3 %collective-permute-start.13 = (bf16[144,1024]{1,0:T(8,128)(2,1)S(1)}, bf16[144,1024]{1,0:T(8,128)(2,1)S(1)}, u32[]{:S(2)}, u32[]{:S(2)}) collective-permute-start(bf16[144,1024]{1,0:T(8,128)(2,1)S(1)} %get-tuple-element.54), channel_id=1, source_target_pairs={{4,0},{5,1},{12,8},{13,9},{20,16},{21,17},{28,24},{29,25}} | collective-permute-start | bytes 884744 | tf_op jit(solution)/shard_map/ppermute | solution.py:505
  24.3 1.6 %collective-permute-start.11 = (bf16[256,512]{1,0:T(8,128)(2,1)S(1)}, bf16[256,512]{1,0:T(8,128)(2,1)S(1)}, u32[]{:S(2)}, u32[]{:S(2)}) collective-permute-start(bf16[256,512]{1,0:T(8,128)(2,1)S(1)} %get-tuple-element.53), channel_id=1, source_target_pairs={{0,8},{8,0},{16,24},{24,16},{1,9},{9,1},{17,25},{25,17},{2,10},{10... | collective-permute-start | bytes 786440 | tf_op jit(solution)/shard_map/ppermute | solution.py:511
  25.9 2.7 %share_0.2 = (s16[272,512]{1,0:T(8,128)(2,1)S(1)}, f32[2,128,512]{2,1,0:T(8,128)S(1)}, f32[2,16,384]{2,1,0:T(8,128)}) custom-call(s32[2]{0:T(128)S(1)} %copy-done, bf16[2,2048,1024]{2,1,0:T(8,128)(2,1)S(1)} %load_weight.1.refs_2_.weight, bf16[144,1024]{1,0:T(8,128)(2,1)S(1)} %pick.3.refs_0_, bf16[144,1024]{1,0:T(8,128)(2,1)S(1)} %collective-permute-done.2.refs_1_), custom_call_target="tpu_custom_call" | custom-call | flops 536870912 | bytes 8978432 | tf_op jit(solution)/shard_map/share_0/pallas_call | solution.py:370
  29.2 2.3 %share_1.2 = (s16[272,512]{1,0:T(8,128)(2,1)S(1)}, f32[2,128,512]{2,1,0:T(8,128)S(1)}, f32[2,16,384]{2,1,0:T(8,128)S(1)}) custom-call(s32[2]{0:T(128)S(1)} %copy-done, bf16[2,2048,1024]{2,1,0:T(8,128)(2,1)S(1)} %load_weight.1.refs_2_.weight, bf16[144,1024]{1,0:T(8,128)(2,1)S(1)} %pick.3.refs_0_, bf16[144,1024]{1,0:T(8,128)(2,1)S(1)} %collective-permute-done.2.refs_1_, ...), custom_call_target="tpu_custom_call" | custom-call | flops 536870912 | bytes 8978432 | tf_op jit(solution)/shard_map/share_1/pallas_call | solution.py:370
  31.5 1.6 %collective-permute-start.8 = (s16[272,512]{1,0:T(8,128)(2,1)S(1)}, s16[272,512]{1,0:T(8,128)(2,1)S(1)}, u32[]{:S(2)}, u32[]{:S(2)}) collective-permute-start(s16[272,512]{1,0:T(8,128)(2,1)S(1)} %get-tuple-element.49.refs_4_), channel_id=1, source_target_pairs={{0,16},{8,24},{16,0},{24,8},{1,17},{9,25},{17,1},{25,9},{2,18},{10... | collective-permute-start | bytes 835592 | tf_op jit(solution)/shard_map/ppermute | solution.py:511
  34.3 2.8 %collective-permute-done.6.got = s16[272,512]{1,0:T(8,128)(2,1)S(1)} collective-permute-done((s16[272,512]{1,0:T(8,128)(2,1)S(1)}, s16[272,512]{1,0:T(8,128)(2,1)S(1)}, u32[]{:S(2)}, u32[]{:S(2)}) %collective-permute-start.6) | collective-permute-done | bytes 278560 | tf_op jit(solution)/shard_map/ppermute | solution.py:511
  37.6 1.6 %collective-permute-start.7 = (s16[144,512]{1,0:T(8,128)(2,1)S(1)}, s16[144,512]{1,0:T(8,128)(2,1)S(1)}, u32[]{:S(2)}, u32[]{:S(2)}) collective-permute-start(s16[144,512]{1,0:T(8,128)(2,1)S(1)} %get-tuple-element.47), channel_id=1, source_target_pairs={{0,16},{8,24},{16,0},{24,8},{1,17},{9,25},{17,1},{25,9},{2,18},{10... | collective-permute-start | bytes 442376 | tf_op jit(solution)/shard_map/ppermute | solution.py:511
  39.7 1.2 %collective-permute-start.9 = (s16[144,512]{1,0:T(8,128)(2,1)S(1)}, s16[144,512]{1,0:T(8,128)(2,1)S(1)}, u32[]{:S(2)}, u32[]{:S(2)}) collective-permute-start(s16[144,512]{1,0:T(8,128)(2,1)S(1)} %get-tuple-element.51), channel_id=1, source_target_pairs={{0,8},{8,0},{16,24},{24,16},{1,9},{9,1},{17,25},{25,17},{2,10},{10... | collective-permute-start | bytes 442376 | tf_op jit(solution)/shard_map/ppermute | solution.py:511
  40.9 2.8 %share_1.3 = (s16[528,512]{1,0:T(8,128)(2,1)S(1)}, f32[2,256,512]{2,1,0:T(8,128)S(1)}, f32[256,128]{1,0:T(8,128)S(1)}, f32[3,8,128]{2,1,0:T(8,128)S(1)}, f32[3,8,128]{2,1,0:T(8,128)S(1)}) custom-call(s32[2]{0:T(128)S(1)} %copy-done, bf16[2,2048,1024]{2,1,0:T(8,128)(2,1)S(1)} %load_weight.1.refs_2_.weight, bf16[144,1024]{1,0:T(8,128)(2,1)S(1)} %pick.4.refs_0_, ...), custom_call_target="tpu_custom_call" | custom-call | flops 1073741824 | bytes 9568256 | tf_op jit(solution)/shard_map/share_1/pallas_call | solution.py:370
  43.6 1.1 %collective-permute-start.20 = (s16[528,512]{1,0:T(8,128)(2,1)S(1)}, s16[528,512]{1,0:T(8,128)(2,1)S(1)}, u32[]{:S(2)}, u32[]{:S(2)}) collective-permute-start(s16[528,512]{1,0:T(8,128)(2,1)S(1)} %get-tuple-element.68), channel_id=1, source_target_pairs={{0,16},{8,24},{16,0},{24,8},{1,17},{9,25},{17,1},{25,9},{2,18},{10... | collective-permute-start | bytes 1622024 | tf_op jit(solution)/shard_map/ppermute | solution.py:511
  44.9 2.8 %share_0.3 = (s16[528,512]{1,0:T(8,128)(2,1)S(1)}, f32[2,256,512]{2,1,0:T(8,128)S(1)}, f32[256,128]{1,0:T(8,128)S(1)}, f32[3,8,128]{2,1,0:T(8,128)S(1)}, f32[3,8,128]{2,1,0:T(8,128)S(1)}) custom-call(s32[2]{0:T(128)S(1)} %copy-done, bf16[2,2048,1024]{2,1,0:T(8,128)(2,1)S(1)} %load_weight.1.refs_2_.weight, bf16[144,1024]{1,0:T(8,128)(2,1)S(1)} %pick.4.refs_0_, ...), custom_call_target="tpu_custom_call" | custom-call | flops 1073741824 | bytes 9568256 | tf_op jit(solution)/shard_map/share_0/pallas_call | solution.py:370
  47.7 1.1 %collective-permute-start.16 = (s16[528,512]{1,0:T(8,128)(2,1)S(1)}, s16[528,512]{1,0:T(8,128)(2,1)S(1)}, u32[]{:S(2)}, u32[]{:S(2)}) collective-permute-start(s16[528,512]{1,0:T(8,128)(2,1)S(1)} %get-tuple-element.60), channel_id=1, source_target_pairs={{0,8},{8,0},{16,24},{24,16},{1,9},{9,1},{17,25},{25,17},{2,10},{10... | collective-permute-start | bytes 1622024 | tf_op jit(solution)/shard_map/ppermute | solution.py:511
  49.9 1.2 %collective-permute-done.17.refs_1_ = f32[3,8,128]{2,1,0:T(8,128)S(1)} collective-permute-done((f32[3,8,128]{2,1,0:T(8,128)S(1)}, f32[3,8,128]{2,1,0:T(8,128)S(1)}, u32[]{:S(2)}, u32[]{:S(2)}) %collective-permute-start.17) | collective-permute-done | bytes 12320 | tf_op jit(solution)/shard_map/ppermute | solution.py:508
  51.0 5.4 %collective-permute-start.18 = (f32[2,8,128]{2,1,0:T(8,128)S(1)}, f32[2,8,128]{2,1,0:T(8,128)S(1)}, u32[]{:S(2)}, u32[]{:S(2)}) collective-permute-start(f32[2,8,128]{2,1,0:T(8,128)S(1)} %get-tuple-element.65), channel_id=1, source_target_pairs={{0,4},{1,5},{2,6},{3,7},{4,0},{5,1},{6,2},{7,3},{8,12},{9,13},{10,... | collective-permute-start | bytes 24584 | tf_op jit(solution)/shard_map/ppermute | solution.py:505
  56.4 1.7 %collective-permute-done.18.refs_1_ = f32[2,8,128]{2,1,0:T(8,128)S(1)} collective-permute-done((f32[2,8,128]{2,1,0:T(8,128)S(1)}, f32[2,8,128]{2,1,0:T(8,128)S(1)}, u32[]{:S(2)}, u32[]{:S(2)}) %collective-permute-start.18) | collective-permute-done | bytes 8224 | tf_op jit(solution)/shard_map/ppermute | solution.py:505
  58.2 1.3 %collective-permute-start.19 = (f32[8,128]{1,0:T(8,128)S(1)}, f32[8,128]{1,0:T(8,128)S(1)}, u32[]{:S(2)}, u32[]{:S(2)}) collective-permute-start(f32[8,128]{1,0:T(8,128)S(1)} %get-tuple-element.67.refs_0_), channel_id=1, source_target_pairs={{0,2},{1,3},{2,0},{3,1},{4,6},{5,7},{6,4},{7,5},{8,10},{9,11},{10,... | collective-permute-start | bytes 12296 | tf_op jit(solution)/shard_map/ppermute | solution.py:505
  60.2 1.6 %collective-permute-start.22 = (s16[272,512]{1,0:T(8,128)(2,1)S(1)}, s16[272,512]{1,0:T(8,128)(2,1)S(1)}, u32[]{:S(2)}, u32[]{:S(2)}) collective-permute-start(s16[272,512]{1,0:T(8,128)(2,1)S(1)} %get-tuple-element.70.refs_2_), channel_id=1, source_target_pairs={{0,8},{8,0},{16,24},{24,16},{1,9},{9,1},{17,25},{25,17},{2,10},{10... | collective-permute-start | bytes 835592 | tf_op jit(solution)/shard_map/ppermute | solution.py:511
  62.5 1.4 %collective-permute-start.21 = (s16[272,512]{1,0:T(8,128)(2,1)S(1)}, s16[272,512]{1,0:T(8,128)(2,1)S(1)}, u32[]{:S(2)}, u32[]{:S(2)}) collective-permute-start(s16[272,512]{1,0:T(8,128)(2,1)S(1)} %get-tuple-element.71), channel_id=1, source_target_pairs={{0,16},{8,24},{16,0},{24,8},{1,17},{9,25},{17,1},{25,9},{2,18},{10... | collective-permute-start | bytes 835592 | tf_op jit(solution)/shard_map/ppermute | solution.py:511
  63.9 1.2 %collective-permute-start.25 = (f32[8,128]{1,0:T(8,128)S(1)}, f32[8,128]{1,0:T(8,128)S(1)}, u32[]{:S(2)}, u32[]{:S(2)}) collective-permute-start(f32[8,128]{1,0:T(8,128)S(1)} %add_kernel.1.refs_0_), channel_id=1, source_target_pairs={{0,24},{8,16},{16,8},{24,0},{1,25},{9,17},{17,9},{25,1},{2,26},{10... | collective-permute-start | bytes 12296 | tf_op jit(solution)/shard_map/ppermute | solution.py:511
  65.1 1.2 %collective-permute-start.24 = (f32[8,128]{1,0:T(8,128)S(1)}, f32[8,128]{1,0:T(8,128)S(1)}, u32[]{:S(2)}, u32[]{:S(2)}) collective-permute-start(f32[8,128]{1,0:T(8,128)S(1)} %add_kernel.1.refs_0_), channel_id=1, source_target_pairs={{0,16},{8,24},{16,0},{24,8},{1,17},{9,25},{17,1},{25,9},{2,18},{10... | collective-permute-start | bytes 12296 | tf_op jit(solution)/shard_map/ppermute | solution.py:511
  66.3 1.1 %collective-permute-start.23 = (f32[8,128]{1,0:T(8,128)S(1)}, f32[8,128]{1,0:T(8,128)S(1)}, u32[]{:S(2)}, u32[]{:S(2)}) collective-permute-start(f32[8,128]{1,0:T(8,128)S(1)} %add_kernel.1.refs_0_), channel_id=1, source_target_pairs={{0,8},{8,0},{16,24},{24,16},{1,9},{9,1},{17,25},{25,17},{2,10},{10... | collective-permute-start | bytes 12296 | tf_op jit(solution)/shard_map/ppermute | solution.py:511
  67.4 1.6 %collective-permute-done.25.refs_3_ = f32[8,128]{1,0:T(8,128)S(1)} collective-permute-done((f32[8,128]{1,0:T(8,128)S(1)}, f32[8,128]{1,0:T(8,128)S(1)}, u32[]{:S(2)}, u32[]{:S(2)}) %collective-permute-start.25) | collective-permute-done | bytes 4128 | tf_op jit(solution)/shard_map/ppermute | solution.py:511
  70.0 1.5 %finish.1 = (f32[2,384,512]{2,1,0:T(8,128)}, f32[8,128]{1,0:T(8,128)}) custom-call(f32[2,128,512]{2,1,0:T(8,128)S(1)} %get-tuple-element.59.first, s16[272,512]{1,0:T(8,128)(2,1)S(1)} %collective-permute-done.21.got0, f32[256,512]{1,0:T(8,128)S(1)} %get-tuple-element.72.rest0, f32[256,128]{1,0:T(8,128)S(1)} %get-tuple-element.73.gates0, ...), custom_call_target="tpu_custom_call" | custom-call | bytes 2916352 | tf_op jit(solution)/shard_map/finish/pallas_call | solution.py:452
  (41 shorter events, 9.1 us)
Async XLA Ops:
  2.0 11.2 %collective-permute-start = (bf16[144,1024]{1,0:T(8,128)(2,1)S(1)}, bf16[144,1024]{1,0:T(8,128)(2,1)S(1)}, u32[]{:S(2)}, u32[]{:S(2)}) collective-permute-start(bf16[144,1024]{1,0:T(8,128)(2,1)S(1)} %get-tuple-element.41.after.refs_0_.block), channel_id=1, source_target_pairs={{0,2},{1,3},{2,4},{3,5},{4,6},{5,7},{8,10},{9,11},{10,12},{11,13},... | collective-permute-start | bytes 884744 | tf_op jit(solution)/shard_map/ppermute | solution.py:505
  7.0 13.4 %collective-permute-start.4 = (bf16[2,256,512]{2,1,0:T(8,128)(2,1)S(1)}, bf16[2,256,512]{2,1,0:T(8,128)(2,1)S(1)}, u32[]{:S(2)}, u32[]{:S(2)}) collective-permute-start(bf16[2,256,512]{2,1,0:T(8,128)(2,1)S(1)} %get-tuple-element.42.refs_4_), channel_id=1, source_target_pairs={{0,16},{8,24},{16,0},{24,8},{1,17},{9,25},{17,1},{25,9},{2,18},{10... | collective-permute-start | bytes 1572872 | tf_op jit(solution)/shard_map/ppermute | solution.py:511
  8.5 13.1 %collective-permute-start.3 = (bf16[2,256,512]{2,1,0:T(8,128)(2,1)S(1)}, bf16[2,256,512]{2,1,0:T(8,128)(2,1)S(1)}, u32[]{:S(2)}, u32[]{:S(2)}) collective-permute-start(bf16[2,256,512]{2,1,0:T(8,128)(2,1)S(1)} %get-tuple-element.42.refs_4_), channel_id=1, source_target_pairs={{0,8},{8,0},{16,24},{24,16},{1,9},{9,1},{17,25},{25,17},{2,10},{10... | collective-permute-start | bytes 1572872 | tf_op jit(solution)/shard_map/ppermute | solution.py:511
  10.0 9.8 %collective-permute-start.1 = (bf16[144,1024]{1,0:T(8,128)(2,1)S(1)}, bf16[144,1024]{1,0:T(8,128)(2,1)S(1)}, u32[]{:S(2)}, u32[]{:S(2)}) collective-permute-start(bf16[144,1024]{1,0:T(8,128)(2,1)S(1)} %get-tuple-element.41.after.refs_0_.block), channel_id=1, source_target_pairs={{4,2},{5,3},{2,0},{3,1},{12,10},{13,11},{10,8},{11,9},{20,18},{21,... | collective-permute-start | bytes 884744 | tf_op jit(solution)/shard_map/ppermute | solution.py:505
  13.2 10.5 %collective-permute-start.10 = (bf16[144,1024]{1,0:T(8,128)(2,1)S(1)}, bf16[144,1024]{1,0:T(8,128)(2,1)S(1)}, u32[]{:S(2)}, u32[]{:S(2)}) collective-permute-start(bf16[144,1024]{1,0:T(8,128)(2,1)S(1)} %collective-permute-done.refs_1_.refs_0_), channel_id=1, source_target_pairs={{2,4},{3,5},{4,6},{5,7},{10,12},{11,13},{12,14},{13,15},{18,20},{1... | collective-permute-start | bytes 884744 | tf_op jit(solution)/shard_map/ppermute | solution.py:505
  17.3 8.6 %copy-start = (s32[2]{0:T(128)S(1)}, s32[2]{0:T(128)}, u32[]{:S(2)}) copy-start(s32[2]{0:T(128)} %cap.9) | copy-start | bytes 28
  19.9 6.0 %collective-permute-start.2 = (bf16[144,1024]{1,0:T(8,128)(2,1)S(1)}, bf16[144,1024]{1,0:T(8,128)(2,1)S(1)}, u32[]{:S(2)}, u32[]{:S(2)}) collective-permute-start(bf16[144,1024]{1,0:T(8,128)(2,1)S(1)} %pick.3.refs_0_), channel_id=1, source_target_pairs={{0,1},{1,0},{2,3},{3,2},{4,5},{5,4},{6,7},{7,6},{8,9},{9,8},{10,11... | collective-permute-start | bytes 884744 | tf_op jit(solution)/shard_map/ppermute | solution.py:508
  21.8 7.4 %collective-permute-start.5 = (bf16[256,512]{1,0:T(8,128)(2,1)S(1)}, bf16[256,512]{1,0:T(8,128)(2,1)S(1)}, u32[]{:S(2)}, u32[]{:S(2)}) collective-permute-start(bf16[256,512]{1,0:T(8,128)(2,1)S(1)} %get-tuple-element.43), channel_id=1, source_target_pairs={{0,16},{8,24},{16,0},{24,8},{1,17},{9,25},{17,1},{25,9},{2,18},{10... | collective-permute-start | bytes 786440 | tf_op jit(solution)/shard_map/ppermute | solution.py:511
  22.3 11.8 %collective-permute-start.13 = (bf16[144,1024]{1,0:T(8,128)(2,1)S(1)}, bf16[144,1024]{1,0:T(8,128)(2,1)S(1)}, u32[]{:S(2)}, u32[]{:S(2)}) collective-permute-start(bf16[144,1024]{1,0:T(8,128)(2,1)S(1)} %get-tuple-element.54), channel_id=1, source_target_pairs={{4,0},{5,1},{12,8},{13,9},{20,16},{21,17},{28,24},{29,25}} | collective-permute-start | bytes 884744 | tf_op jit(solution)/shard_map/ppermute | solution.py:505
  23.6 10.5 %collective-permute-start.14 = (bf16[144,1024]{1,0:T(8,128)(2,1)S(1)}, bf16[144,1024]{1,0:T(8,128)(2,1)S(1)}, u32[]{:S(2)}, u32[]{:S(2)}) collective-permute-start(bf16[144,1024]{1,0:T(8,128)(2,1)S(1)} %collective-permute-done.10.refs_1_.refs_2_), channel_id=1, source_target_pairs={{4,6},{5,7},{12,14},{13,15},{20,22},{21,23},{28,30},{29,31}} | collective-permute-start | bytes 884744 | tf_op jit(solution)/shard_map/ppermute | solution.py:505
  24.3 8.9 %collective-permute-start.11 = (bf16[256,512]{1,0:T(8,128)(2,1)S(1)}, bf16[256,512]{1,0:T(8,128)(2,1)S(1)}, u32[]{:S(2)}, u32[]{:S(2)}) collective-permute-start(bf16[256,512]{1,0:T(8,128)(2,1)S(1)} %get-tuple-element.53), channel_id=1, source_target_pairs={{0,8},{8,0},{16,24},{24,16},{1,9},{9,1},{17,25},{25,17},{2,10},{10... | collective-permute-start | bytes 786440 | tf_op jit(solution)/shard_map/ppermute | solution.py:511
  28.6 8.5 %collective-permute-start.6 = (s16[272,512]{1,0:T(8,128)(2,1)S(1)}, s16[272,512]{1,0:T(8,128)(2,1)S(1)}, u32[]{:S(2)}, u32[]{:S(2)}) collective-permute-start(s16[272,512]{1,0:T(8,128)(2,1)S(1)} %get-tuple-element.45.refs_3_), channel_id=1, source_target_pairs={{0,8},{8,0},{16,24},{24,16},{1,9},{9,1},{17,25},{25,17},{2,10},{10... | collective-permute-start | bytes 835592 | tf_op jit(solution)/shard_map/ppermute | solution.py:511
  31.5 7.8 %collective-permute-start.8 = (s16[272,512]{1,0:T(8,128)(2,1)S(1)}, s16[272,512]{1,0:T(8,128)(2,1)S(1)}, u32[]{:S(2)}, u32[]{:S(2)}) collective-permute-start(s16[272,512]{1,0:T(8,128)(2,1)S(1)} %get-tuple-element.49.refs_4_), channel_id=1, source_target_pairs={{0,16},{8,24},{16,0},{24,8},{1,17},{9,25},{17,1},{25,9},{2,18},{10... | collective-permute-start | bytes 835592 | tf_op jit(solution)/shard_map/ppermute | solution.py:511
  33.3 7.5 %collective-permute-start.12 = (bf16[144,1024]{1,0:T(8,128)(2,1)S(1)}, bf16[144,1024]{1,0:T(8,128)(2,1)S(1)}, u32[]{:S(2)}, u32[]{:S(2)}) collective-permute-start(bf16[144,1024]{1,0:T(8,128)(2,1)S(1)} %pick.4.refs_0_), channel_id=1, source_target_pairs={{0,1},{1,0},{2,3},{3,2},{4,5},{5,4},{6,7},{7,6},{8,9},{9,8},{10,11... | collective-permute-start | bytes 884744 | tf_op jit(solution)/shard_map/ppermute | solution.py:508
  34.2 6.6 %collective-permute-start.15 = (bf16[144,1024]{1,0:T(8,128)(2,1)S(1)}, bf16[144,1024]{1,0:T(8,128)(2,1)S(1)}, u32[]{:S(2)}, u32[]{:S(2)}) collective-permute-start(bf16[144,1024]{1,0:T(8,128)(2,1)S(1)} %pick.5.refs_2_), channel_id=1, source_target_pairs={{0,1},{1,0},{2,3},{3,2},{4,5},{5,4},{6,7},{7,6},{8,9},{9,8},{10,11... | collective-permute-start | bytes 884744 | tf_op jit(solution)/shard_map/ppermute | solution.py:508
  37.6 7.1 %collective-permute-start.7 = (s16[144,512]{1,0:T(8,128)(2,1)S(1)}, s16[144,512]{1,0:T(8,128)(2,1)S(1)}, u32[]{:S(2)}, u32[]{:S(2)}) collective-permute-start(s16[144,512]{1,0:T(8,128)(2,1)S(1)} %get-tuple-element.47), channel_id=1, source_target_pairs={{0,16},{8,24},{16,0},{24,8},{1,17},{9,25},{17,1},{25,9},{2,18},{10... | collective-permute-start | bytes 442376 | tf_op jit(solution)/shard_map/ppermute | solution.py:511
  39.7 5.2 %collective-permute-start.9 = (s16[144,512]{1,0:T(8,128)(2,1)S(1)}, s16[144,512]{1,0:T(8,128)(2,1)S(1)}, u32[]{:S(2)}, u32[]{:S(2)}) collective-permute-start(s16[144,512]{1,0:T(8,128)(2,1)S(1)} %get-tuple-element.51), channel_id=1, source_target_pairs={{0,8},{8,0},{16,24},{24,16},{1,9},{9,1},{17,25},{25,17},{2,10},{10... | collective-permute-start | bytes 442376 | tf_op jit(solution)/shard_map/ppermute | solution.py:511
  43.6 15.8 %collective-permute-start.20 = (s16[528,512]{1,0:T(8,128)(2,1)S(1)}, s16[528,512]{1,0:T(8,128)(2,1)S(1)}, u32[]{:S(2)}, u32[]{:S(2)}) collective-permute-start(s16[528,512]{1,0:T(8,128)(2,1)S(1)} %get-tuple-element.68), channel_id=1, source_target_pairs={{0,16},{8,24},{16,0},{24,8},{1,17},{9,25},{17,1},{25,9},{2,18},{10... | collective-permute-start | bytes 1622024 | tf_op jit(solution)/shard_map/ppermute | solution.py:511
  47.7 14.1 %collective-permute-start.16 = (s16[528,512]{1,0:T(8,128)(2,1)S(1)}, s16[528,512]{1,0:T(8,128)(2,1)S(1)}, u32[]{:S(2)}, u32[]{:S(2)}) collective-permute-start(s16[528,512]{1,0:T(8,128)(2,1)S(1)} %get-tuple-element.60), channel_id=1, source_target_pairs={{0,8},{8,0},{16,24},{24,16},{1,9},{9,1},{17,25},{25,17},{2,10},{10... | collective-permute-start | bytes 1622024 | tf_op jit(solution)/shard_map/ppermute | solution.py:511
  49.8 1.2 %collective-permute-start.17 = (f32[3,8,128]{2,1,0:T(8,128)S(1)}, f32[3,8,128]{2,1,0:T(8,128)S(1)}, u32[]{:S(2)}, u32[]{:S(2)}) collective-permute-start(f32[3,8,128]{2,1,0:T(8,128)S(1)} %get-tuple-element.63), channel_id=1, source_target_pairs={{0,1},{1,0},{2,3},{3,2},{4,5},{5,4},{6,7},{7,6},{8,9},{9,8},{10,11... | collective-permute-start | bytes 36872 | tf_op jit(solution)/shard_map/ppermute | solution.py:508
  51.0 7.1 %collective-permute-start.18 = (f32[2,8,128]{2,1,0:T(8,128)S(1)}, f32[2,8,128]{2,1,0:T(8,128)S(1)}, u32[]{:S(2)}, u32[]{:S(2)}) collective-permute-start(f32[2,8,128]{2,1,0:T(8,128)S(1)} %get-tuple-element.65), channel_id=1, source_target_pairs={{0,4},{1,5},{2,6},{3,7},{4,0},{5,1},{6,2},{7,3},{8,12},{9,13},{10,... | collective-permute-start | bytes 24584 | tf_op jit(solution)/shard_map/ppermute | solution.py:505
  58.2 3.6 %collective-permute-start.19 = (f32[8,128]{1,0:T(8,128)S(1)}, f32[8,128]{1,0:T(8,128)S(1)}, u32[]{:S(2)}, u32[]{:S(2)}) collective-permute-start(f32[8,128]{1,0:T(8,128)S(1)} %get-tuple-element.67.refs_0_), channel_id=1, source_target_pairs={{0,2},{1,3},{2,0},{3,1},{4,6},{5,7},{6,4},{7,5},{8,10},{9,11},{10,... | collective-permute-start | bytes 12296 | tf_op jit(solution)/shard_map/ppermute | solution.py:505
  60.2 9.8 %collective-permute-start.22 = (s16[272,512]{1,0:T(8,128)(2,1)S(1)}, s16[272,512]{1,0:T(8,128)(2,1)S(1)}, u32[]{:S(2)}, u32[]{:S(2)}) collective-permute-start(s16[272,512]{1,0:T(8,128)(2,1)S(1)} %get-tuple-element.70.refs_2_), channel_id=1, source_target_pairs={{0,8},{8,0},{16,24},{24,16},{1,9},{9,1},{17,25},{25,17},{2,10},{10... | collective-permute-start | bytes 835592 | tf_op jit(solution)/shard_map/ppermute | solution.py:511
  62.5 7.4 %collective-permute-start.21 = (s16[272,512]{1,0:T(8,128)(2,1)S(1)}, s16[272,512]{1,0:T(8,128)(2,1)S(1)}, u32[]{:S(2)}, u32[]{:S(2)}) collective-permute-start(s16[272,512]{1,0:T(8,128)(2,1)S(1)} %get-tuple-element.71), channel_id=1, source_target_pairs={{0,16},{8,24},{16,0},{24,8},{1,17},{9,25},{17,1},{25,9},{2,18},{10... | collective-permute-start | bytes 835592 | tf_op jit(solution)/shard_map/ppermute | solution.py:511
  63.9 5.1 %collective-permute-start.25 = (f32[8,128]{1,0:T(8,128)S(1)}, f32[8,128]{1,0:T(8,128)S(1)}, u32[]{:S(2)}, u32[]{:S(2)}) collective-permute-start(f32[8,128]{1,0:T(8,128)S(1)} %add_kernel.1.refs_0_), channel_id=1, source_target_pairs={{0,24},{8,16},{16,8},{24,0},{1,25},{9,17},{17,9},{25,1},{2,26},{10... | collective-permute-start | bytes 12296 | tf_op jit(solution)/shard_map/ppermute | solution.py:511
  65.1 4.7 %collective-permute-start.24 = (f32[8,128]{1,0:T(8,128)S(1)}, f32[8,128]{1,0:T(8,128)S(1)}, u32[]{:S(2)}, u32[]{:S(2)}) collective-permute-start(f32[8,128]{1,0:T(8,128)S(1)} %add_kernel.1.refs_0_), channel_id=1, source_target_pairs={{0,16},{8,24},{16,0},{24,8},{1,17},{9,25},{17,1},{25,9},{2,18},{10... | collective-permute-start | bytes 12296 | tf_op jit(solution)/shard_map/ppermute | solution.py:511
  66.3 3.6 %collective-permute-start.23 = (f32[8,128]{1,0:T(8,128)S(1)}, f32[8,128]{1,0:T(8,128)S(1)}, u32[]{:S(2)}, u32[]{:S(2)}) collective-permute-start(f32[8,128]{1,0:T(8,128)S(1)} %add_kernel.1.refs_0_), channel_id=1, source_target_pairs={{0,8},{8,0},{16,24},{24,16},{1,9},{9,1},{17,25},{25,17},{2,10},{10... | collective-permute-start | bytes 12296 | tf_op jit(solution)/shard_map/ppermute | solution.py:511
